TPU v7x, 128 devices: a whole 4x4x4 slice. The times are simulated.
128 devices in a mesh: island: 8 (over x, y_lo), shard: 16 (over z, y_hi, core).
Axes of the slice: x: 4, y: 4 (y_hi: 2, y_lo: 2; y = y_hi * 2 + y_lo), z: 4, core: 2. Of those that a mesh axis runs over, the one named last changes fastest.
Arguments:
- partials: bfloat16 [8, 16, 512, 8192], P('island', 'shard'), may hold values from -6 to 6
- error_buf: float32 [8, 512, 8192], P('island', 'shard'), may hold values from -200 to 200
- momentum: float32 [512, 8192], P('shard'), may hold values from -6 to 6
- params: float32 [512, 8192], P('shard'), may hold values from -6 to 6
- start_q: float32 [8192, 256], P('shard'), may hold values from -6 to 6
Outputs:
- params_full: bfloat16 [512, 8192], replicated
- new_params: float32 [512, 8192], P('shard')
- new_momentum: float32 [512, 8192], P('shard')
- new_error: float32 [8, 512, 8192], P('island', 'shard')
All inputs are finite; a program needn't handle non-finite values.
Results may differ from a plain program's by a relative error of at most 0.017.
Values may be sent and summed in bfloat16 or wider, within the bound.
No kernel may reach another device: no remote copies, remote signals or barrier semaphores. Data moves between devices by JAX's collectives and lax.ppermute only.
A program may use at most 128 MiB of HBM per device.

v0:
```python
import jax
import jax.numpy as jnp
from jax import lax
from jax.sharding import PartitionSpec as P

NS_ITERS = 5


HIGH = lax.Precision.HIGHEST


def matmul(left, right):
    return jnp.dot(left, right, precision=HIGH, preferred_element_type=jnp.float32)


def inner_left(left, right):
    return lax.dot_general(
        left, right, (((0,), (0,)), ((), ())), precision=HIGH, preferred_element_type=jnp.float32
    )


def newton_step(orth, gram_mat):
    return 1.5 * orth - 0.5 * matmul(orth, gram_mat)


def on_device(partials, error_buf, momentum, params, start_q):
    islands = lax.axis_size("island")
    summed = lax.psum_scatter(partials[0, 0], "shard", scatter_dimension=0, tiled=True).astype(
        jnp.float32
    )
    merged = summed + error_buf[0]
    local_proj = matmul(
        merged,
        lax.all_gather(start_q.astype(jnp.bfloat16), "shard", axis=0, tiled=True).astype(
            jnp.float32
        ),
    )
    proj = lax.psum(local_proj.astype(jnp.bfloat16), "island").astype(jnp.float32) / islands
    total = lax.psum(jnp.sum(proj * proj), "shard")
    orth = proj * lax.rsqrt(total + 1e-06)
    for step in range(NS_ITERS):
        gram_mat = lax.psum(inner_left(orth, orth).astype(jnp.bfloat16), "shard").astype(
            jnp.float32
        )
        orth = newton_step(orth, gram_mat)
    qnew = lax.psum(inner_left(merged, orth), ("island", "shard")) / islands
    delta = lax.dot_general(
        orth, qnew, (((1,), (1,)), ((), ())), precision=HIGH, preferred_element_type=jnp.float32
    )
    new_error = merged - delta
    new_momentum = 0.9 * momentum + delta
    new_params = params - 0.7 * (delta + 0.9 * new_momentum)
    params_full = lax.all_gather(new_params.astype(jnp.bfloat16), "shard", axis=0, tiled=True)
    return (params_full, new_params, new_momentum, new_error[None])


def solution(mesh):
    in_specs = (
        P("island", "shard", None, None),
        P("island", "shard", None),
        P("shard", None),
        P("shard", None),
        P("shard", None),
    )
    out_specs = (P(), P("shard", None), P("shard", None), P("island", "shard", None))
    return jax.shard_map(
        on_device, mesh=mesh, in_specs=in_specs, out_specs=out_specs, check_vma=False
    )
```

profile of v0, /device:TPU:1, one launch (start us, length us, event | category | flops | bytes accessed | tf_op | source)
XLA Modules:
  0.0 1211.5 jit_solution(13810865479246185176)
XLA Ops:
  7.2 0.0 copy-start
  7.2 0.0 all-gather.3.cloned.1.call-start
  7.2 1.8 convert_element_type.37
  9.1 0.0 all-gather.3.cloned.1.call-update
  9.1 0.0 reduce-scatter.2.cloned.1.call-start
  9.1 0.7 reduce-scatter.2.cloned.1.call-update
  9.8 0.0 all-reduce.7.cloned.1.call-start
  9.9 60.3 %all-gather.3.cloned.1.call-done = bf16[8192,256]{1,0:T(8,128)(2,1)} async-done(((bf16[512,256]{1,0:T(8,128)(2,1)}), bf16[8192,256]{1,0:T(8,128)(2,1)}) %all-gather.3.cloned.1.call-update) | async-done | bytes 4194320 | tf_op jit(solution)/shard_map/all_gather | solution.py:34
  70.2 103.1 %reduce-scatter.2.cloned.1.call-done = bf16[32,8192]{1,0:T(8,128)(2,1)} async-done(((bf16[512,8192]{1,0:T(8,128)(2,1)}), bf16[32,8192]{1,0:T(8,128)(2,1)}) %reduce-scatter.2.cloned.1.call-update) | async-done | bytes 524304 | tf_op jit(solution)/shard_map/reduce_scatter | solution.py:28
  173.3 0.0 copy-done
  173.3 0.0 copy-start.1
  173.3 4.5 convolution_convert_fusion.5
  177.8 25.9 %psum.56 = bf16[32,256]{1,0:T(8,128)(2,1)S(1)} all-reduce(bf16[32,256]{1,0:T(8,128)(2,1)S(1)} %convolution_convert_fusion.5), channel_id=1, replica_groups=mesh['island'=8,'shard'=16] {'island'}, use_global_device_ids=true, to_apply=%region_1.0 | all-reduce | flops 8192 | bytes 32768 | tf_op jit(solution)/shard_map/psum | solution.py:38
  203.7 0.6 fusion.11
  204.3 42.1 %psum.57 = f32[]{:T(128)} all-reduce(f32[]{:T(128)} %fusion.11), channel_id=1, replica_groups=mesh['island'=8,'shard'=16] {'shard'}, use_global_device_ids=true, to_apply=%region_3.0 | all-reduce | flops 1 | bytes 8 | tf_op jit(solution)/shard_map/psum | solution.py:39
  247.1 1.1 convolution_convert_fusion.4
  248.2 0.0 all-reduce.7.cloned.1.call-update
  248.2 0.0 all-reduce.9.cloned.1.call-start
  248.2 129.8 %all-reduce.7.cloned.1.call-done = bf16[256,256]{1,0:T(8,128)(2,1)} async-done(((bf16[256,256]{1,0:T(8,128)(2,1)}), bf16[256,256]{1,0:T(8,128)(2,1)}) %all-reduce.7.cloned.1.call-update) | async-done | bytes 131088 | tf_op jit(solution)/shard_map/psum | solution.py:42
  378.1 1.1 fusion.7
  379.2 1.1 convolution_convert_fusion.3
  380.2 0.0 all-reduce.9.cloned.1.call-update
  380.3 0.0 all-reduce.11.cloned.1.call-start
  380.3 138.1 %all-reduce.9.cloned.1.call-done = bf16[256,256]{1,0:T(8,128)(2,1)} async-done(((bf16[256,256]{1,0:T(8,128)(2,1)}), bf16[256,256]{1,0:T(8,128)(2,1)}) %all-reduce.9.cloned.1.call-update) | async-done | bytes 131088 | tf_op jit(solution)/shard_map/psum | solution.py:42
  518.4 1.1 fusion.6
  519.5 1.1 convolution_convert_fusion.2
  520.6 0.0 all-reduce.11.cloned.1.call-update
  520.6 0.0 all-reduce.13.cloned.1.call-start
  520.7 137.9 %all-reduce.11.cloned.1.call-done = bf16[256,256]{1,0:T(8,128)(2,1)} async-done(((bf16[256,256]{1,0:T(8,128)(2,1)}), bf16[256,256]{1,0:T(8,128)(2,1)}) %all-reduce.11.cloned.1.call-update) | async-done | bytes 131088 | tf_op jit(solution)/shard_map/psum | solution.py:42
  658.6 1.1 fusion.5
  659.7 1.1 convolution_convert_fusion.1
  660.8 0.0 all-reduce.13.cloned.1.call-update
  660.8 0.0 all-reduce.15.cloned.1.call-start
  660.9 138.1 %all-reduce.13.cloned.1.call-done = bf16[256,256]{1,0:T(8,128)(2,1)} async-done(((bf16[256,256]{1,0:T(8,128)(2,1)}), bf16[256,256]{1,0:T(8,128)(2,1)}) %all-reduce.13.cloned.1.call-update) | async-done | bytes 131088 | tf_op jit(solution)/shard_map/psum | solution.py:42
  799.0 1.1 fusion.4
  800.1 1.1 convolution_convert_fusion
  801.2 0.0 all-reduce.15.cloned.1.call-update
  801.2 0.0 all-reduce.17.cloned.1.call-start
  801.2 138.1 %all-reduce.15.cloned.1.call-done = bf16[256,256]{1,0:T(8,128)(2,1)} async-done(((bf16[256,256]{1,0:T(8,128)(2,1)}), bf16[256,256]{1,0:T(8,128)(2,1)}) %all-reduce.15.cloned.1.call-update) | async-done | bytes 131088 | tf_op jit(solution)/shard_map/psum | solution.py:42
  939.3 1.1 fusion.3
  940.4 0.0 copy-done.1
  940.4 9.0 fusion.8
  949.4 0.0 copy-start.2
  949.4 0.0 all-reduce.17.cloned.1.call-update
  949.4 0.2 all-gather.5.cloned.1.call-start
  949.7 162.5 %all-reduce.17.cloned.1.call-done = f32[8192,256]{1,0:T(8,128)} async-done(((f32[8192,256]{1,0:T(8,128)}), f32[8192,256]{1,0:T(8,128)}) %all-reduce.17.cloned.1.call-update) | async-done | bytes 8388624 | tf_op jit(solution)/shard_map/psum | solution.py:46
  1112.1 0.0 copy-done.2
  1112.1 12.9 %fusion.15 = (bf16[32,8192]{1,0:T(8,128)(2,1)}, f32[32,8192]{1,0:T(8,128)}, f32[32,8192]{1,0:T(8,128)}, f32[1,32,8192]{2,1,0:T(8,128)}) fusion(f32[32,8192]{1,0:T(8,128)S(1)} %copy-done.2, f32[32,8192]{1,0:T(8,128)} %param.7, f32[1,32,8192]{2,1,0:T(8,128)S(1)} %copy-done, bf16[32,8192]{1,0:T(8,128)(2,1)S(1)} %copy-done.1, f32[32,256]{1,0:T(8,128)S(1)} %fusion.3, ...), kind=kOutput, calls=%fused_computation.32 | convolution fusion | flops 810024960 | bytes 15761408 | tf_op jit(solution)/shard_map/dot_general | solution.py:47
  1125.0 0.0 all-gather.5.cloned.1.call-update
  1125.0 72.1 %all-gather.5.cloned.1.call-done = bf16[512,8192]{1,0:T(8,128)(2,1)} async-done(((bf16[32,8192]{1,0:T(8,128)(2,1)}), bf16[512,8192]{1,0:T(8,128)(2,1)}) %all-gather.5.cloned.1.call-update) | async-done | bytes 8388624 | tf_op jit(solution)/shard_map/all_gather | solution.py:53
  1197.2 7.8 copy.16
Async XLA Ops:
  7.2 166.1 %copy-start = (f32[1,32,8192]{2,1,0:T(8,128)S(1)}, f32[1,32,8192]{2,1,0:T(8,128)}, u32[]{:S(2)}) copy-start(f32[1,32,8192]{2,1,0:T(8,128)} %param.6) | copy-start | bytes 3145732
  7.2 63.0 %all-gather.3.cloned.1.call-start = ((), (), s32[]{:S(2)}) async-start(), calls=%async_computation.2 | async-start | bytes 4456448 | tf_op jit(solution)/shard_map/all_gather | solution.py:34
  9.1 164.2 %reduce-scatter.2.cloned.1.call-start = ((), (), s32[]{:S(2)}) async-start(), calls=%async_computation.1 | async-start | bytes 8912896 | tf_op jit(solution)/shard_map/reduce_scatter | solution.py:28
  9.8 368.2 %all-reduce.7.cloned.1.call-start = ((), (), s32[]{:S(2)}) async-start(), calls=%async_computation.3 | async-start | bytes 262144 | tf_op jit(solution)/shard_map/psum | solution.py:42
  173.3 767.1 %copy-start.1 = (bf16[32,8192]{1,0:T(8,128)(2,1)S(1)}, bf16[32,8192]{1,0:T(8,128)(2,1)}, u32[]{:S(2)}) copy-start(bf16[32,8192]{1,0:T(8,128)(2,1)} %reduce-scatter.2.cloned.1.call-done) | copy-start | bytes 1572868
  248.2 270.2 %all-reduce.9.cloned.1.call-start = ((), (), s32[]{:S(2)}) async-start(), calls=%async_computation.4 | async-start | bytes 262144 | tf_op jit(solution)/shard_map/psum | solution.py:42
  380.3 278.3 %all-reduce.11.cloned.1.call-start = ((), (), s32[]{:S(2)}) async-start(), calls=%async_computation.5 | async-start | bytes 262144 | tf_op jit(solution)/shard_map/psum | solution.py:42
  520.6 278.3 %all-reduce.13.cloned.1.call-start = ((), (), s32[]{:S(2)}) async-start(), calls=%async_computation.6 | async-start | bytes 262144 | tf_op jit(solution)/shard_map/psum | solution.py:42
  660.8 278.5 %all-reduce.15.cloned.1.call-start = ((), (), s32[]{:S(2)}) async-start(), calls=%async_computation.7 | async-start | bytes 262144 | tf_op jit(solution)/shard_map/psum | solution.py:42
  801.2 311.0 %all-reduce.17.cloned.1.call-start = ((), (), s32[]{:S(2)}) async-start(), calls=%async_computation.8 | async-start | bytes 16777216 | tf_op jit(solution)/shard_map/psum | solution.py:46
  949.4 162.7 %copy-start.2 = (f32[32,8192]{1,0:T(8,128)S(1)}, f32[32,8192]{1,0:T(8,128)}, u32[]{:S(2)}) copy-start(f32[32,8192]{1,0:T(8,128)} %param.8) | copy-start | bytes 3145732
  949.4 247.7 %all-gather.5.cloned.1.call-start = ((), (), s32[]{:S(2)}) async-start(), calls=%async_computation.9 | async-start | bytes 8912896 | tf_op jit(solution)/shard_map/all_gather | solution.py:53
Sparse Core Ops, SparseCore 0:
  11.0 59.0 all-gather.2
  74.4 98.7 reduce-scatter.1
  248.3 129.7 all-reduce.6
  381.1 137.2 all-reduce.8
  521.3 137.2 all-reduce.10
  661.7 137.2 all-reduce.12
  802.0 137.2 all-reduce.14
  949.6 162.5 all-reduce.16
  1125.2 71.9 all-gather.4
where the time goes:
time: 1210 us
  waiting for transfers between devices  1080 us (89%)
  blocking collectives  68 us (6%)
  matrix products  37.3 us (3%)
  between operations  14.6 us (1%)
    psum x5, waiting for transfers between devices, on_device(): lax.psum(inner_left(orth, orth).astype(jnp.bfloat16), 'shard')  682 us
    psum x1, waiting for transfers between devices, on_device(): qnew = lax.psum(inner_left(merged, orth), ('island', 'shard')) / islands  162 us
    reduce_scatter x1, waiting for transfers between devices, on_device(): lax.psum_scatter(partials[0, 0], 'shard', scatter_dimension=0, tiled=True)  103 us
    all_gather x1, waiting for transfers between devices, on_device(): lax.all_gather(new_params.astype(jnp.bfloat16), 'shard', axis=0, tiled=True)  72.1 us
    all_gather x1, waiting for transfers between devices, on_device(): lax.all_gather(start_q.astype(jnp.bfloat16), 'shard', axis=0, tiled=True)  60.3 us
    psum x1, blocking collectives, on_device(): total = lax.psum(jnp.sum(proj * proj), 'shard')  42.1 us
    psum x1, blocking collectives, on_device(): lax.psum(local_proj.astype(jnp.bfloat16), 'island').astype(jnp.float32)  25.9 us
  transfers between devices with their start and end apart: 9, of which 9 were waited for; matrix products, arithmetic and copies ran while one was open for 0% of the time, Pallas kernels for 0%

commit v1 on v0

v1 whole, which is shorter than its diff:
```python
import jax
import jax.numpy as jnp
from jax import lax
from jax.experimental import pallas as pl
from jax.experimental.pallas import tpu as pltpu
from jax.sharding import Mesh
from jax.sharding import PartitionSpec as P

NS_ITERS = 5
F32 = jnp.float32
BF16 = jnp.bfloat16
ISLAND = ("x", "ylo")
ZY = ("z", "yhi")
SHARD = ("z", "yhi", "core")
CHIPS = ("x", "ylo", "z", "yhi")
SWAP = [(0, 1), (1, 0)]


def dot_nn(left, right):
    return jnp.dot(left, right, preferred_element_type=F32)


def dot_tn(left, right):
    return lax.dot_general(left, right, (((0,), (0,)), ((), ())), preferred_element_type=F32)


def dot_nt(left, right):
    return lax.dot_general(left, right, (((1,), (1,)), ((), ())), preferred_element_type=F32)


def orth_kernel(proj_ref, orth_ref):
    proj = proj_ref[...]
    orth = proj * lax.rsqrt(jnp.sum(proj * proj) + 1e-06)
    for _ in range(NS_ITERS):
        low = orth.astype(BF16)
        gram_mat = dot_tn(low, low).astype(BF16)
        orth = 1.5 * orth - 0.5 * dot_nn(low, gram_mat)
    orth_ref[...] = orth


def orthogonalize(proj):
    return pl.pallas_call(
        orth_kernel, out_shape=jax.ShapeDtypeStruct(proj.shape, F32)
    )(proj)


def swap_cores(value):
    return lax.ppermute(value, "core", SWAP)


def to_all_chips(value):
    return lax.all_to_all(
        jnp.broadcast_to(value[None], (64,) + value.shape), CHIPS, 0, 0, tiled=True
    )


def on_device(partials, error_buf, momentum, params, start_q):
    core = lax.axis_index("core")
    isl = lax.axis_index(ISLAND)
    shard = lax.axis_index(SHARD)

    own_q = lax.dynamic_slice(start_q, ((isl % 4) * 128, 0), (128, 256)).astype(BF16)
    q_cols = jnp.where(isl // 4 == core, own_q, swap_cores(own_q))

    parts = partials[0, 0].reshape(8, 2, 32, 8192)
    theirs = lax.dynamic_index_in_dim(parts, 1 - core, 1, keepdims=False)
    ours = lax.dynamic_index_in_dim(parts, core, 1, keepdims=False)
    pair = (ours.astype(F32) + swap_cores(theirs).astype(F32)).astype(BF16)
    pieces = lax.all_to_all(pair, ZY, 0, 0, tiled=True)
    merged = jnp.sum(pieces.astype(F32), 0) + error_buf[0]

    blocks = merged.astype(BF16).reshape(32, 8, 8, 128).transpose(2, 1, 0, 3).reshape(64, 32, 128)
    blocks = lax.all_to_all(blocks, CHIPS, 0, 0, tiled=True).reshape(8, 256, 128)
    half = (jnp.sum(blocks.astype(F32), 0) * 0.125).astype(BF16)
    other_half = swap_cores(half)

    before = (params - (0.7 * 0.9 * 0.9) * momentum).astype(BF16)
    before, half = lax.optimization_barrier((before, half))
    before_full = lax.all_gather(before, SHARD, axis=0, tiled=True)

    local_proj = dot_nn(half, q_cols).astype(BF16)
    local_proj = local_proj.reshape(32, 8, 2, 128).transpose(0, 2, 1, 3).reshape(64, 8, 128)
    terms = lax.all_to_all(local_proj, CHIPS, 0, 0, tiled=True)
    piece = jnp.sum(terms.astype(F32), 0).astype(BF16)
    proj_half = to_all_chips(piece).reshape(32, 2, 8, 128).transpose(0, 2, 1, 3).reshape(8, 32, 256)
    proj_other = swap_cores(proj_half)
    proj = jnp.where(
        core == 0,
        jnp.stack([proj_half, proj_other], 1),
        jnp.stack([proj_other, proj_half], 1),
    ).reshape(512, 256)
    orth = orthogonalize(proj.astype(F32))
    low_orth = orth.astype(BF16)

    half = half.reshape(8, 32, 128)
    other_half = other_half.reshape(8, 32, 128)
    mean = jnp.where(
        core == 0,
        jnp.stack([half, other_half], 1),
        jnp.stack([other_half, half], 1),
    ).reshape(512, 128)
    qnew_cols = dot_tn(mean, low_orth).astype(BF16)
    qnew_mine = lax.dynamic_slice(qnew_cols, (core * 64, 0), (64, 256))
    qnew_mine = to_all_chips(qnew_mine)
    qnew_other = swap_cores(qnew_mine)
    qnew = jnp.where(
        core == 0,
        jnp.stack([qnew_mine, qnew_other], 1),
        jnp.stack([qnew_other, qnew_mine], 1),
    )
    qnew = qnew.reshape(8, 8, 128, 256).transpose(1, 0, 2, 3).reshape(8192, 256)

    delta_full = dot_nt(low_orth, qnew)
    params_full = (before_full.astype(F32) - (0.7 * 1.9) * delta_full).astype(BF16)
    orth_rows = lax.dynamic_slice(low_orth, (shard * 32, 0), (32, 256))
    delta = dot_nt(orth_rows, qnew)
    new_error = merged - delta
    new_momentum = 0.9 * momentum + delta
    new_params = params - 0.7 * (delta + 0.9 * new_momentum)
    return (params_full, new_params, new_momentum, new_error[None])


def solution(mesh):
    fine = Mesh(mesh.devices.reshape(4, 2, 4, 2, 2), ("x", "ylo", "z", "yhi", "core"))
    in_specs = (
        P(ISLAND, SHARD, None, None),
        P(ISLAND, SHARD, None),
        P(SHARD, None),
        P(SHARD, None),
        P(SHARD, None),
    )
    out_specs = (P(), P(SHARD, None), P(SHARD, None), P(ISLAND, SHARD, None))
    return jax.shard_map(
        on_device, mesh=fine, in_specs=in_specs, out_specs=out_specs, check_vma=False
    )
```

time: 1210 us -> 224 us (0.19)
  waiting for transfers between devices: 1080 us -> 76.5 us
  starting transfers between devices: 0.55 us -> 35.3 us
  matrix products: 37.3 us -> 11.6 us
  blocking collectives: 68 us -> 51.5 us
  other arithmetic: 2.46 us -> 18.8 us
    psum x6 -> x0, waiting for transfers between devices: 845 us -> none  [the longest x5 682 us: on_device(): lax.psum(inner_left(orth, orth).astype(jnp.bfloat16), 'shard')]
    all_gather x2 -> x1, waiting for transfers between devices: 132 us -> 0.01 us  [on_device(): before_full = lax.all_gather(before, SHARD, axis=0, tiled=True)]
    reduce_scatter x1 -> x0, waiting for transfers between devices: 103 us -> none  [on_device(): lax.psum_scatter(partials[0, 0], 'shard', scatter_dimension=0, tiled=True)]
    psum x2 -> x0, blocking collectives: 68 us -> none  [the longest x1 42.1 us: on_device(): total = lax.psum(jnp.sum(proj * proj), 'shard')]
    all_to_all x0 -> x3, waiting for transfers between devices: none -> 63.3 us  [the longest x1 49.3 us: on_device(): pieces = lax.all_to_all(pair, ZY, 0, 0, tiled=True)]
    all_to_all x0 -> x2, blocking collectives: none -> 51.5 us  [the longest x1 38.2 us: to_all_chips(): lax.all_to_all(jnp.broadcast_to(value[None], (64,) + value.shape), CHIPS,...]
    dot_general x13 -> x4, matrix products: 37.3 us -> 11.6 us  [the longest x2 11.2 us: dot_nt(): lax.dot_general(left, right, (((1,), (1,)), ((), ())), preferred_element_...]
    all_to_all x0 -> x3, starting transfers between devices: none -> 19.9 us  [the longest x1 7.88 us: on_device(): pieces = lax.all_to_all(pair, ZY, 0, 0, tiled=True)]
  transfers between devices with their start and end apart: 9 -> 9, of which waited for: 9 -> 7; matrix products, arithmetic and copies ran while one was open for 0% -> 7% of each run, Pallas kernels for 0% -> 2%
where the time goes in v1:
time: 224 us; the launch traced here: 223 us
  waiting for transfers between devices  76.5 us (34%)
  blocking collectives  51.5 us (23%)
  starting transfers between devices  35.3 us (16%)
  other arithmetic  18.8 us (8%)
  between operations  14.2 us (6%)
  matrix products  11.6 us (5%)
  local copies, waits for them, and re-layouts  10.6 us (5%)
  Pallas kernels  4.58 us (2%)
    all_to_all x1, waiting for transfers between devices, on_device(): pieces = lax.all_to_all(pair, ZY, 0, 0, tiled=True)  49.3 us
    all_to_all x1, blocking collectives, to_all_chips(): lax.all_to_all(jnp.broadcast_to(value[None], (64,) + value.shape), CHIPS,...  38.2 us
    ppermute x5, starting transfers between devices, swap_cores(): return lax.ppermute(value, 'core', SWAP)  15.4 us
    all_to_all x1, blocking collectives, on_device(): terms = lax.all_to_all(local_proj, CHIPS, 0, 0, tiled=True)  13.3 us
    ppermute x5, waiting for transfers between devices, swap_cores(): return lax.ppermute(value, 'core', SWAP)  13.1 us
    dot_general x2, matrix products, dot_nt(): lax.dot_general(left, right, (((1,), (1,)), ((), ())), preferred_element_...  11.2 us
    all_to_all x1, waiting for transfers between devices, on_device(): lax.all_to_all(blocks, CHIPS, 0, 0, tiled=True).reshape(8, 256, 128)  10.1 us
    all_to_all x1, starting transfers between devices, on_device(): pieces = lax.all_to_all(pair, ZY, 0, 0, tiled=True)  7.88 us
  transfers between devices with their start and end apart: 9, of which 7 were waited for; matrix products, arithmetic and copies ran while one was open for 7% of the time, Pallas kernels for 2%

profile of v1, /device:TPU:1, one launch (start us, length us, event | category | flops | bytes accessed | tf_op | source)
XLA Modules:
  0.0 223.2 jit_solution(5119392528395355713)
XLA Ops:
  7.2 0.0 copy-start
  7.2 4.7 %dynamic-slice_bitcast_fusion = bf16[8,32,8192]{2,1,0:T(8,128)(2,1)} fusion(bf16[8,2,32,8192]{3,2,1,0:T(8,128)(2,1)} %bitcast.63, s32[]{:T(128)S(6)} %select_n.70), kind=kLoop, calls=%fused_computation.5 | loop fusion | bytes 8388612 | tf_op jit(solution)/shard_map/jit(dynamic_index_in_dim)/squeeze | solution.py:66
  11.9 1.4 collective-permute-start
  13.3 7.1 %collective-permute-done = bf16[8,32,8192]{2,1,0:T(8,128)(2,1)} collective-permute-done((bf16[8,32,8192]{2,1,0:T(8,128)(2,1)}, bf16[8,32,8192]{2,1,0:T(8,128)(2,1)}, u32[]{:S(2)}, u32[]{:S(2)}) %collective-permute-start) | collective-permute-done | bytes 4194336 | tf_op jit(solution)/shard_map/ppermute | solution.py:48
  20.4 7.0 %fusion = bf16[8,32,8192]{2,1,0:T(8,128)(2,1)} fusion(bf16[8,32,8192]{2,1,0:T(8,128)(2,1)} %collective-permute-done, bf16[8,2,32,8192]{3,2,1,0:T(8,128)(2,1)} %bitcast.64, s32[]{:T(128)S(6)} %select_n.69), kind=kLoop, calls=%fused_computation.2 | loop fusion | flops 8388608 | bytes 12582916 | tf_op jit(solution)/shard_map/convert_element_type | solution.py:68
  27.5 0.0 copy-start.5
  27.5 7.9 %all-to-all-start = ((bf16[8,32,8192]{2,1,0:T(8,128)(2,1)}), bf16[8,32,8192]{2,1,0:T(8,128)(2,1)}, u32[]{:S(2)}, u32[]{:S(2)}) async-start(bf16[8,32,8192]{2,1,0:T(8,128)(2,1)} %fusion), calls=%async_computation | async-start | bytes 8388608 | tf_op jit(solution)/shard_map/all_to_all | solution.py:69
  35.4 0.0 copy-done.5
  35.4 1.2 copy.13
  36.5 49.3 %all-to-all-done = bf16[8,32,8192]{2,1,0:T(8,128)(2,1)} async-done(((bf16[8,32,8192]{2,1,0:T(8,128)(2,1)}), bf16[8,32,8192]{2,1,0:T(8,128)(2,1)}, u32[]{:S(2)}, u32[]{:S(2)}) %all-to-all-start) | async-done | bytes 4194336 | tf_op jit(solution)/shard_map/all_to_all | solution.py:69
  85.8 0.0 copy-start.7
  85.8 3.0 %convert_reduce_fusion = f32[32,8192]{1,0:T(8,128)S(1)} fusion(bf16[8,32,8192]{2,1,0:T(8,128)(2,1)} %all-to-all-done), kind=kLoop, calls=%fused_computation.3 | loop fusion | flops 3932160 | bytes 5242880 | tf_op jit(solution)/shard_map/reduce_sum | solution.py:70
  88.8 0.0 copy-start.3
  88.8 0.2 copy.12
  89.0 0.0 copy-done.7
  89.0 0.2 fusion.3
  89.2 1.1 copy.10
  90.3 7.0 %all-to-all-start.1 = ((bf16[64,32,128]{2,1,0:T(8,128)(2,1)}), bf16[64,32,128]{2,1,0:T(8,128)(2,1)S(1)}, u32[]{:S(2)}, u32[]{:S(2)}) async-start(bf16[64,32,128]{2,1,0:T(8,128)(2,1)} %bitcast.69), calls=%async_computation.1 | async-start | bytes 1048576 | tf_op jit(solution)/shard_map/all_to_all | solution.py:73
  97.3 0.0 all-gather.2.cloned.1.call-start
  97.3 0.0 copy-done.3
  97.3 2.1 subtract_convert_fusion.1
  99.5 10.1 %all-to-all-done.1 = bf16[64,32,128]{2,1,0:T(8,128)(2,1)S(1)} async-done(((bf16[64,32,128]{2,1,0:T(8,128)(2,1)}), bf16[64,32,128]{2,1,0:T(8,128)(2,1)S(1)}, u32[]{:S(2)}, u32[]{:S(2)}) %all-to-all-start.1) | async-done | bytes 524320 | tf_op jit(solution)/shard_map/all_to_all | solution.py:73
  109.6 0.1 convert_reduce_fusion.1
  109.6 0.0 all-gather.2.cloned.1.call-update
  109.7 0.0 copy-done
  109.7 2.0 collective-permute-start.1
  111.7 0.9 collective-permute-done.1
  112.6 0.2 convolution_convert_fusion
  112.8 13.3 %all_to_all.25 = bf16[64,8,128]{2,1,0:T(8,128)(2,1)S(1)} all-to-all(bf16[64,8,128]{2,1,0:T(8,128)(2,1)S(1)} %bitcast.74), channel_id=1, replica_groups=mesh['x'=4,'ylo'=2,'z'=4,'yhi'=2,'core'=2] {'x','ylo','z','yhi'}, dimensions={0} | all-to-all | bytes 262144 | tf_op jit(solution)/shard_map/all_to_all | solution.py:83
  126.1 0.1 reduce_sum.35
  126.2 0.7 broadcast_in_dim.6
  126.9 5.0 %all-to-all-start.3 = ((bf16[64,8,128]{2,1,0:T(8,128)(2,1)}), bf16[64,8,128]{2,1,0:T(8,128)(2,1)S(1)}, u32[]{:S(2)}, u32[]{:S(2)}) async-start(bf16[64,8,128]{2,1,0:T(8,128)(2,1)} %broadcast_in_dim.6), calls=%async_computation.3 | async-start | bytes 262144 | tf_op jit(solution)/shard_map/all_to_all | solution.py:52
  131.9 4.7 %collective-permute-start.3 = (bf16[256,128]{1,0:T(8,128)(2,1)S(1)}, bf16[256,128]{1,0:T(8,128)(2,1)S(1)}, u32[]{:S(2)}, u32[]{:S(2)}) collective-permute-start(bf16[256,128]{1,0:T(8,128)(2,1)S(1)} %multiply_convert_fusion), channel_id=1, source_target_pairs={{0,1},{1,0},{2,3},{3,2},{4,5},{5,4},{6,7},{7,6},{8,9},{9,8},{10,11... | collective-permute-start | bytes 196616 | tf_op jit(solution)/shard_map/ppermute | solution.py:48
  136.6 4.0 %all-to-all-done.3 = bf16[64,8,128]{2,1,0:T(8,128)(2,1)S(1)} async-done(((bf16[64,8,128]{2,1,0:T(8,128)(2,1)}), bf16[64,8,128]{2,1,0:T(8,128)(2,1)S(1)}, u32[]{:S(2)}, u32[]{:S(2)}) %all-to-all-start.3) | async-done | bytes 131104 | tf_op jit(solution)/shard_map/all_to_all | solution.py:52
  140.6 5.8 %collective-permute-start.2 = (bf16[8,32,256]{2,1,0:T(8,128)(2,1)S(1)}, bf16[8,32,256]{2,1,0:T(8,128)(2,1)S(1)}, u32[]{:S(2)}, u32[]{:S(2)}) collective-permute-start(bf16[8,32,256]{2,1,0:T(8,128)(2,1)S(1)} %bitcast.71), channel_id=1, source_target_pairs={{0,1},{1,0},{2,3},{3,2},{4,5},{5,4},{6,7},{7,6},{8,9},{9,8},{10,11... | collective-permute-start | bytes 393224 | tf_op jit(solution)/shard_map/ppermute | solution.py:48
  146.4 0.0 collective-permute-done.3
  146.4 1.0 collective-permute-done.2
  147.4 0.8 bitcast_convert_fusion.proj_ref
  148.3 4.6 %shard_map.84 = f32[512,256]{1,0:T(8,128)} custom-call(f32[512,256]{1,0:T(8,128)} %bitcast_convert_fusion.proj_ref), custom_call_target="tpu_custom_call" | custom-call | tf_op jit(solution)/shard_map/pallas_call | solution.py:42
  152.9 1.1 convert_element_type.71
  153.9 0.2 fusion.11
  154.2 0.2 broadcast_in_dim.7
  154.4 38.2 %all_to_all.26 = bf16[64,64,256]{2,1,0:T(8,128)(2,1)} all-to-all(bf16[64,64,256]{2,1,0:T(8,128)(2,1)S(1)} %broadcast_in_dim.7), channel_id=1, replica_groups=mesh['x'=4,'ylo'=2,'z'=4,'yhi'=2,'core'=2] {'x','ylo','z','yhi'}, dimensions={0} | all-to-all | bytes 4194304 | tf_op jit(solution)/shard_map/all_to_all | solution.py:52
  192.6 1.4 collective-permute-start.4
  194.0 4.1 %collective-permute-done.4 = bf16[64,64,256]{2,1,0:T(8,128)(2,1)} collective-permute-done((bf16[64,64,256]{2,1,0:T(8,128)(2,1)}, bf16[64,64,256]{2,1,0:T(8,128)(2,1)}, u32[]{:S(2)}, u32[]{:S(2)}) %collective-permute-start.4) | collective-permute-done | bytes 2097184 | tf_op jit(solution)/shard_map/ppermute | solution.py:48
  198.2 4.4 %maximum_select_fusion = bf16[64,2,64,256]{3,2,1,0:T(8,128)(2,1)S(1)} fusion(bf16[64,1,64,256]{3,2,1,0:T(8,128)(2,1)} %bitcast.21, bf16[64,1,64,256]{3,2,1,0:T(8,128)(2,1)} %bitcast.20, pred[]{:T(512)S(6)} %eq.10), kind=kLoop, calls=%fused_computation.4 | loop fusion | flops 6291456 | bytes 8388609 | tf_op jit(solution)/shard_map/jit(_where)/select_n | solution.py:106
  202.6 0.0 copy-start.4
  202.6 0.0 copy-start.6
  202.6 0.5 copy.11
  203.1 0.0 copy-start.2
  203.1 2.0 copy-done.2
  205.1 0.0 copy-done.4
  205.1 0.0 copy-done.6
  205.1 3.0 %multiply_subtract_fusion = (f32[32,8192]{1,0:T(8,128)}, f32[32,8192]{1,0:T(8,128)}, f32[1,32,8192]{2,1,0:T(8,128)}) fusion(f32[32,8192]{1,0:T(8,128)S(1)} %copy-done.3, f32[32,8192]{1,0:T(8,128)S(1)} %copy-done.4, f32[32,8192]{1,0:T(8,128)S(1)} %convert_reduce_fusion, f32[1,32,8192]{2,1,0:T(8,128)S(1)} %copy-done.6, bf16[8192,256]{1,0:T(8,128)(2,1)S(1)} %bitcast.59, ...), kind=kOutput, calls=%fused_computation.11 | convolution fusion | flops 136314880 | bytes 11550724 | tf_op jit(solution)/shard_map/dot_general | solution.py:28
  208.1 0.0 all-gather.2.cloned.1.call-done
  208.1 0.0 copy-start.1
  208.1 8.2 %subtract_convert_fusion = bf16[512,8192]{1,0:T(8,128)(2,1)} fusion(bf16[512,8192]{1,0:T(8,128)(2,1)} %all-gather.2.cloned.1.call-done, bf16[512,256]{1,0:T(8,128)(2,1)S(1)} %convert_element_type.71, bf16[8192,256]{1,0:T(8,128)(2,1)} %bitcast.60), kind=kOutput, calls=%fused_computation | convolution fusion | flops 2164260864 | bytes 21233664 | tf_op jit(solution)/shard_map/dot_general | solution.py:28
  216.3 0.0 copy-done.1
  (5 shorter events, 0.1 us)
Async XLA Ops:
  7.2 102.5 %copy-start = (f32[512,256]{1,0:T(8,128)S(1)}, f32[512,256]{1,0:T(8,128)}, u32[]{:S(2)}) copy-start(f32[512,256]{1,0:T(8,128)} %param.9) | copy-start | bytes 1572868
  11.9 8.6 %collective-permute-start = (bf16[8,32,8192]{2,1,0:T(8,128)(2,1)}, bf16[8,32,8192]{2,1,0:T(8,128)(2,1)}, u32[]{:S(2)}, u32[]{:S(2)}) collective-permute-start(bf16[8,32,8192]{2,1,0:T(8,128)(2,1)} %dynamic-slice_bitcast_fusion), channel_id=1, source_target_pairs={{0,1},{1,0},{2,3},{3,2},{4,5},{5,4},{6,7},{7,6},{8,9},{9,8},{10,11... | collective-permute-start | bytes 12582920 | tf_op jit(solution)/shard_map/ppermute | solution.py:48
  27.5 7.9 %copy-start.5 = (f32[1,32,8192]{2,1,0:T(8,128)S(1)}, f32[1,32,8192]{2,1,0:T(8,128)}, u32[]{:S(2)}) copy-start(f32[1,32,8192]{2,1,0:T(8,128)} %param.6) | copy-start | bytes 3145732
  27.5 58.3 %all-to-all-start = ((bf16[8,32,8192]{2,1,0:T(8,128)(2,1)}), bf16[8,32,8192]{2,1,0:T(8,128)(2,1)}, u32[]{:S(2)}, u32[]{:S(2)}) async-start(bf16[8,32,8192]{2,1,0:T(8,128)(2,1)} %fusion), calls=%async_computation | async-start | bytes 8388608 | tf_op jit(solution)/shard_map/all_to_all | solution.py:69
  85.8 3.2 %copy-start.7 = (f32[4,8,64,128]{3,2,1,0:T(8,128)S(1)}, f32[4,8,64,128]{3,2,1,0:T(8,128)}, u32[]{:S(2)}) copy-start(f32[4,8,64,128]{3,2,1,0:T(8,128)} %copy.13) | copy-start | bytes 3145732
  88.8 8.5 %copy-start.3 = (f32[32,8192]{1,0:T(8,128)S(1)}, f32[32,8192]{1,0:T(8,128)}, u32[]{:S(2)}) copy-start(f32[32,8192]{1,0:T(8,128)} %param.8) | copy-start | bytes 3145732
  90.3 19.3 %all-to-all-start.1 = ((bf16[64,32,128]{2,1,0:T(8,128)(2,1)}), bf16[64,32,128]{2,1,0:T(8,128)(2,1)S(1)}, u32[]{:S(2)}, u32[]{:S(2)}) async-start(bf16[64,32,128]{2,1,0:T(8,128)(2,1)} %bitcast.69), calls=%async_computation.1 | async-start | bytes 1048576 | tf_op jit(solution)/shard_map/all_to_all | solution.py:73
  97.3 110.8 %all-gather.2.cloned.1.call-start = ((), (), s32[]{:S(2)}) async-start(), calls=%async_computation.5 | async-start | bytes 8912896 | tf_op jit(solution)/shard_map/all_gather | solution.py:79
  109.7 2.9 %collective-permute-start.1 = (bf16[128,256]{1,0:T(8,128)(2,1)S(1)}, bf16[128,256]{1,0:T(8,128)(2,1)S(1)}, u32[]{:S(2)}, u32[]{:S(2)}) collective-permute-start(bf16[128,256]{1,0:T(8,128)(2,1)S(1)} %dynamic-slice_convert_fusion), channel_id=1, source_target_pairs={{0,1},{1,0},{2,3},{3,2},{4,5},{5,4},{6,7},{7,6},{8,9},{9,8},{10,11... | collective-permute-start | bytes 196616 | tf_op jit(solution)/shard_map/ppermute | solution.py:48
  126.9 13.7 %all-to-all-start.3 = ((bf16[64,8,128]{2,1,0:T(8,128)(2,1)}), bf16[64,8,128]{2,1,0:T(8,128)(2,1)S(1)}, u32[]{:S(2)}, u32[]{:S(2)}) async-start(bf16[64,8,128]{2,1,0:T(8,128)(2,1)} %broadcast_in_dim.6), calls=%async_computation.3 | async-start | bytes 262144 | tf_op jit(solution)/shard_map/all_to_all | solution.py:52
  131.9 14.5 %collective-permute-start.3 = (bf16[256,128]{1,0:T(8,128)(2,1)S(1)}, bf16[256,128]{1,0:T(8,128)(2,1)S(1)}, u32[]{:S(2)}, u32[]{:S(2)}) collective-permute-start(bf16[256,128]{1,0:T(8,128)(2,1)S(1)} %multiply_convert_fusion), channel_id=1, source_target_pairs={{0,1},{1,0},{2,3},{3,2},{4,5},{5,4},{6,7},{7,6},{8,9},{9,8},{10,11... | collective-permute-start | bytes 196616 | tf_op jit(solution)/shard_map/ppermute | solution.py:48
  140.6 6.8 %collective-permute-start.2 = (bf16[8,32,256]{2,1,0:T(8,128)(2,1)S(1)}, bf16[8,32,256]{2,1,0:T(8,128)(2,1)S(1)}, u32[]{:S(2)}, u32[]{:S(2)}) collective-permute-start(bf16[8,32,256]{2,1,0:T(8,128)(2,1)S(1)} %bitcast.71), channel_id=1, source_target_pairs={{0,1},{1,0},{2,3},{3,2},{4,5},{5,4},{6,7},{7,6},{8,9},{9,8},{10,11... | collective-permute-start | bytes 393224 | tf_op jit(solution)/shard_map/ppermute | solution.py:48
  192.6 5.5 %collective-permute-start.4 = (bf16[64,64,256]{2,1,0:T(8,128)(2,1)}, bf16[64,64,256]{2,1,0:T(8,128)(2,1)}, u32[]{:S(2)}, u32[]{:S(2)}) collective-permute-start(bf16[64,64,256]{2,1,0:T(8,128)(2,1)} %all_to_all.26), channel_id=1, source_target_pairs={{0,1},{1,0},{2,3},{3,2},{4,5},{5,4},{6,7},{7,6},{8,9},{9,8},{10,11... | collective-permute-start | bytes 6291464 | tf_op jit(solution)/shard_map/ppermute | solution.py:48
  202.6 2.5 %copy-start.4 = (f32[32,8192]{1,0:T(8,128)S(1)}, f32[32,8192]{1,0:T(8,128)}, u32[]{:S(2)}) copy-start(f32[32,8192]{1,0:T(8,128)} %param.7) | copy-start | bytes 3145732
  202.6 2.5 %copy-start.6 = (f32[1,32,8192]{2,1,0:T(8,128)S(1)}, f32[1,32,8192]{2,1,0:T(8,128)}, u32[]{:S(2)}) copy-start(f32[1,32,8192]{2,1,0:T(8,128)} %param.6) | copy-start | bytes 3145732
  203.1 2.0 copy-start.2
  208.1 8.2 %copy-start.1 = (f32[512,256]{1,0:T(8,128)S(1)}, f32[512,256]{1,0:T(8,128)}, u32[]{:S(2)}) copy-start(f32[512,256]{1,0:T(8,128)} %param.9) | copy-start | bytes 1572868
Sparse Core Ops, SparseCore 0:
  109.8 94.3 all-gather.1

commit v2 on v1

v2 whole, which is shorter than its diff:
```python
import functools

import jax
import jax.numpy as jnp
from jax import lax
from jax.experimental import pallas as pl
from jax.experimental.pallas import tpu as pltpu
from jax.sharding import Mesh
from jax.sharding import PartitionSpec as P

NS_ITERS = 5
F32 = jnp.float32
BF16 = jnp.bfloat16
ISLAND = ("x", "ylo")
ZY = ("z", "yhi")
SHARD = ("z", "yhi", "core")
SWAP = [(0, 1), (1, 0)]
CHIPS = ("x", "ylo", "z", "yhi")
WIDE = 4096
VMEM = 60 * 1024 * 1024


def dot_nn(left, right):
    return jnp.dot(left, right, preferred_element_type=F32)


def dot_tn(left, right):
    return lax.dot_general(left, right, (((0,), (0,)), ((), ())), preferred_element_type=F32)


def dot_nt(left, right):
    return lax.dot_general(left, right, (((1,), (1,)), ((), ())), preferred_element_type=F32)


def factor_kernel(own_ref, other_ref, out):
    def left_factor(ref):
        return jnp.concatenate([ref[0], ref[1]], 1).astype(F32)

    own, other = left_factor(own_ref), left_factor(other_ref)
    scale = lax.rsqrt(jnp.sum(own * own) + jnp.sum(other * other) + 1e-06)
    own, other = own * scale, other * scale
    for _ in range(NS_ITERS):
        low_own, low_other = own.astype(BF16), other.astype(BF16)
        gram_mat = (dot_tn(low_own, low_own) + dot_tn(low_other, low_other)).astype(BF16)
        own = 1.5 * own - 0.5 * dot_nn(low_own, gram_mat)
        other = 1.5 * other - 0.5 * dot_nn(low_other, gram_mat)
    low_own, low_other = own.astype(BF16), other.astype(BF16)
    qnew = dot_tn(own_ref[2], low_own) + dot_tn(other_ref[2], low_other)
    delta = dot_nt(low_own, qnew.astype(BF16))
    weights = (own_ref[3].astype(F32) - (0.7 * 1.9) * delta).astype(BF16)
    delta = delta.astype(BF16).reshape(8, 32, 128)

    @pl.loop(0, 8)
    def _(island):
        for chip in range(8):
            out[island * 8 + chip, :256] = weights
            out[island * 8 + chip, 256:] = delta[chip]


def factors(own, other):
    vmem = pl.BlockSpec(memory_space=pltpu.VMEM)
    return pl.pallas_call(
        factor_kernel,
        in_specs=[vmem, vmem],
        out_specs=vmem,
        out_shape=jax.ShapeDtypeStruct((64, 288, 128), BF16),
        compiler_params=pltpu.CompilerParams(vmem_limit_bytes=32 * 1024 * 1024),
    )(own, other)


def put_weights(moved, full):
    for n in range(8):
        full[:, 0, :, n * 128 : (n + 1) * 128] = moved[n, 0, :256].reshape(8, 32, 128)


def own_kernel(place, moved, merged, momentum, params, full, new_params, new_momentum, new_error):
    put_weights(moved, full)
    for n in range(8):
        cols = slice(n * 128, (n + 1) * 128)
        delta = moved[n, 0, 256:].astype(F32)
        new_error[:, cols] = merged[:, cols] - delta
        step = 0.9 * momentum[:, cols] + delta
        new_momentum[:, cols] = step
        new_params[:, cols] = params[:, cols] - 0.7 * (delta + 0.9 * step)


def other_kernel(place, moved, _, full):
    put_weights(moved, full)


MOVED_SPEC = pl.BlockSpec((8, 1, 288, 128), lambda g, _: (0, g, 0, 0))
FULL_SHAPE = jax.ShapeDtypeStruct((8, 2, 32, 8192), BF16)


def own_rows(place, moved, merged, momentum, params):
    rows = pl.BlockSpec((32, 1024), lambda g, _: (0, g))
    row_shape = jax.ShapeDtypeStruct((32, 8192), F32)
    return pl.pallas_call(
        own_kernel,
        grid_spec=pltpu.PrefetchScalarGridSpec(
            num_scalar_prefetch=1,
            grid=(8,),
            in_specs=[MOVED_SPEC, rows, rows, rows],
            out_specs=[
                pl.BlockSpec((8, 1, 32, 1024), lambda g, at: (0, at[0], 0, g)), rows, rows, rows,
            ],
        ),
        out_shape=[FULL_SHAPE, row_shape, row_shape, row_shape],
        compiler_params=pltpu.CompilerParams(vmem_limit_bytes=VMEM),
    )(place, moved.reshape(8, 8, 288, 128), merged, momentum, params)


def other_rows(place, moved, full):
    return pl.pallas_call(
        other_kernel,
        grid_spec=pltpu.PrefetchScalarGridSpec(
            num_scalar_prefetch=1,
            grid=(8,),
            in_specs=[MOVED_SPEC, pl.BlockSpec(memory_space=pl.ANY)],
            out_specs=pl.BlockSpec((8, 1, 32, 1024), lambda g, at: (0, 1 - at[0], 0, g)),
        ),
        out_shape=FULL_SHAPE,
        input_output_aliases={2: 0},
        compiler_params=pltpu.CompilerParams(vmem_limit_bytes=VMEM),
    )(place, moved.reshape(8, 8, 288, 128), full)


def swap_cores(value):
    return lax.ppermute(value, "core", SWAP)


def along_z(value, step):
    return lax.ppermute(value, "z", [(at, (at + step) % 4) for at in range(4)])


def copies(value, axes):
    count = lax.axis_size(axes)
    value = jnp.broadcast_to(value[None], (count,) + value.shape)
    return lax.all_to_all(value, axes, 0, 0, tiled=True)


def ring_order(ring, z):
    ring = jnp.stack([ring[0], ring[3], ring[2], ring[1]])
    return lax.dynamic_slice_in_dim(jnp.concatenate([ring, ring]), (4 - z) % 4, 4, 0)


def block_at(place, k, j, side):
    return lax.rem(place[1] + k, 4) * 4 + lax.rem(place[2] + j, 2) * 2 + lax.rem(place[0] + side, 2)


BLOCKS = [(k, j) for k in range(4) for j in range(2)]


def block_copies(place, parts, out, sems, side, half):
    return [
        pltpu.make_async_copy(
            parts.at[block_at(place, k, j, side), :, pl.ds(half * WIDE, WIDE)],
            out.at[k, j],
            sems.at[k, j],
        )
        for k, j in BLOCKS
    ]


def theirs_kernel(half, place, parts, out, sems):
    copies = block_copies(place, parts, out, sems, 1, half)
    for copy in copies:
        copy.start()
    for copy in copies:
        copy.wait()


def theirs(place, parts, half):
    return pl.pallas_call(
        functools.partial(theirs_kernel, half),
        in_specs=[
            pl.BlockSpec(memory_space=pltpu.SMEM),
            pl.BlockSpec(memory_space=pl.ANY),
        ],
        out_specs=pl.BlockSpec(memory_space=pltpu.VMEM),
        out_shape=pltpu.VMEM((4, 2, 32, WIDE), BF16),
        scratch_shapes=[pltpu.SemaphoreType.DMA((4, 2))],
    )(place, parts)


def add(left, right):
    return (left.astype(F32) + right.astype(F32)).astype(BF16)


def pair_sums(half, place, parts, received, ours, theirs, sems, in_sems):
    copies = list(zip(
        block_copies(place, parts, ours, sems, 0, half),
        [pltpu.make_async_copy(received.at[k, j], theirs.at[k, j], in_sems.at[k, j]) for k, j in BLOCKS],
    ))
    for own, other in copies:
        own.start()
        other.start()
    for (k, j), (own, other) in zip(BLOCKS, copies):
        own.wait()
        other.wait()
        yield k, j, add(ours[k, j], theirs[k, j])


def right_kernel(place, parts, received, keep, send, *scratch):
    for k, j, total in pair_sums(1, place, parts, received, *scratch):
        (send if j else keep)[k] = total


def left_kernel(place, parts, received, piece, keep, up, far, down, *scratch):
    outs = (keep, up, far, down)
    for out in outs[1:]:
        out[:, WIDE:] = piece[...]
    for k, j, total in pair_sums(0, place, parts, received, *scratch):
        outs[k][32 * j : 32 * j + 32, :WIDE] = total


def pair_call(kernel, shapes, place, parts, received, *rest):
    vmem = pl.BlockSpec(memory_space=pltpu.VMEM)
    anywhere = pl.BlockSpec(memory_space=pl.ANY)
    return pl.pallas_call(
        kernel,
        in_specs=[pl.BlockSpec(memory_space=pltpu.SMEM), anywhere, anywhere] + [vmem] * len(rest),
        out_specs=[vmem] * len(shapes),
        out_shape=[pltpu.VMEM(shape, BF16) for shape in shapes],
        scratch_shapes=[pltpu.VMEM((4, 2, 32, WIDE), BF16)] * 2 + [pltpu.SemaphoreType.DMA((4, 2))] * 2,
    )(place, parts, received, *rest)


def turn_kernel(left, up, far, down, piece, keep, back):
    def total(rows):
        value = left[rows, :].astype(F32)
        for ref in (up, far, down):
            value = value + ref[rows, :WIDE].astype(F32)
        return value

    keep[...] = total(slice(0, 32))
    back[:, :WIDE] = total(slice(32, 64)).astype(BF16)
    for k, ref in enumerate((piece, up, far, down)):
        at = 0 if k == 0 else WIDE
        for j in range(2):
            back[:, WIDE + k * 1024 + j * 512 : WIDE + k * 1024 + (j + 1) * 512] = ref[
                32 * j : 32 * j + 32, at : at + 512
            ]


def turn(left, up, far, down, piece):
    vmem = pl.BlockSpec(memory_space=pltpu.VMEM)
    return pl.pallas_call(
        turn_kernel,
        in_specs=[vmem] * 5,
        out_specs=[vmem] * 2,
        out_shape=[pltpu.VMEM((32, WIDE), F32), pltpu.VMEM((32, 2 * WIDE), BF16)],
    )(left, up, far, down, piece)


def summed_rows(partials, piece, place, z, yhi):
    parts = partials.reshape(16, 32, 8192)
    right_out, parts_later = lax.optimization_barrier((theirs(place, parts, 1), parts))
    right_in, left_in = swap_cores(right_out), swap_cores(theirs(place, parts_later, 0))
    right, across = pair_call(right_kernel, [(4, 32, WIDE)] * 2, place, parts, right_in)
    left_in, right = lax.optimization_barrier((left_in, right))
    across = lax.ppermute(across, "yhi", SWAP)
    shapes = [(64, WIDE)] + [(64, WIDE + 512)] * 3
    left, up, far, down = pair_call(left_kernel, shapes, place, parts, left_in, piece)
    far, up, down = along_z(far, 2), along_z(up, 1), along_z(down, 3)
    sums = [right[k].astype(F32) + across[k].astype(F32) for k in range(4)]
    moved = [along_z(sums[k].astype(BF16), k) for k in (2, 1, 3)]
    left, sent = turn(left, up, far, down, piece)
    back = lax.ppermute(sent, "yhi", SWAP)
    right = sums[0] + sum(moved_in.astype(F32) for moved_in in moved)
    left = left + back[:, :WIDE].astype(F32)
    ours, others = (
        ring_order([value[:, WIDE + k * 1024 : WIDE + (k + 1) * 1024] for k in range(4)], z)
        for value in (sent, back)
    )
    pieces = jnp.where(yhi == 0, jnp.stack([ours, others], 1), jnp.stack([others, ours], 1))
    return jnp.concatenate([left, right], 1), pieces.reshape(8, 32, 4, 256)


def on_device(partials, error_buf, momentum, params, start_q):
    core, z, yhi = (lax.axis_index(name) for name in ("core", "z", "yhi"))
    isl = lax.axis_index(ISLAND)
    place = jnp.stack([core, z, yhi]).astype(jnp.int32)

    own_q = lax.dynamic_slice(start_q, ((isl % 4) * 128, 0), (128, 256)).astype(BF16)
    piece = jnp.concatenate([own_q[:64], own_q[64:]], 1)
    merged, pieces = summed_rows(partials[0, 0], piece, place, z, yhi)
    merged = merged + error_buf[0]
    q_own = jnp.stack([pieces[:, :, n] for n in (0, 2, 1, 3)], 1).reshape(1024, 256)
    q_cols = jnp.where(isl // 4 == core, q_own, swap_cores(q_own))

    def columns(value):
        return lax.dynamic_index_in_dim(value.reshape(32, 8, 8, 128), isl, 2, False)

    before = (columns(params) - (0.7 * 0.9 * 0.9) * columns(momentum)).astype(BF16)
    before = before.transpose(1, 0, 2)

    blocks = merged.astype(BF16).reshape(32, 8, 8, 128).transpose(2, 1, 0, 3)
    blocks = lax.all_to_all(blocks, ISLAND, 0, 0, tiled=True)
    mean = (jnp.sum(blocks.astype(F32), 0) * 0.125).astype(BF16)
    local_proj = dot_nn(mean.transpose(1, 0, 2).reshape(32, 1024), q_cols).astype(BF16)
    proj = jnp.sum(copies(local_proj, ISLAND).astype(F32), 0).astype(BF16)

    proj = proj.reshape(32, 2, 128).transpose(1, 0, 2)
    proj = jnp.broadcast_to(proj[None], (8, 2, 32, 128))
    own = jnp.concatenate([proj, mean[:, None], before[:, None]], 1)
    own = lax.all_to_all(own, ZY, 0, 0, tiled=True).transpose(1, 0, 2, 3).reshape(4, 256, 128)
    other = swap_cores(own)

    moved_own = lax.all_to_all(factors(own, other), CHIPS, 0, 0, tiled=True)
    moved_other = swap_cores(moved_own)
    params_full, new_params, new_momentum, new_error = own_rows(
        place, moved_own, merged, momentum, params
    )
    params_full = other_rows(place, moved_other, params_full)
    return (params_full.reshape(512, 8192), new_params, new_momentum, new_error[None])


def solution(mesh):
    fine = Mesh(mesh.devices.reshape(4, 2, 4, 2, 2), ("x", "ylo", "z", "yhi", "core"))
    in_specs = (
        P(ISLAND, SHARD, None, None),
        P(ISLAND, SHARD, None),
        P(SHARD, None),
        P(SHARD, None),
        P(SHARD, None),
    )
    out_specs = (P(), P(SHARD, None), P(SHARD, None), P(ISLAND, SHARD, None))
    return jax.shard_map(
        on_device, mesh=fine, in_specs=in_specs, out_specs=out_specs, check_vma=False
    )
```

time: 224 us -> 204 us (0.911)
  waiting for transfers between devices: 76.5 us -> 36.2 us
  Pallas kernels: 4.58 us -> 36.2 us
  blocking collectives: 51.5 us -> 75.8 us
  between operations: 14.2 us -> 1.09 us
  matrix products: 11.6 us -> 1.25 us
  other arithmetic: 18.8 us -> 8.47 us
    all_to_all x3 -> x2, waiting for transfers between devices: 63.3 us -> 7.36 us  [the longest x1 5.22 us: copies(): return lax.all_to_all(value, axes, 0, 0, tiled=True)]
    pallas_call x1 -> x8, Pallas kernels: 4.58 us -> 36.2 us  [the longest x1 9.41 us: own_rows(): pl.pallas_call(own_kernel, grid_spec=pltpu.PrefetchScalarGridSpec(num_sca...]
    ppermute x0 -> x8, waiting for transfers between devices: none -> 27.6 us  [the longest x6 22.8 us: along_z(): return lax.ppermute(value, 'z', [(at, (at + step) % 4) for at in range(4)])]
    all_to_all x2, blocking collectives: 51.5 us -> 75.8 us  [the longest x1 62.3 us: on_device(): moved_own = lax.all_to_all(factors(own, other), CHIPS, 0, 0, tiled=True)]
    ppermute x0 -> x8, starting transfers between devices: none -> 15.5 us  [the longest x6 9.59 us: along_z(): return lax.ppermute(value, 'z', [(at, (at + step) % 4) for at in range(4)])]
    ppermute x5, waiting for transfers between devices: 13.1 us -> 1.17 us  [swap_cores(): return lax.ppermute(value, 'core', SWAP)]
    dot_general x3 -> x0, matrix products: 11.5 us -> none  [the longest x2 11.2 us: dot_nt(): lax.dot_general(left, right, (((1,), (1,)), ((), ())), preferred_element_...]
    all_to_all x3 -> x2, starting transfers between devices: 19.9 us -> 9.07 us  [the longest x1 4.92 us: copies(): return lax.all_to_all(value, axes, 0, 0, tiled=True)]
  transfers between devices with their start and end apart: 9 -> 15, of which waited for: 7 -> 7; matrix products, arithmetic and copies ran while one was open for 7% -> 7% of each run, Pallas kernels for 2% -> 9%
where the time goes in v2:
time: 204 us; the launch traced here: 203 us
  blocking collectives  75.8 us (37%)
  Pallas kernels  36.2 us (18%)
  waiting for transfers between devices  36.2 us (18%)
  starting transfers between devices  33.5 us (16%)
  local copies, waits for them, and re-layouts  10.5 us (5%)
  other arithmetic  8.47 us (4%)
    all_to_all x1, blocking collectives, on_device(): moved_own = lax.all_to_all(factors(own, other), CHIPS, 0, 0, tiled=True)  62.3 us
    ppermute x6, waiting for transfers between devices, along_z(): return lax.ppermute(value, 'z', [(at, (at + step) % 4) for at in range(4)])  22.8 us
    all_to_all x1, blocking collectives, on_device(): lax.all_to_all(own, ZY, 0, 0, tiled=True).transpose(1, 0, 2, 3)  13.5 us
    ppermute x6, starting transfers between devices, along_z(): return lax.ppermute(value, 'z', [(at, (at + step) % 4) for at in range(4)])  9.59 us
    pallas_call x1, Pallas kernels, own_rows(): pl.pallas_call(own_kernel, grid_spec=pltpu.PrefetchScalarGridSpec(num_sca...  9.41 us
    ppermute x5, starting transfers between devices, swap_cores(): return lax.ppermute(value, 'core', SWAP)  8.93 us
    pallas_call x1, Pallas kernels, other_rows(): pl.pallas_call(other_kernel, grid_spec=pltpu.PrefetchScalarGridSpec(num_s...  7.93 us
    pallas_call x2, Pallas kernels, theirs(): pl.pallas_call(functools.partial(theirs_kernel, half), in_specs=[pl.Block...  7.12 us
  transfers between devices with their start and end apart: 15, of which 7 were waited for; matrix products, arithmetic and copies ran while one was open for 7% of the time, Pallas kernels for 9%

profile of v2, /device:TPU:1, one launch (start us, length us, event | category | flops | bytes accessed | tf_op | source)
XLA Modules:
  0.0 203.0 jit_solution(6958772322032421138)
XLA Ops:
  0.6 0.0 copy-start
  0.7 0.6 pad_add_fusion.place
  1.2 3.6 %shard_map.84 = bf16[4,2,32,4096]{3,2,1,0:T(8,128)(2,1)} custom-call(s32[3]{0:T(128)} %pad_add_fusion.place, bf16[16,32,8192]{2,1,0:T(8,128)(2,1)} %bitcast.107), custom_call_target="tpu_custom_call" | custom-call | tf_op jit(solution)/shard_map/pallas_call | solution.py:174
  4.8 1.5 collective-permute-start.1
  6.3 3.6 %shard_map.85 = bf16[4,2,32,4096]{3,2,1,0:T(8,128)(2,1)} custom-call(s32[3]{0:T(128)} %pad_add_fusion.place, bf16[16,32,8192]{2,1,0:T(8,128)(2,1)} %bitcast.108), custom_call_target="tpu_custom_call" | custom-call | tf_op jit(solution)/shard_map/pallas_call | solution.py:174
  9.9 0.1 collective-permute-start
  10.0 0.6 pad_maximum_fusion.2.piece
  10.7 0.0 collective-permute-done.1.received
  10.7 3.0 %shard_map.86 = (bf16[4,32,4096]{2,1,0:T(8,128)(2,1)S(1)}, bf16[4,32,4096]{2,1,0:T(8,128)(2,1)S(1)}) custom-call(s32[3]{0:T(128)} %pad_add_fusion.place, bf16[16,32,8192]{2,1,0:T(8,128)(2,1)} %bitcast.109, bf16[4,2,32,4096]{3,2,1,0:T(8,128)(2,1)} %collective-permute-done.1.received), custom_call_target="tpu_custom_call" | custom-call | tf_op jit(solution)/shard_map/pallas_call | solution.py:220
  13.7 0.0 copy-start.3
  13.7 1.0 copy-done.3
  14.6 3.2 %shard_map.87 = (bf16[64,4096]{1,0:T(8,128)(2,1)S(1)}, bf16[64,4608]{1,0:T(8,128)(2,1)S(1)}, bf16[64,4608]{1,0:T(8,128)(2,1)S(1)}, bf16[64,4608]{1,0:T(8,128)(2,1)S(1)}) custom-call(s32[3]{0:T(128)} %pad_add_fusion.place, bf16[16,32,8192]{2,1,0:T(8,128)(2,1)} %bitcast.110, bf16[4,2,32,4096]{3,2,1,0:T(8,128)(2,1)} %collective-permute-done.received, ...), custom_call_target="tpu_custom_call" | custom-call | tf_op jit(solution)/shard_map/pallas_call | solution.py:220
  17.8 0.0 copy-start.2
  17.9 1.8 collective-permute-start.2
  19.6 3.3 %collective-permute-start.3 = (bf16[64,4608]{1,0:T(8,128)(2,1)S(1)}, bf16[64,4608]{1,0:T(8,128)(2,1)}, u32[]{:S(2)}, u32[]{:S(2)}) collective-permute-start(bf16[64,4608]{1,0:T(8,128)(2,1)S(1)} %get-tuple-element.26), channel_id=1, source_target_pairs={{0,8},{4,12},{8,0},{12,4},{1,9},{5,13},{9,1},{13,5},{2,10},{6,14},... | collective-permute-start | bytes 1769480 | tf_op jit(solution)/shard_map/ppermute | solution.py:133
  22.9 0.7 collective-permute-start.4
  23.7 2.4 %copy.83 = f32[4,8,64,128]{3,2,1,0:T(8,128)} copy(f32[4,8,64,128]{3,1,2,0:T(8,128)} %bitcast.114) | data formatting | bytes 2097152
  26.1 2.9 %collective-permute-start.6 = (bf16[4,32,4096]{2,1,0:T(8,128)(2,1)}, bf16[4,32,4096]{2,1,0:T(8,128)(2,1)}, u32[]{:S(2)}, u32[]{:S(2)}) collective-permute-start(bf16[4,32,4096]{2,1,0:T(8,128)(2,1)} %copy-done.3), channel_id=1, source_target_pairs={{0,2},{2,0},{1,3},{3,1},{4,6},{6,4},{5,7},{7,5},{8,10},{10,8},{9,1... | collective-permute-start | bytes 3145736 | tf_op jit(solution)/shard_map/ppermute | solution.py:262
  29.0 6.2 %collective-permute-done.2.up = bf16[64,4608]{1,0:T(8,128)(2,1)} collective-permute-done((bf16[64,4608]{1,0:T(8,128)(2,1)S(1)}, bf16[64,4608]{1,0:T(8,128)(2,1)}, u32[]{:S(2)}, u32[]{:S(2)}) %collective-permute-start.2) | collective-permute-done | bytes 589856 | tf_op jit(solution)/shard_map/ppermute | solution.py:133
  35.2 13.5 %collective-permute-done.3.far = bf16[64,4608]{1,0:T(8,128)(2,1)} collective-permute-done((bf16[64,4608]{1,0:T(8,128)(2,1)S(1)}, bf16[64,4608]{1,0:T(8,128)(2,1)}, u32[]{:S(2)}, u32[]{:S(2)}) %collective-permute-start.3) | collective-permute-done | bytes 589856 | tf_op jit(solution)/shard_map/ppermute | solution.py:133
  48.7 1.8 shard_map.88
  50.5 3.0 %collective-permute-start.5 = (bf16[32,8192]{1,0:T(8,128)(2,1)S(1)}, bf16[32,8192]{1,0:T(8,128)(2,1)S(1)}, u32[]{:S(2)}, u32[]{:S(2)}) collective-permute-start(bf16[32,8192]{1,0:T(8,128)(2,1)S(1)} %get-tuple-element.29), channel_id=1, source_target_pairs={{0,2},{2,0},{1,3},{3,1},{4,6},{6,4},{5,7},{7,5},{8,10},{10,8},{9,1... | collective-permute-start | bytes 1572872 | tf_op jit(solution)/shard_map/ppermute | solution.py:269
  53.7 2.1 %fusion.4 = (bf16[32,4096]{1,0:T(8,128)(2,1)}, bf16[32,4096]{1,0:T(8,128)(2,1)}, bf16[32,4096]{1,0:T(8,128)(2,1)}) fusion(bf16[4,32,4096]{2,1,0:T(8,128)(2,1)} %collective-permute-done.6, bf16[4,32,4096]{2,1,0:T(8,128)(2,1)S(1)} %get-tuple-element.30), kind=kLoop, calls=%fused_computation.15 | loop fusion | flops 1572864 | bytes 2359296 | tf_op jit(solution)/shard_map/convert_element_type | solution.py:267
  55.7 1.7 collective-permute-start.7
  57.4 2.1 %collective-permute-start.9 = (bf16[32,4096]{1,0:T(8,128)(2,1)}, bf16[32,4096]{1,0:T(8,128)(2,1)}, u32[]{:S(2)}, u32[]{:S(2)}) collective-permute-start(bf16[32,4096]{1,0:T(8,128)(2,1)} %get-tuple-element.37), channel_id=1, source_target_pairs={{0,12},{4,0},{8,4},{12,8},{1,13},{5,1},{9,5},{13,9},{2,14},{6,2},{... | collective-permute-start | bytes 786440 | tf_op jit(solution)/shard_map/ppermute | solution.py:133
  59.5 4.8 %collective-permute-done.5 = bf16[32,8192]{1,0:T(8,128)(2,1)S(1)} collective-permute-done((bf16[32,8192]{1,0:T(8,128)(2,1)S(1)}, bf16[32,8192]{1,0:T(8,128)(2,1)S(1)}, u32[]{:S(2)}, u32[]{:S(2)}) %collective-permute-start.5) | collective-permute-done | bytes 524320 | tf_op jit(solution)/shard_map/ppermute | solution.py:269
  64.5 0.1 maximum_select_fusion
  64.5 0.4 select_n.57
  64.9 0.0 copy-start.7
  65.0 1.8 fusion.17
  66.8 0.1 copy.81
  66.9 0.7 copy_bitcast_fusion.2
  67.6 3.1 %collective-permute-done.9 = bf16[32,4096]{1,0:T(8,128)(2,1)} collective-permute-done((bf16[32,4096]{1,0:T(8,128)(2,1)}, bf16[32,4096]{1,0:T(8,128)(2,1)}, u32[]{:S(2)}, u32[]{:S(2)}) %collective-permute-start.9) | collective-permute-done | bytes 262176 | tf_op jit(solution)/shard_map/ppermute | solution.py:133
  70.7 1.3 bitcast_add_fusion
  72.0 0.0 copy-start.6
  72.0 0.1 copy.82
  72.1 0.0 copy-start.5
  72.2 0.2 fusion.1
  72.3 0.9 copy.69
  73.2 4.1 %all-to-all-start = ((bf16[8,8,32,128]{3,1,2,0:T(8,128)(2,1)}), bf16[8,8,32,128]{3,1,2,0:T(8,128)(2,1)}, u32[]{:S(2)}, u32[]{:S(2)}) async-start(bf16[8,8,32,128]{3,1,2,0:T(8,128)(2,1)} %copy.69), calls=%async_computation | async-start | bytes 1048576 | tf_op jit(solution)/shard_map/all_to_all | solution.py:299
  77.4 1.0 copy_bitcast_fusion
  78.4 1.0 pad_maximum_fusion
  79.3 0.8 copy.70
  80.2 1.8 collective-permute-start.10
  82.0 0.2 copy.85
  82.2 0.2 copy.86
  82.4 0.3 subtract_convert_fusion
  82.7 2.1 %all-to-all-done = bf16[8,8,32,128]{3,1,2,0:T(8,128)(2,1)} async-done(((bf16[8,8,32,128]{3,1,2,0:T(8,128)(2,1)}), bf16[8,8,32,128]{3,1,2,0:T(8,128)(2,1)}, u32[]{:S(2)}, u32[]{:S(2)}) %all-to-all-start) | async-done | bytes 524320 | tf_op jit(solution)/shard_map/all_to_all | solution.py:299
  84.8 1.1 convert_reduce_fusion
  86.0 1.2 convolution_convert_fusion
  87.2 0.7 broadcast_in_dim.8
  87.9 4.9 %all-to-all-start.1 = ((bf16[8,32,256]{2,1,0:T(8,128)(2,1)}), bf16[8,32,256]{2,1,0:T(8,128)(2,1)S(1)}, u32[]{:S(2)}, u32[]{:S(2)}) async-start(bf16[8,32,256]{2,1,0:T(8,128)(2,1)} %broadcast_in_dim.8), calls=%async_computation.1 | async-start | bytes 262144 | tf_op jit(solution)/shard_map/all_to_all | solution.py:139
  92.9 5.2 %all-to-all-done.1 = bf16[8,32,256]{2,1,0:T(8,128)(2,1)S(1)} async-done(((bf16[8,32,256]{2,1,0:T(8,128)(2,1)}), bf16[8,32,256]{2,1,0:T(8,128)(2,1)S(1)}, u32[]{:S(2)}, u32[]{:S(2)}) %all-to-all-start.1) | async-done | bytes 131104 | tf_op jit(solution)/shard_map/all_to_all | solution.py:139
  98.2 13.5 %all_to_all.20 = bf16[8,4,32,128]{3,2,1,0:T(8,128)(2,1)S(1)} all-to-all(bf16[8,4,32,128]{3,2,1,0:T(8,128)(2,1)S(1)} %pad_maximum_fusion.1), channel_id=1, replica_groups=mesh['x'=4,'ylo'=2,'z'=4,'yhi'=2,'core'=2] {'z','yhi'}, dimensions={0} | all-to-all | bytes 524288 | tf_op jit(solution)/shard_map/all_to_all | solution.py:307
  111.8 4.0 %collective-permute-start.11 = (bf16[4,256,128]{2,1,0:T(8,128)(2,1)S(1)}, bf16[4,256,128]{2,1,0:T(8,128)(2,1)S(1)}, u32[]{:S(2)}, u32[]{:S(2)}) collective-permute-start(bf16[4,256,128]{2,1,0:T(8,128)(2,1)S(1)} %bitcast.105), channel_id=1, source_target_pairs={{0,1},{1,0},{2,3},{3,2},{4,5},{5,4},{6,7},{7,6},{8,9},{9,8},{10,11... | collective-permute-start | bytes 786440 | tf_op jit(solution)/shard_map/ppermute | solution.py:129
  115.8 1.2 collective-permute-done.11.other_ref
  116.9 3.7 %shard_map.89 = bf16[64,288,128]{2,1,0:T(8,128)(2,1)S(1)} custom-call(bf16[4,256,128]{2,1,0:T(8,128)(2,1)S(1)} %bitcast.106, bf16[4,256,128]{2,1,0:T(8,128)(2,1)S(1)} %collective-permute-done.11.other_ref), custom_call_target="tpu_custom_call" | custom-call | tf_op jit(solution)/shard_map/pallas_call | solution.py:62
  120.6 0.0 copy-start.4
  120.6 62.3 %all_to_all.21 = bf16[64,288,128]{2,1,0:T(8,128)(2,1)} all-to-all(bf16[64,288,128]{2,1,0:T(8,128)(2,1)S(1)} %shard_map.89), channel_id=1, replica_groups=mesh['x'=4,'ylo'=2,'z'=4,'yhi'=2,'core'=2] {'x','ylo','z','yhi'}, dimensions={0} | all-to-all | bytes 9437184 | tf_op jit(solution)/shard_map/all_to_all | solution.py:310
  182.9 1.5 collective-permute-start.12
  184.4 1.1 maximum_add_fusion.1.merged
  185.6 9.4 %shard_map.90 = (bf16[8,2,32,8192]{3,2,1,0:T(8,128)(2,1)}, f32[32,8192]{1,0:T(8,128)}, f32[32,8192]{1,0:T(8,128)}, f32[32,8192]{1,0:T(8,128)}) custom-call(s32[3]{0:T(128)} %pad_add_fusion.place, bf16[8,8,288,128]{3,2,1,0:T(8,128)(2,1)} %bitcast.28.moved, f32[32,8192]{1,0:T(8,128)} %maximum_add_fusion.1.merged, f32[32,8192]{1,0:T(8,128)} %momentum.1, ...), custom_call_target="tpu_custom_call" | custom-call | tf_op jit(solution)/shard_map/pallas_call | solution.py:98
  195.0 0.0 copy-start.1
  195.0 7.9 %shard_map.91 = bf16[8,2,32,8192]{3,2,1,0:T(8,128)(2,1)} custom-call(s32[3]{0:T(128)} %pad_add_fusion.place, bf16[8,8,288,128]{3,2,1,0:T(8,128)(2,1)} %bitcast.27.moved, bf16[8,2,32,8192]{3,2,1,0:T(8,128)(2,1)} %get-tuple-element.32._), custom_call_target="tpu_custom_call", output_to_operand_aliasing={{}: (2, {})} | custom-call | tf_op jit(solution)/shard_map/pallas_call | solution.py:114
  (46 shorter events, 0.4 us)
Async XLA Ops:
  0.6 9.3 %copy-start = (f32[512,256]{1,0:T(8,128)S(1)}, f32[512,256]{1,0:T(8,128)}, u32[]{:S(2)}) copy-start(f32[512,256]{1,0:T(8,128)} %param.9) | copy-start | bytes 1572868
  4.8 5.9 %collective-permute-start.1 = (bf16[4,2,32,4096]{3,2,1,0:T(8,128)(2,1)}, bf16[4,2,32,4096]{3,2,1,0:T(8,128)(2,1)}, u32[]{:S(2)}, u32[]{:S(2)}) collective-permute-start(bf16[4,2,32,4096]{3,2,1,0:T(8,128)(2,1)} %shard_map.84), channel_id=1, source_target_pairs={{0,1},{1,0},{2,3},{3,2},{4,5},{5,4},{6,7},{7,6},{8,9},{9,8},{10,11... | collective-permute-start | bytes 6291464 | tf_op jit(solution)/shard_map/ppermute | solution.py:129
  9.9 4.8 %collective-permute-start = (bf16[4,2,32,4096]{3,2,1,0:T(8,128)(2,1)}, bf16[4,2,32,4096]{3,2,1,0:T(8,128)(2,1)}, u32[]{:S(2)}, u32[]{:S(2)}) collective-permute-start(bf16[4,2,32,4096]{3,2,1,0:T(8,128)(2,1)} %shard_map.85), channel_id=1, source_target_pairs={{0,1},{1,0},{2,3},{3,2},{4,5},{5,4},{6,7},{7,6},{8,9},{9,8},{10,11... | collective-permute-start | bytes 6291464 | tf_op jit(solution)/shard_map/ppermute | solution.py:129
  13.7 1.0 copy-start.3
  17.8 30.8 %copy-start.2 = (bf16[64,4096]{1,0:T(8,128)(2,1)}, bf16[64,4096]{1,0:T(8,128)(2,1)S(1)}, u32[]{:S(2)}) copy-start(bf16[64,4096]{1,0:T(8,128)(2,1)S(1)} %get-tuple-element.24.left) | copy-start | bytes 1572868
  17.9 17.3 %collective-permute-start.2 = (bf16[64,4608]{1,0:T(8,128)(2,1)S(1)}, bf16[64,4608]{1,0:T(8,128)(2,1)}, u32[]{:S(2)}, u32[]{:S(2)}) collective-permute-start(bf16[64,4608]{1,0:T(8,128)(2,1)S(1)} %get-tuple-element.25), channel_id=1, source_target_pairs={{0,4},{4,8},{8,12},{12,0},{1,5},{5,9},{9,13},{13,1},{2,6},{6,10},{... | collective-permute-start | bytes 1769480 | tf_op jit(solution)/shard_map/ppermute | solution.py:133
  19.6 29.0 %collective-permute-start.3 = (bf16[64,4608]{1,0:T(8,128)(2,1)S(1)}, bf16[64,4608]{1,0:T(8,128)(2,1)}, u32[]{:S(2)}, u32[]{:S(2)}) collective-permute-start(bf16[64,4608]{1,0:T(8,128)(2,1)S(1)} %get-tuple-element.26), channel_id=1, source_target_pairs={{0,8},{4,12},{8,0},{12,4},{1,9},{5,13},{9,1},{13,5},{2,10},{6,14},... | collective-permute-start | bytes 1769480 | tf_op jit(solution)/shard_map/ppermute | solution.py:133
  22.9 25.7 %collective-permute-start.4 = (bf16[64,4608]{1,0:T(8,128)(2,1)S(1)}, bf16[64,4608]{1,0:T(8,128)(2,1)}, u32[]{:S(2)}, u32[]{:S(2)}) collective-permute-start(bf16[64,4608]{1,0:T(8,128)(2,1)S(1)} %get-tuple-element.27), channel_id=1, source_target_pairs={{0,12},{4,0},{8,4},{12,8},{1,13},{5,1},{9,5},{13,9},{2,14},{6,2},{... | collective-permute-start | bytes 1769480 | tf_op jit(solution)/shard_map/ppermute | solution.py:133
  26.1 27.6 %collective-permute-start.6 = (bf16[4,32,4096]{2,1,0:T(8,128)(2,1)}, bf16[4,32,4096]{2,1,0:T(8,128)(2,1)}, u32[]{:S(2)}, u32[]{:S(2)}) collective-permute-start(bf16[4,32,4096]{2,1,0:T(8,128)(2,1)} %copy-done.3), channel_id=1, source_target_pairs={{0,2},{2,0},{1,3},{3,1},{4,6},{6,4},{5,7},{7,5},{8,10},{10,8},{9,1... | collective-permute-start | bytes 3145736 | tf_op jit(solution)/shard_map/ppermute | solution.py:262
  50.5 13.8 %collective-permute-start.5 = (bf16[32,8192]{1,0:T(8,128)(2,1)S(1)}, bf16[32,8192]{1,0:T(8,128)(2,1)S(1)}, u32[]{:S(2)}, u32[]{:S(2)}) collective-permute-start(bf16[32,8192]{1,0:T(8,128)(2,1)S(1)} %get-tuple-element.29), channel_id=1, source_target_pairs={{0,2},{2,0},{1,3},{3,1},{4,6},{6,4},{5,7},{7,5},{8,10},{10,8},{9,1... | collective-permute-start | bytes 1572872 | tf_op jit(solution)/shard_map/ppermute | solution.py:269
  55.7 11.8 %collective-permute-start.7 = (bf16[32,4096]{1,0:T(8,128)(2,1)}, bf16[32,4096]{1,0:T(8,128)(2,1)}, u32[]{:S(2)}, u32[]{:S(2)}) collective-permute-start(bf16[32,4096]{1,0:T(8,128)(2,1)} %get-tuple-element.36), channel_id=1, source_target_pairs={{0,8},{4,12},{8,0},{12,4},{1,9},{5,13},{9,1},{13,5},{2,10},{6,14},... | collective-permute-start | bytes 786440 | tf_op jit(solution)/shard_map/ppermute | solution.py:133
  57.4 13.3 %collective-permute-start.9 = (bf16[32,4096]{1,0:T(8,128)(2,1)}, bf16[32,4096]{1,0:T(8,128)(2,1)}, u32[]{:S(2)}, u32[]{:S(2)}) collective-permute-start(bf16[32,4096]{1,0:T(8,128)(2,1)} %get-tuple-element.37), channel_id=1, source_target_pairs={{0,12},{4,0},{8,4},{12,8},{1,13},{5,1},{9,5},{13,9},{2,14},{6,2},{... | collective-permute-start | bytes 786440 | tf_op jit(solution)/shard_map/ppermute | solution.py:133
  59.5 11.2 %collective-permute-start.8 = (bf16[32,4096]{1,0:T(8,128)(2,1)}, bf16[32,4096]{1,0:T(8,128)(2,1)}, u32[]{:S(2)}, u32[]{:S(2)}) collective-permute-start(bf16[32,4096]{1,0:T(8,128)(2,1)} %get-tuple-element.38), channel_id=1, source_target_pairs={{0,4},{4,8},{8,12},{12,0},{1,5},{5,9},{9,13},{13,1},{2,6},{6,10},{... | collective-permute-start | bytes 786440 | tf_op jit(solution)/shard_map/ppermute | solution.py:133
  64.9 7.2 %copy-start.7 = (f32[4,8,64,128]{3,2,1,0:T(8,128)S(1)}, f32[4,8,64,128]{3,2,1,0:T(8,128)}, u32[]{:S(2)}) copy-start(f32[4,8,64,128]{3,2,1,0:T(8,128)} %copy.83) | copy-start | bytes 3145732
  72.0 10.0 %copy-start.6 = (f32[32,8192]{1,0:T(8,128)S(1)}, f32[32,8192]{1,0:T(8,128)}, u32[]{:S(2)}) copy-start(f32[32,8192]{1,0:T(8,128)} %params.1) | copy-start | bytes 3145732
  72.1 10.0 %copy-start.5 = (f32[32,8192]{1,0:T(8,128)S(1)}, f32[32,8192]{1,0:T(8,128)}, u32[]{:S(2)}) copy-start(f32[32,8192]{1,0:T(8,128)} %momentum.1) | copy-start | bytes 3145732
  73.2 11.6 %all-to-all-start = ((bf16[8,8,32,128]{3,1,2,0:T(8,128)(2,1)}), bf16[8,8,32,128]{3,1,2,0:T(8,128)(2,1)}, u32[]{:S(2)}, u32[]{:S(2)}) async-start(bf16[8,8,32,128]{3,1,2,0:T(8,128)(2,1)} %copy.69), calls=%async_computation | async-start | bytes 1048576 | tf_op jit(solution)/shard_map/all_to_all | solution.py:299
  80.2 5.8 %collective-permute-start.10 = (bf16[1024,256]{1,0:T(8,128)(2,1)}, bf16[1024,256]{1,0:T(8,128)(2,1)}, u32[]{:S(2)}, u32[]{:S(2)}) collective-permute-start(bf16[1024,256]{1,0:T(8,128)(2,1)} %bitcast.20), channel_id=1, source_target_pairs={{0,1},{1,0},{2,3},{3,2},{4,5},{5,4},{6,7},{7,6},{8,9},{9,8},{10,11... | collective-permute-start | bytes 1572872 | tf_op jit(solution)/shard_map/ppermute | solution.py:129
  87.9 10.2 %all-to-all-start.1 = ((bf16[8,32,256]{2,1,0:T(8,128)(2,1)}), bf16[8,32,256]{2,1,0:T(8,128)(2,1)S(1)}, u32[]{:S(2)}, u32[]{:S(2)}) async-start(bf16[8,32,256]{2,1,0:T(8,128)(2,1)} %broadcast_in_dim.8), calls=%async_computation.1 | async-start | bytes 262144 | tf_op jit(solution)/shard_map/all_to_all | solution.py:139
  111.8 5.2 %collective-permute-start.11 = (bf16[4,256,128]{2,1,0:T(8,128)(2,1)S(1)}, bf16[4,256,128]{2,1,0:T(8,128)(2,1)S(1)}, u32[]{:S(2)}, u32[]{:S(2)}) collective-permute-start(bf16[4,256,128]{2,1,0:T(8,128)(2,1)S(1)} %bitcast.105), channel_id=1, source_target_pairs={{0,1},{1,0},{2,3},{3,2},{4,5},{5,4},{6,7},{7,6},{8,9},{9,8},{10,11... | collective-permute-start | bytes 786440 | tf_op jit(solution)/shard_map/ppermute | solution.py:129
  120.6 63.8 %copy-start.4 = (f32[1,32,8192]{2,1,0:T(8,128)S(1)}, f32[1,32,8192]{2,1,0:T(8,128)}, u32[]{:S(2)}) copy-start(f32[1,32,8192]{2,1,0:T(8,128)} %param.6) | copy-start | bytes 3145732
  182.9 12.1 %collective-permute-start.12 = (bf16[64,288,128]{2,1,0:T(8,128)(2,1)}, bf16[64,288,128]{2,1,0:T(8,128)(2,1)}, u32[]{:S(2)}, u32[]{:S(2)}) collective-permute-start(bf16[64,288,128]{2,1,0:T(8,128)(2,1)} %all_to_all.21), channel_id=1, source_target_pairs={{0,1},{1,0},{2,3},{3,2},{4,5},{5,4},{6,7},{7,6},{8,9},{9,8},{10,11... | collective-permute-start | bytes 14155784 | tf_op jit(solution)/shard_map/ppermute | solution.py:129
  195.0 7.9 %copy-start.1 = (f32[512,256]{1,0:T(8,128)S(1)}, f32[512,256]{1,0:T(8,128)}, u32[]{:S(2)}) copy-start(f32[512,256]{1,0:T(8,128)} %param.9) | copy-start | bytes 1572868

commit v3 on v2

--- a/solution.py
+++ b/solution.py
@@ -68,75 +68,198 @@
     )(own, other)
 
 
+def block_cols(g):
+    return pl.ds(g * 1024, 1024)
+
+
 def put_weights(moved, full):
     for n in range(8):
-        full[:, 0, :, n * 128 : (n + 1) * 128] = moved[n, 0, :256].reshape(8, 32, 128)
-
-
-def own_kernel(place, moved, merged, momentum, params, full, new_params, new_momentum, new_error):
-    put_weights(moved, full)
-    for n in range(8):
-        cols = slice(n * 128, (n + 1) * 128)
-        delta = moved[n, 0, 256:].astype(F32)
-        new_error[:, cols] = merged[:, cols] - delta
-        step = 0.9 * momentum[:, cols] + delta
-        new_momentum[:, cols] = step
-        new_params[:, cols] = params[:, cols] - 0.7 * (delta + 0.9 * step)
-
-
-def other_kernel(place, moved, _, full):
-    put_weights(moved, full)
-
-
-MOVED_SPEC = pl.BlockSpec((8, 1, 288, 128), lambda g, _: (0, g, 0, 0))
+        full[:, :, n * 128 : (n + 1) * 128] = moved[n, :256].reshape(8, 32, 128)
+
+
+def own_kernel(place, *refs):
+    ins, outs, rest = refs[:4], refs[4:8], refs[8:]
+    held, made, in_sems, out_sems = rest[:4], rest[4:8], rest[8], rest[9]
+    loads, stores = [], []
+    for g in range(8):
+        views = [ins[0].at[:, g]] + [ref.at[:, block_cols(g)] for ref in ins[1:]]
+        loads.append([
+            pltpu.make_async_copy(view, to.at[g], in_sems.at[n, g])
+            for n, (view, to) in enumerate(zip(views, held))
+        ])
+        views = [outs[0].at[:, place[0], :, block_cols(g)]]
+        views += [ref.at[:, block_cols(g)] for ref in outs[1:]]
+        stores.append([
+            pltpu.make_async_copy(of.at[g], view, out_sems.at[n, g])
+            for n, (of, view) in enumerate(zip(made, views))
+        ])
+    for copies in loads:
+        for copy in copies:
+            copy.start()
+    moved, merged, momentum, params = held
+    full, new_params, new_momentum, new_error = made
+    for g in range(8):
+        for copy in loads[g]:
+            copy.wait()
+        put_weights(moved.at[g], full.at[g])
+        for n in range(8):
+            at = (g, slice(None), slice(n * 128, (n + 1) * 128))
+            delta = moved[g, n, 256:].astype(F32)
+            new_error[at] = merged[at] - delta
+            step = 0.9 * momentum[at] + delta
+            new_momentum[at] = step
+            new_params[at] = params[at] - 0.7 * (delta + 0.9 * step)
+        for copy in stores[g]:
+            copy.start()
+    for copies in stores:
+        for copy in copies:
+            copy.wait()
+
+
 FULL_SHAPE = jax.ShapeDtypeStruct((8, 2, 32, 8192), BF16)
+SMEM = pl.BlockSpec(memory_space=pltpu.SMEM)
+ANYWHERE = pl.BlockSpec(memory_space=pl.ANY)
 
 
 def own_rows(place, moved, merged, momentum, params):
-    rows = pl.BlockSpec((32, 1024), lambda g, _: (0, g))
     row_shape = jax.ShapeDtypeStruct((32, 8192), F32)
+    rows = pltpu.VMEM((8, 32, 1024), F32)
     return pl.pallas_call(
         own_kernel,
-        grid_spec=pltpu.PrefetchScalarGridSpec(
-            num_scalar_prefetch=1,
-            grid=(8,),
-            in_specs=[MOVED_SPEC, rows, rows, rows],
-            out_specs=[
-                pl.BlockSpec((8, 1, 32, 1024), lambda g, at: (0, at[0], 0, g)), rows, rows, rows,
-            ],
-        ),
+        in_specs=[SMEM] + [ANYWHERE] * 4,
+        out_specs=[ANYWHERE] * 4,
         out_shape=[FULL_SHAPE, row_shape, row_shape, row_shape],
+        scratch_shapes=[
+            pltpu.VMEM((8, 8, 288, 128), BF16), rows, rows, rows,
+            pltpu.VMEM((8, 8, 32, 1024), BF16), rows, rows, rows,
+            pltpu.SemaphoreType.DMA((4, 8)),
+            pltpu.SemaphoreType.DMA((4, 8)),
+        ],
         compiler_params=pltpu.CompilerParams(vmem_limit_bytes=VMEM),
     )(place, moved.reshape(8, 8, 288, 128), merged, momentum, params)
 
 
+def other_kernel(place, moved, _, full, held, made, in_sems, out_sems):
+    side = 1 - place[0]
+    loads = [
+        pltpu.make_async_copy(moved.at[:, g, pl.ds(0, 256)], held.at[g], in_sems.at[g])
+        for g in range(8)
+    ]
+    stores = [
+        pltpu.make_async_copy(made.at[g], full.at[:, side, :, block_cols(g)], out_sems.at[g])
+        for g in range(8)
+    ]
+    for copy in loads:
+        copy.start()
+    for g in range(8):
+        loads[g].wait()
+        put_weights(held.at[g], made.at[g])
+        stores[g].start()
+    for copy in stores:
+        copy.wait()
+
+
 def other_rows(place, moved, full):
     return pl.pallas_call(
         other_kernel,
-        grid_spec=pltpu.PrefetchScalarGridSpec(
-            num_scalar_prefetch=1,
-            grid=(8,),
-            in_specs=[MOVED_SPEC, pl.BlockSpec(memory_space=pl.ANY)],
-            out_specs=pl.BlockSpec((8, 1, 32, 1024), lambda g, at: (0, 1 - at[0], 0, g)),
-        ),
+        in_specs=[SMEM, ANYWHERE, ANYWHERE],
+        out_specs=ANYWHERE,
         out_shape=FULL_SHAPE,
         input_output_aliases={2: 0},
+        scratch_shapes=[
+            pltpu.VMEM((8, 8, 256, 128), BF16),
+            pltpu.VMEM((8, 8, 32, 1024), BF16),
+            pltpu.SemaphoreType.DMA((8,)),
+            pltpu.SemaphoreType.DMA((8,)),
+        ],
         compiler_params=pltpu.CompilerParams(vmem_limit_bytes=VMEM),
     )(place, moved.reshape(8, 8, 288, 128), full)
 
 
+def middle_kernel(place, blocks, q_own, q_other, mean, out):
+    total = blocks[0].astype(F32)
+    for n in range(1, 8):
+        total = total + blocks[n].astype(F32)
+    low = (total * 0.125).astype(BF16)
+    mean[...] = low
+    low = jnp.concatenate([low[n] for n in range(8)], 1)
+    for flag, q_ref in ((1, q_own), (0, q_other)):
+
+        @pl.when(place[3] == flag)
+        def _():
+            value = dot_nn(low, q_ref[...]).astype(BF16)
+            for n in range(8):
+                out[n] = value
+
+
+def middle(place, blocks, q_own, q_other):
+    vmem = pl.BlockSpec(memory_space=pltpu.VMEM)
+    return pl.pallas_call(
+        middle_kernel,
+        in_specs=[SMEM] + [vmem] * 3,
+        out_specs=[vmem] * 2,
+        out_shape=[
+            pltpu.VMEM((8, 32, 128), BF16),
+            jax.ShapeDtypeStruct((8, 32, 256), BF16),
+        ],
+    )(place, blocks, q_own, q_other)
+
+
+def gather_kernel(terms, mean, before, out):
+    total = terms[0].astype(F32)
+    for n in range(1, 8):
+        total = total + terms[n].astype(F32)
+    total = total.astype(BF16)
+    for n in range(8):
+        out[n, 0] = total[:, :128]
+        out[n, 1] = total[:, 128:]
+        out[n, 2] = mean[n]
+        out[n, 3] = before[n]
+
+
+def gathered(terms, mean, before):
+    vmem = pl.BlockSpec(memory_space=pltpu.VMEM)
+    return pl.pallas_call(
+        gather_kernel,
+        in_specs=[vmem] * 3,
+        out_specs=vmem,
+        out_shape=jax.ShapeDtypeStruct((8, 4, 32, 128), BF16),
+    )(terms, mean, before)
+
+
+def merge_kernel(left, back, right, far, up, down, error, merged, blocks):
+    for n in range(64):
+        at = slice((n % 32) * 128, (n % 32 + 1) * 128)
+        if n < 32:
+            value = left[:, at] + back[:, at].astype(F32)
+        else:
+            value = right[:, at]
+            for ref in (far, up, down):
+                value = value + ref[:, at].astype(F32)
+        value = value + error[:, n * 128 : (n + 1) * 128]
+        merged[:, n * 128 : (n + 1) * 128] = value
+        blocks[n % 8, n // 8] = value.astype(BF16)
+
+
+def merge(left, back, right, moved, error):
+    vmem = pl.BlockSpec(memory_space=pltpu.VMEM)
+    return pl.pallas_call(
+        merge_kernel,
+        in_specs=[vmem] * 7,
+        out_specs=[vmem] * 2,
+        out_shape=[
+            jax.ShapeDtypeStruct((32, 8192), F32),
+            jax.ShapeDtypeStruct((8, 8, 32, 128), BF16),
+        ],
+    )(left, back, right, *moved, error)
+
+
 def swap_cores(value):
     return lax.ppermute(value, "core", SWAP)
 
 
 def along_z(value, step):
     return lax.ppermute(value, "z", [(at, (at + step) % 4) for at in range(4)])
-
-
-def copies(value, axes):
-    count = lax.axis_size(axes)
-    value = jnp.broadcast_to(value[None], (count,) + value.shape)
-    return lax.all_to_all(value, axes, 0, 0, tiled=True)
 
 
 def ring_order(ring, z):
@@ -253,41 +376,39 @@
     )(left, up, far, down, piece)
 
 
-def summed_rows(partials, piece, place, z, yhi):
+def summed_rows(partials, error, piece, place, z, yhi):
     parts = partials.reshape(16, 32, 8192)
-    right_out, parts_later = lax.optimization_barrier((theirs(place, parts, 1), parts))
-    right_in, left_in = swap_cores(right_out), swap_cores(theirs(place, parts_later, 0))
-    right, across = pair_call(right_kernel, [(4, 32, WIDE)] * 2, place, parts, right_in)
-    left_in, right = lax.optimization_barrier((left_in, right))
-    across = lax.ppermute(across, "yhi", SWAP)
+    left_out, parts_later = lax.optimization_barrier((theirs(place, parts, 0), parts))
+    left_in, right_in = swap_cores(left_out), swap_cores(theirs(place, parts_later, 1))
     shapes = [(64, WIDE)] + [(64, WIDE + 512)] * 3
     left, up, far, down = pair_call(left_kernel, shapes, place, parts, left_in, piece)
+    right_in, left = lax.optimization_barrier((right_in, left))
+    right, across = pair_call(right_kernel, [(4, 32, WIDE)] * 2, place, parts, right_in)
+    across = lax.ppermute(across, "yhi", SWAP)
     far, up, down = along_z(far, 2), along_z(up, 1), along_z(down, 3)
     sums = [right[k].astype(F32) + across[k].astype(F32) for k in range(4)]
     moved = [along_z(sums[k].astype(BF16), k) for k in (2, 1, 3)]
     left, sent = turn(left, up, far, down, piece)
     back = lax.ppermute(sent, "yhi", SWAP)
-    right = sums[0] + sum(moved_in.astype(F32) for moved_in in moved)
-    left = left + back[:, :WIDE].astype(F32)
+    merged, blocks = merge(left, back, sums[0], moved, error)
     ours, others = (
         ring_order([value[:, WIDE + k * 1024 : WIDE + (k + 1) * 1024] for k in range(4)], z)
         for value in (sent, back)
     )
     pieces = jnp.where(yhi == 0, jnp.stack([ours, others], 1), jnp.stack([others, ours], 1))
-    return jnp.concatenate([left, right], 1), pieces.reshape(8, 32, 4, 256)
+    return merged, blocks, pieces.reshape(8, 32, 4, 256)
 
 
 def on_device(partials, error_buf, momentum, params, start_q):
     core, z, yhi = (lax.axis_index(name) for name in ("core", "z", "yhi"))
     isl = lax.axis_index(ISLAND)
-    place = jnp.stack([core, z, yhi]).astype(jnp.int32)
+    place = jnp.stack([core, z, yhi, isl // 4 == core]).astype(jnp.int32)
 
     own_q = lax.dynamic_slice(start_q, ((isl % 4) * 128, 0), (128, 256)).astype(BF16)
     piece = jnp.concatenate([own_q[:64], own_q[64:]], 1)
-    merged, pieces = summed_rows(partials[0, 0], piece, place, z, yhi)
-    merged = merged + error_buf[0]
+    merged, blocks, pieces = summed_rows(partials[0, 0], error_buf[0], piece, place, z, yhi)
     q_own = jnp.stack([pieces[:, :, n] for n in (0, 2, 1, 3)], 1).reshape(1024, 256)
-    q_cols = jnp.where(isl // 4 == core, q_own, swap_cores(q_own))
+    q_other = swap_cores(q_own)
 
     def columns(value):
         return lax.dynamic_index_in_dim(value.reshape(32, 8, 8, 128), isl, 2, False)
@@ -295,16 +416,12 @@
     before = (columns(params) - (0.7 * 0.9 * 0.9) * columns(momentum)).astype(BF16)
     before = before.transpose(1, 0, 2)
 
-    blocks = merged.astype(BF16).reshape(32, 8, 8, 128).transpose(2, 1, 0, 3)
     blocks = lax.all_to_all(blocks, ISLAND, 0, 0, tiled=True)
-    mean = (jnp.sum(blocks.astype(F32), 0) * 0.125).astype(BF16)
-    local_proj = dot_nn(mean.transpose(1, 0, 2).reshape(32, 1024), q_cols).astype(BF16)
-    proj = jnp.sum(copies(local_proj, ISLAND).astype(F32), 0).astype(BF16)
-
-    proj = proj.reshape(32, 2, 128).transpose(1, 0, 2)
-    proj = jnp.broadcast_to(proj[None], (8, 2, 32, 128))
-    own = jnp.concatenate([proj, mean[:, None], before[:, None]], 1)
-    own = lax.all_to_all(own, ZY, 0, 0, tiled=True).transpose(1, 0, 2, 3).reshape(4, 256, 128)
+    mean, terms = middle(place, blocks, q_own, q_other)
+    terms = lax.all_to_all(terms, ISLAND, 0, 0, tiled=True)
+
+    own = lax.all_to_all(gathered(terms, mean, before), ZY, 0, 0, tiled=True)
+    own = own.transpose(1, 0, 2, 3).reshape(4, 256, 128)
     other = swap_cores(own)
 
     moved_own = lax.all_to_all(factors(own, other), CHIPS, 0, 0, tiled=True)

time: 204 us -> 198 us (0.971)
  local copies, waits for them, and re-layouts: 10.5 us -> 4.55 us
  other arithmetic: 8.47 us -> 4.34 us
  Pallas kernels: 36.2 us -> 38.9 us
  blocking collectives: 75.8 us -> 78.3 us
    all_to_all x1, waiting for transfers between devices: 2.14 us -> 6.38 us  [on_device(): blocks = lax.all_to_all(blocks, ISLAND, 0, 0, tiled=True)]
    unnamed x37 -> x44, local copies, waits for them, and re-layouts: 5.74 us -> 2.71 us
    add x3 -> x0, other arithmetic: 2.54 us -> none  [the longest x1 1.34 us: summed_rows(): right = sums[0] + sum((moved_in.astype(F32) for moved_in in moved))]
    all_to_all x1, blocking collectives: 13.5 us -> 16 us  [on_device(): own = lax.all_to_all(gathered(terms, mean, before), ZY, 0, 0, tiled=True)]
    ppermute x6, waiting for transfers between devices: 22.8 us -> 20.8 us  [along_z(): return lax.ppermute(value, 'z', [(at, (at + step) % 4) for at in range(4)])]
    pallas_call x2 -> x5, Pallas kernels: 17.3 us -> 18.9 us  [the longest x1 7.45 us: own_rows(): pl.pallas_call(own_kernel, in_specs=[SMEM] + [ANYWHERE] * 4, out_specs=[A...]
  transfers between devices with their start and end apart: 15 -> 15, of which waited for: 7 -> 8; matrix products, arithmetic and copies ran while one was open for 7% -> 3% of each run, Pallas kernels for 9% -> 12%
where the time goes in v3:
time: 198 us
  blocking collectives  78.3 us (40%)
  Pallas kernels  38.9 us (20%)
  waiting for transfers between devices  37.6 us (19%)
  starting transfers between devices  32.7 us (17%)
  local copies, waits for them, and re-layouts  4.55 us (2%)
  other arithmetic  4.34 us (2%)
    all_to_all x1, blocking collectives, on_device(): moved_own = lax.all_to_all(factors(own, other), CHIPS, 0, 0, tiled=True)  62.3 us
    ppermute x6, waiting for transfers between devices, along_z(): return lax.ppermute(value, 'z', [(at, (at + step) % 4) for at in range(4)])  20.8 us
    all_to_all x1, blocking collectives, on_device(): own = lax.all_to_all(gathered(terms, mean, before), ZY, 0, 0, tiled=True)  16 us
    ppermute x6, starting transfers between devices, along_z(): return lax.ppermute(value, 'z', [(at, (at + step) % 4) for at in range(4)])  9.7 us
    ppermute x5, starting transfers between devices, swap_cores(): return lax.ppermute(value, 'core', SWAP)  9.46 us
    pallas_call x1, Pallas kernels, own_rows(): pl.pallas_call(own_kernel, in_specs=[SMEM] + [ANYWHERE] * 4, out_specs=[A...  7.45 us
    pallas_call x2, Pallas kernels, pair_call(): pl.pallas_call(kernel, in_specs=[pl.BlockSpec(memory_space=pltpu.SMEM), a...  7.34 us
    pallas_call x2, Pallas kernels, theirs(): pl.pallas_call(functools.partial(theirs_kernel, half), in_specs=[pl.Block...  7.17 us
  transfers between devices with their start and end apart: 15, of which 8 were waited for; matrix products, arithmetic and copies ran while one was open for 3% of the time, Pallas kernels for 12%

profile of v3, /device:TPU:1, one launch (start us, length us, event | category | flops | bytes accessed | tf_op | source)
XLA Modules:
  0.0 197.7 jit_solution(15594819454916261494)
XLA Ops:
  0.6 0.0 copy-start
  0.7 0.6 pad_add_fusion.place
  1.3 3.6 %shard_map.84 = bf16[4,2,32,4096]{3,2,1,0:T(8,128)(2,1)} custom-call(s32[4]{0:T(128)} %pad_add_fusion.place, bf16[16,32,8192]{2,1,0:T(8,128)(2,1)} %bitcast.83), custom_call_target="tpu_custom_call" | custom-call | tf_op jit(solution)/shard_map/pallas_call | solution.py:297
  4.8 1.5 collective-permute-start.1
  6.3 3.6 %shard_map.85 = bf16[4,2,32,4096]{3,2,1,0:T(8,128)(2,1)} custom-call(s32[4]{0:T(128)} %pad_add_fusion.place, bf16[16,32,8192]{2,1,0:T(8,128)(2,1)} %bitcast.84), custom_call_target="tpu_custom_call" | custom-call | tf_op jit(solution)/shard_map/pallas_call | solution.py:297
  9.9 0.1 collective-permute-start
  10.1 0.6 pad_maximum_fusion.1.piece
  10.7 0.0 collective-permute-done.1.received
  10.7 4.3 %shard_map.86 = (bf16[64,4096]{1,0:T(8,128)(2,1)S(1)}, bf16[64,4608]{1,0:T(8,128)(2,1)}, bf16[64,4608]{1,0:T(8,128)(2,1)}, bf16[64,4608]{1,0:T(8,128)(2,1)}) custom-call(s32[4]{0:T(128)} %pad_add_fusion.place, bf16[16,32,8192]{2,1,0:T(8,128)(2,1)} %bitcast.85, bf16[4,2,32,4096]{3,2,1,0:T(8,128)(2,1)} %collective-permute-done.1.received, ...), custom_call_target="tpu_custom_call" | custom-call | tf_op jit(solution)/shard_map/pallas_call | solution.py:343
  15.1 0.0 copy-start.3
  15.1 1.8 collective-permute-start.2
  16.9 3.3 %collective-permute-start.3 = (bf16[64,4608]{1,0:T(8,128)(2,1)}, bf16[64,4608]{1,0:T(8,128)(2,1)}, u32[]{:S(2)}, u32[]{:S(2)}) collective-permute-start(bf16[64,4608]{1,0:T(8,128)(2,1)} %get-tuple-element.29), channel_id=1, source_target_pairs={{0,8},{4,12},{8,0},{12,4},{1,9},{5,13},{9,1},{13,5},{2,10},{6,14},... | collective-permute-start | bytes 1769480 | tf_op jit(solution)/shard_map/ppermute | solution.py:262
  20.2 0.7 collective-permute-start.4
  20.9 0.0 collective-permute-done.received
  20.9 3.0 %shard_map.88 = (bf16[4,32,4096]{2,1,0:T(8,128)(2,1)S(1)}, bf16[4,32,4096]{2,1,0:T(8,128)(2,1)S(1)}) custom-call(s32[4]{0:T(128)} %pad_add_fusion.place, bf16[16,32,8192]{2,1,0:T(8,128)(2,1)} %bitcast.86, bf16[4,2,32,4096]{3,2,1,0:T(8,128)(2,1)} %collective-permute-done.received), custom_call_target="tpu_custom_call" | custom-call | tf_op jit(solution)/shard_map/pallas_call | solution.py:343
  23.9 3.0 %collective-permute-start.6 = (bf16[4,32,4096]{2,1,0:T(8,128)(2,1)S(1)}, bf16[4,32,4096]{2,1,0:T(8,128)(2,1)}, u32[]{:S(2)}, u32[]{:S(2)}) collective-permute-start(bf16[4,32,4096]{2,1,0:T(8,128)(2,1)S(1)} %get-tuple-element.35), channel_id=1, source_target_pairs={{0,2},{2,0},{1,3},{3,1},{4,6},{6,4},{5,7},{7,5},{8,10},{10,8},{9,1... | collective-permute-start | bytes 3145736 | tf_op jit(solution)/shard_map/ppermute | solution.py:387
  26.9 5.7 %collective-permute-done.2.up = bf16[64,4608]{1,0:T(8,128)(2,1)} collective-permute-done((bf16[64,4608]{1,0:T(8,128)(2,1)}, bf16[64,4608]{1,0:T(8,128)(2,1)}, u32[]{:S(2)}, u32[]{:S(2)}) %collective-permute-start.2) | collective-permute-done | bytes 589856 | tf_op jit(solution)/shard_map/ppermute | solution.py:262
  32.6 13.5 %collective-permute-done.3.far = bf16[64,4608]{1,0:T(8,128)(2,1)} collective-permute-done((bf16[64,4608]{1,0:T(8,128)(2,1)}, bf16[64,4608]{1,0:T(8,128)(2,1)}, u32[]{:S(2)}, u32[]{:S(2)}) %collective-permute-start.3) | collective-permute-done | bytes 589856 | tf_op jit(solution)/shard_map/ppermute | solution.py:262
  46.1 0.0 collective-permute-done.4.down
  46.1 1.8 shard_map.87
  47.9 0.0 copy-start.2
  48.0 3.0 %collective-permute-start.5 = (bf16[32,8192]{1,0:T(8,128)(2,1)S(1)}, bf16[32,8192]{1,0:T(8,128)(2,1)S(1)}, u32[]{:S(2)}, u32[]{:S(2)}) collective-permute-start(bf16[32,8192]{1,0:T(8,128)(2,1)S(1)} %get-tuple-element.32), channel_id=1, source_target_pairs={{0,2},{2,0},{1,3},{3,1},{4,6},{6,4},{5,7},{7,5},{8,10},{10,8},{9,1... | collective-permute-start | bytes 1572872 | tf_op jit(solution)/shard_map/ppermute | solution.py:392
  51.1 0.0 collective-permute-done.6
  51.1 2.3 %fusion.2 = (bf16[32,4096]{1,0:T(8,128)(2,1)}, bf16[32,4096]{1,0:T(8,128)(2,1)}, bf16[32,4096]{1,0:T(8,128)(2,1)S(1)}, f32[32,4096]{1,0:T(8,128)}) fusion(bf16[4,32,4096]{2,1,0:T(8,128)(2,1)} %collective-permute-done.6, bf16[4,32,4096]{2,1,0:T(8,128)(2,1)S(1)} %get-tuple-element.34), kind=kLoop, calls=%fused_computation.8 | loop fusion | flops 1966080 | bytes 3407872 | tf_op jit(solution)/shard_map/convert_element_type | solution.py:390
  53.4 2.7 %collective-permute-start.9 = (bf16[32,4096]{1,0:T(8,128)(2,1)}, bf16[32,4096]{1,0:T(8,128)(2,1)S(1)}, u32[]{:S(2)}, u32[]{:S(2)}) collective-permute-start(bf16[32,4096]{1,0:T(8,128)(2,1)} %get-tuple-element.44), channel_id=1, source_target_pairs={{0,12},{4,0},{8,4},{12,8},{1,13},{5,1},{9,5},{13,9},{2,14},{6,2},{... | collective-permute-start | bytes 786440 | tf_op jit(solution)/shard_map/ppermute | solution.py:262
  56.1 0.0 collective-permute-start.8
  56.1 1.2 collective-permute-start.7
  57.3 4.4 %collective-permute-done.5.back = bf16[32,8192]{1,0:T(8,128)(2,1)S(1)} collective-permute-done((bf16[32,8192]{1,0:T(8,128)(2,1)S(1)}, bf16[32,8192]{1,0:T(8,128)(2,1)S(1)}, u32[]{:S(2)}, u32[]{:S(2)}) %collective-permute-start.5) | collective-permute-done | bytes 524320 | tf_op jit(solution)/shard_map/ppermute | solution.py:392
  61.8 0.6 copy-done.7
  62.5 0.1 maximum_select_fusion
  62.5 0.4 select_n.48
  62.9 0.0 copy-start.6
  62.9 1.1 fusion.14
  64.1 0.0 copy-start.5
  64.2 0.1 pad_maximum_fusion
  64.3 0.0 copy-start.8
  64.3 2.3 %collective-permute-start.10 = (bf16[1024,256]{1,0:T(8,128)(2,1)S(1)}, bf16[1024,256]{1,0:T(8,128)(2,1)}, u32[]{:S(2)}, u32[]{:S(2)}) collective-permute-start(bf16[1024,256]{1,0:T(8,128)(2,1)S(1)} %bitcast.90), channel_id=1, source_target_pairs={{0,1},{1,0},{2,3},{3,2},{4,5},{5,4},{6,7},{7,6},{8,9},{9,8},{10,11... | collective-permute-start | bytes 1572872 | tf_op jit(solution)/shard_map/ppermute | solution.py:258
  66.6 0.0 collective-permute-done.9.down
  66.6 0.0 collective-permute-done.8.up
  66.6 0.0 copy-start.12
  66.6 1.6 collective-permute-done.7.far
  68.2 3.3 %shard_map.89 = (f32[32,8192]{1,0:T(8,128)}, bf16[8,8,32,128]{3,2,1,0:T(8,128)(2,1)}) custom-call(f32[32,4096]{1,0:T(8,128)} %copy-done.2, bf16[32,8192]{1,0:T(8,128)(2,1)} %copy-done.7, f32[32,4096]{1,0:T(8,128)} %get-tuple-element.47.right, bf16[32,4096]{1,0:T(8,128)(2,1)} %collective-permute-done.7.far, bf16[32,4096]{1,0:T(8,128)(2,1)} %copy-done.12, ...), custom_call_target="tpu_custom_call" | custom-call | tf_op jit(solution)/shard_map/pallas_call | solution.py:246
  71.5 4.2 %all-to-all-start = ((bf16[8,8,32,128]{3,2,1,0:T(8,128)(2,1)}), bf16[8,8,32,128]{3,2,1,0:T(8,128)(2,1)S(1)}, u32[]{:S(2)}, u32[]{:S(2)}) async-start(bf16[8,8,32,128]{3,2,1,0:T(8,128)(2,1)} %get-tuple-element.36), calls=%async_computation | async-start | bytes 1048576 | tf_op jit(solution)/shard_map/all_to_all | solution.py:419
  75.7 0.2 copy.46
  75.9 0.2 copy.47
  76.1 0.2 constant_dynamic-slice_fusion
  76.3 0.0 collective-permute-done.10.q_other
  76.3 6.4 %all-to-all-done.blocks = bf16[8,8,32,128]{3,2,1,0:T(8,128)(2,1)S(1)} async-done(((bf16[8,8,32,128]{3,2,1,0:T(8,128)(2,1)}), bf16[8,8,32,128]{3,2,1,0:T(8,128)(2,1)S(1)}, u32[]{:S(2)}, u32[]{:S(2)}) %all-to-all-start) | async-done | bytes 524320 | tf_op jit(solution)/shard_map/all_to_all | solution.py:419
  82.7 0.8 copy-done.9
  83.5 2.3 %shard_map.90 = (bf16[8,32,128]{2,1,0:T(8,128)(2,1)S(1)}, bf16[8,32,256]{2,1,0:T(8,128)(2,1)}) custom-call(s32[4]{0:T(128)} %pad_add_fusion.place, bf16[8,8,32,128]{3,2,1,0:T(8,128)(2,1)} %copy-done.9, bf16[1024,256]{1,0:T(8,128)(2,1)} %bitcast.91, bf16[1024,256]{1,0:T(8,128)(2,1)} %collective-permute-done.10.q_other), custom_call_target="tpu_custom_call" | custom-call | tf_op jit(solution)/shard_map/pallas_call | solution.py:197
  85.8 3.4 %all-to-all-start.1 = ((bf16[8,32,256]{2,1,0:T(8,128)(2,1)}), bf16[8,32,256]{2,1,0:T(8,128)(2,1)S(1)}, u32[]{:S(2)}, u32[]{:S(2)}) async-start(bf16[8,32,256]{2,1,0:T(8,128)(2,1)} %get-tuple-element.37), calls=%async_computation.1 | async-start | bytes 262144 | tf_op jit(solution)/shard_map/all_to_all | solution.py:421
  89.2 0.7 fusion.5.before
  89.9 4.5 %all-to-all-done.1.terms = bf16[8,32,256]{2,1,0:T(8,128)(2,1)S(1)} async-done(((bf16[8,32,256]{2,1,0:T(8,128)(2,1)}), bf16[8,32,256]{2,1,0:T(8,128)(2,1)S(1)}, u32[]{:S(2)}, u32[]{:S(2)}) %all-to-all-start.1) | async-done | bytes 131104 | tf_op jit(solution)/shard_map/all_to_all | solution.py:421
  94.4 0.7 copy-done.10
  95.1 1.7 shard_map.91
  96.7 16.0 %all_to_all.20 = bf16[8,4,32,128]{3,2,1,0:T(8,128)(2,1)S(1)} all-to-all(bf16[8,4,32,128]{3,2,1,0:T(8,128)(2,1)} %shard_map.91), channel_id=1, replica_groups=mesh['x'=4,'ylo'=2,'z'=4,'yhi'=2,'core'=2] {'z','yhi'}, dimensions={0} | all-to-all | bytes 524288 | tf_op jit(solution)/shard_map/all_to_all | solution.py:423
  112.8 4.0 %collective-permute-start.11 = (bf16[4,256,128]{2,1,0:T(8,128)(2,1)S(1)}, bf16[4,256,128]{2,1,0:T(8,128)(2,1)S(1)}, u32[]{:S(2)}, u32[]{:S(2)}) collective-permute-start(bf16[4,256,128]{2,1,0:T(8,128)(2,1)S(1)} %bitcast.81), channel_id=1, source_target_pairs={{0,1},{1,0},{2,3},{3,2},{4,5},{5,4},{6,7},{7,6},{8,9},{9,8},{10,11... | collective-permute-start | bytes 786440 | tf_op jit(solution)/shard_map/ppermute | solution.py:258
  116.8 1.2 collective-permute-done.11.other_ref
  117.9 3.7 %shard_map.92 = bf16[64,288,128]{2,1,0:T(8,128)(2,1)S(1)} custom-call(bf16[4,256,128]{2,1,0:T(8,128)(2,1)S(1)} %bitcast.82, bf16[4,256,128]{2,1,0:T(8,128)(2,1)S(1)} %collective-permute-done.11.other_ref), custom_call_target="tpu_custom_call" | custom-call | tf_op jit(solution)/shard_map/pallas_call | solution.py:62
  121.6 62.3 %all_to_all.21 = bf16[64,288,128]{2,1,0:T(8,128)(2,1)} all-to-all(bf16[64,288,128]{2,1,0:T(8,128)(2,1)S(1)} %shard_map.92), channel_id=1, replica_groups=mesh['x'=4,'ylo'=2,'z'=4,'yhi'=2,'core'=2] {'x','ylo','z','yhi'}, dimensions={0} | all-to-all | bytes 9437184 | tf_op jit(solution)/shard_map/all_to_all | solution.py:427
  183.9 1.5 collective-permute-start.12
  185.5 7.5 %shard_map.93 = (bf16[8,2,32,8192]{3,2,1,0:T(8,128)(2,1)}, f32[32,8192]{1,0:T(8,128)}, f32[32,8192]{1,0:T(8,128)}, f32[32,8192]{1,0:T(8,128)}) custom-call(s32[4]{0:T(128)} %pad_add_fusion.place, bf16[8,8,288,128]{3,2,1,0:T(8,128)(2,1)} %bitcast.26.refs_0_, f32[32,8192]{1,0:T(8,128)} %get-tuple-element.39.refs_1_, f32[32,8192]{1,0:T(8,128)} %refs_2_.1, ...), custom_call_target="tpu_custom_call" | custom-call | tf_op jit(solution)/shard_map/pallas_call | solution.py:127
  193.0 0.4 collective-permute-done.12
  193.4 4.2 %shard_map.94 = bf16[8,2,32,8192]{3,2,1,0:T(8,128)(2,1)} custom-call(s32[4]{0:T(128)} %pad_add_fusion.place, bf16[8,8,288,128]{3,2,1,0:T(8,128)(2,1)} %bitcast.25.moved, bf16[8,2,32,8192]{3,2,1,0:T(8,128)(2,1)} %get-tuple-element.40._), custom_call_target="tpu_custom_call", output_to_operand_aliasing={{}: (2, {})} | custom-call | tf_op jit(solution)/shard_map/pallas_call | solution.py:163
  (40 shorter events, 0.4 us)
Async XLA Ops:
  0.6 9.4 %copy-start = (f32[512,256]{1,0:T(8,128)S(1)}, f32[512,256]{1,0:T(8,128)}, u32[]{:S(2)}) copy-start(f32[512,256]{1,0:T(8,128)} %param.9) | copy-start | bytes 1572868
  4.8 5.9 %collective-permute-start.1 = (bf16[4,2,32,4096]{3,2,1,0:T(8,128)(2,1)}, bf16[4,2,32,4096]{3,2,1,0:T(8,128)(2,1)}, u32[]{:S(2)}, u32[]{:S(2)}) collective-permute-start(bf16[4,2,32,4096]{3,2,1,0:T(8,128)(2,1)} %shard_map.84), channel_id=1, source_target_pairs={{0,1},{1,0},{2,3},{3,2},{4,5},{5,4},{6,7},{7,6},{8,9},{9,8},{10,11... | collective-permute-start | bytes 6291464 | tf_op jit(solution)/shard_map/ppermute | solution.py:258
  9.9 11.0 %collective-permute-start = (bf16[4,2,32,4096]{3,2,1,0:T(8,128)(2,1)}, bf16[4,2,32,4096]{3,2,1,0:T(8,128)(2,1)}, u32[]{:S(2)}, u32[]{:S(2)}) collective-permute-start(bf16[4,2,32,4096]{3,2,1,0:T(8,128)(2,1)} %shard_map.85), channel_id=1, source_target_pairs={{0,1},{1,0},{2,3},{3,2},{4,5},{5,4},{6,7},{7,6},{8,9},{9,8},{10,11... | collective-permute-start | bytes 6291464 | tf_op jit(solution)/shard_map/ppermute | solution.py:258
  15.1 8.9 %copy-start.3 = (bf16[64,4096]{1,0:T(8,128)(2,1)}, bf16[64,4096]{1,0:T(8,128)(2,1)S(1)}, u32[]{:S(2)}) copy-start(bf16[64,4096]{1,0:T(8,128)(2,1)S(1)} %get-tuple-element.27.left) | copy-start | bytes 1572868
  15.1 17.5 %collective-permute-start.2 = (bf16[64,4608]{1,0:T(8,128)(2,1)}, bf16[64,4608]{1,0:T(8,128)(2,1)}, u32[]{:S(2)}, u32[]{:S(2)}) collective-permute-start(bf16[64,4608]{1,0:T(8,128)(2,1)} %get-tuple-element.28), channel_id=1, source_target_pairs={{0,4},{4,8},{8,12},{12,0},{1,5},{5,9},{9,13},{13,1},{2,6},{6,10},{... | collective-permute-start | bytes 1769480 | tf_op jit(solution)/shard_map/ppermute | solution.py:262
  16.9 29.2 %collective-permute-start.3 = (bf16[64,4608]{1,0:T(8,128)(2,1)}, bf16[64,4608]{1,0:T(8,128)(2,1)}, u32[]{:S(2)}, u32[]{:S(2)}) collective-permute-start(bf16[64,4608]{1,0:T(8,128)(2,1)} %get-tuple-element.29), channel_id=1, source_target_pairs={{0,8},{4,12},{8,0},{12,4},{1,9},{5,13},{9,1},{13,5},{2,10},{6,14},... | collective-permute-start | bytes 1769480 | tf_op jit(solution)/shard_map/ppermute | solution.py:262
  20.2 25.9 %collective-permute-start.4 = (bf16[64,4608]{1,0:T(8,128)(2,1)}, bf16[64,4608]{1,0:T(8,128)(2,1)}, u32[]{:S(2)}, u32[]{:S(2)}) collective-permute-start(bf16[64,4608]{1,0:T(8,128)(2,1)} %get-tuple-element.30), channel_id=1, source_target_pairs={{0,12},{4,0},{8,4},{12,8},{1,13},{5,1},{9,5},{13,9},{2,14},{6,2},{... | collective-permute-start | bytes 1769480 | tf_op jit(solution)/shard_map/ppermute | solution.py:262
  23.9 27.2 %collective-permute-start.6 = (bf16[4,32,4096]{2,1,0:T(8,128)(2,1)S(1)}, bf16[4,32,4096]{2,1,0:T(8,128)(2,1)}, u32[]{:S(2)}, u32[]{:S(2)}) collective-permute-start(bf16[4,32,4096]{2,1,0:T(8,128)(2,1)S(1)} %get-tuple-element.35), channel_id=1, source_target_pairs={{0,2},{2,0},{1,3},{3,1},{4,6},{6,4},{5,7},{7,5},{8,10},{10,8},{9,1... | collective-permute-start | bytes 3145736 | tf_op jit(solution)/shard_map/ppermute | solution.py:387
  47.9 16.1 %copy-start.2 = (f32[32,4096]{1,0:T(8,128)}, f32[32,4096]{1,0:T(8,128)S(1)}, u32[]{:S(2)}) copy-start(f32[32,4096]{1,0:T(8,128)S(1)} %get-tuple-element.31.left) | copy-start | bytes 1572868
  48.0 13.7 %collective-permute-start.5 = (bf16[32,8192]{1,0:T(8,128)(2,1)S(1)}, bf16[32,8192]{1,0:T(8,128)(2,1)S(1)}, u32[]{:S(2)}, u32[]{:S(2)}) collective-permute-start(bf16[32,8192]{1,0:T(8,128)(2,1)S(1)} %get-tuple-element.32), channel_id=1, source_target_pairs={{0,2},{2,0},{1,3},{3,1},{4,6},{6,4},{5,7},{7,5},{8,10},{10,8},{9,1... | collective-permute-start | bytes 1572872 | tf_op jit(solution)/shard_map/ppermute | solution.py:392
  53.4 13.2 %collective-permute-start.9 = (bf16[32,4096]{1,0:T(8,128)(2,1)}, bf16[32,4096]{1,0:T(8,128)(2,1)S(1)}, u32[]{:S(2)}, u32[]{:S(2)}) collective-permute-start(bf16[32,4096]{1,0:T(8,128)(2,1)} %get-tuple-element.44), channel_id=1, source_target_pairs={{0,12},{4,0},{8,4},{12,8},{1,13},{5,1},{9,5},{13,9},{2,14},{6,2},{... | collective-permute-start | bytes 786440 | tf_op jit(solution)/shard_map/ppermute | solution.py:262
  56.1 10.5 %collective-permute-start.8 = (bf16[32,4096]{1,0:T(8,128)(2,1)}, bf16[32,4096]{1,0:T(8,128)(2,1)S(1)}, u32[]{:S(2)}, u32[]{:S(2)}) collective-permute-start(bf16[32,4096]{1,0:T(8,128)(2,1)} %get-tuple-element.45), channel_id=1, source_target_pairs={{0,4},{4,8},{8,12},{12,0},{1,5},{5,9},{9,13},{13,1},{2,6},{6,10},{... | collective-permute-start | bytes 786440 | tf_op jit(solution)/shard_map/ppermute | solution.py:262
  56.1 12.1 %collective-permute-start.7 = (bf16[32,4096]{1,0:T(8,128)(2,1)S(1)}, bf16[32,4096]{1,0:T(8,128)(2,1)}, u32[]{:S(2)}, u32[]{:S(2)}) collective-permute-start(bf16[32,4096]{1,0:T(8,128)(2,1)S(1)} %get-tuple-element.46), channel_id=1, source_target_pairs={{0,8},{4,12},{8,0},{12,4},{1,9},{5,13},{9,1},{13,5},{2,10},{6,14},... | collective-permute-start | bytes 786440 | tf_op jit(solution)/shard_map/ppermute | solution.py:262
  61.7 0.8 copy-start.7
  62.9 12.8 %copy-start.6 = (f32[32,8192]{1,0:T(8,128)S(1)}, f32[32,8192]{1,0:T(8,128)}, u32[]{:S(2)}) copy-start(f32[32,8192]{1,0:T(8,128)} %refs_3_.1) | copy-start | bytes 3145732
  64.1 11.8 %copy-start.5 = (f32[32,8192]{1,0:T(8,128)S(1)}, f32[32,8192]{1,0:T(8,128)}, u32[]{:S(2)}) copy-start(f32[32,8192]{1,0:T(8,128)} %refs_2_.1) | copy-start | bytes 3145732
  64.3 18.4 %copy-start.8 = (bf16[8,4,32,256]{3,2,1,0:T(8,128)(2,1)}, bf16[8,4,32,256]{3,2,1,0:T(8,128)(2,1)S(1)}, u32[]{:S(2)}) copy-start(bf16[8,4,32,256]{3,2,1,0:T(8,128)(2,1)S(1)} %copy.36) | copy-start | bytes 1572868
  64.3 12.1 %collective-permute-start.10 = (bf16[1024,256]{1,0:T(8,128)(2,1)S(1)}, bf16[1024,256]{1,0:T(8,128)(2,1)}, u32[]{:S(2)}, u32[]{:S(2)}) collective-permute-start(bf16[1024,256]{1,0:T(8,128)(2,1)S(1)} %bitcast.90), channel_id=1, source_target_pairs={{0,1},{1,0},{2,3},{3,2},{4,5},{5,4},{6,7},{7,6},{8,9},{9,8},{10,11... | collective-permute-start | bytes 1572872 | tf_op jit(solution)/shard_map/ppermute | solution.py:258
  66.6 1.6 copy-start.11
  66.6 1.6 copy-start.12
  71.5 11.2 %all-to-all-start = ((bf16[8,8,32,128]{3,2,1,0:T(8,128)(2,1)}), bf16[8,8,32,128]{3,2,1,0:T(8,128)(2,1)S(1)}, u32[]{:S(2)}, u32[]{:S(2)}) async-start(bf16[8,8,32,128]{3,2,1,0:T(8,128)(2,1)} %get-tuple-element.36), calls=%async_computation | async-start | bytes 1048576 | tf_op jit(solution)/shard_map/all_to_all | solution.py:419
  82.7 0.8 copy-start.9
  85.8 8.6 %copy-start.4 = (bf16[8,32,128]{2,1,0:T(8,128)(2,1)}, bf16[8,32,128]{2,1,0:T(8,128)(2,1)S(1)}, u32[]{:S(2)}) copy-start(bf16[8,32,128]{2,1,0:T(8,128)(2,1)S(1)} %get-tuple-element.38.mean) | copy-start | bytes 196612
  85.8 8.6 %all-to-all-start.1 = ((bf16[8,32,256]{2,1,0:T(8,128)(2,1)}), bf16[8,32,256]{2,1,0:T(8,128)(2,1)S(1)}, u32[]{:S(2)}, u32[]{:S(2)}) async-start(bf16[8,32,256]{2,1,0:T(8,128)(2,1)} %get-tuple-element.37), calls=%async_computation.1 | async-start | bytes 262144 | tf_op jit(solution)/shard_map/all_to_all | solution.py:421
  94.4 0.7 copy-start.10
  112.8 5.2 %collective-permute-start.11 = (bf16[4,256,128]{2,1,0:T(8,128)(2,1)S(1)}, bf16[4,256,128]{2,1,0:T(8,128)(2,1)S(1)}, u32[]{:S(2)}, u32[]{:S(2)}) collective-permute-start(bf16[4,256,128]{2,1,0:T(8,128)(2,1)S(1)} %bitcast.81), channel_id=1, source_target_pairs={{0,1},{1,0},{2,3},{3,2},{4,5},{5,4},{6,7},{7,6},{8,9},{9,8},{10,11... | collective-permute-start | bytes 786440 | tf_op jit(solution)/shard_map/ppermute | solution.py:258
  183.9 9.4 %collective-permute-start.12 = (bf16[64,288,128]{2,1,0:T(8,128)(2,1)}, bf16[64,288,128]{2,1,0:T(8,128)(2,1)}, u32[]{:S(2)}, u32[]{:S(2)}) collective-permute-start(bf16[64,288,128]{2,1,0:T(8,128)(2,1)} %all_to_all.21), channel_id=1, source_target_pairs={{0,1},{1,0},{2,3},{3,2},{4,5},{5,4},{6,7},{7,6},{8,9},{9,8},{10,11... | collective-permute-start | bytes 14155784 | tf_op jit(solution)/shard_map/ppermute | solution.py:258
  193.4 4.2 %copy-start.1 = (f32[512,256]{1,0:T(8,128)S(1)}, f32[512,256]{1,0:T(8,128)}, u32[]{:S(2)}) copy-start(f32[512,256]{1,0:T(8,128)} %param.9) | copy-start | bytes 1572868

commit v4 on v3

--- a/solution.py
+++ b/solution.py
@@ -32,6 +32,10 @@
     return lax.dot_general(left, right, (((1,), (1,)), ((), ())), preferred_element_type=F32)
 
 
+def updated(before, delta):
+    return (before.astype(F32) - (0.7 * 1.9) * delta.astype(F32)).astype(BF16)
+
+
 def factor_kernel(own_ref, other_ref, out):
     def left_factor(ref):
         return jnp.concatenate([ref[0], ref[1]], 1).astype(F32)
@@ -46,15 +50,15 @@
         other = 1.5 * other - 0.5 * dot_nn(low_other, gram_mat)
     low_own, low_other = own.astype(BF16), other.astype(BF16)
     qnew = dot_tn(own_ref[2], low_own) + dot_tn(other_ref[2], low_other)
-    delta = dot_nt(low_own, qnew.astype(BF16))
-    weights = (own_ref[3].astype(F32) - (0.7 * 1.9) * delta).astype(BF16)
-    delta = delta.astype(BF16).reshape(8, 32, 128)
+    delta = dot_nt(low_own, qnew.astype(BF16)).astype(BF16)
+    weights = updated(own_ref[3], delta)
+    delta = delta.reshape(8, 32, 128)
 
     @pl.loop(0, 8)
     def _(island):
         for chip in range(8):
-            out[island * 8 + chip, :256] = weights
-            out[island * 8 + chip, 256:] = delta[chip]
+            out[island * 8 + chip] = weights
+            out[island * 8 + chip, chip * 32 : chip * 32 + 32] = delta[chip]
 
 
 def factors(own, other):
@@ -63,7 +67,7 @@
         factor_kernel,
         in_specs=[vmem, vmem],
         out_specs=vmem,
-        out_shape=jax.ShapeDtypeStruct((64, 288, 128), BF16),
+        out_shape=jax.ShapeDtypeStruct((64, 256, 128), BF16),
         compiler_params=pltpu.CompilerParams(vmem_limit_bytes=32 * 1024 * 1024),
     )(own, other)
 
@@ -72,14 +76,21 @@
     return pl.ds(g * 1024, 1024)
 
 
-def put_weights(moved, full):
+def put_weights(moved, before, full, chip):
+    at = pl.ds(pl.multiple_of(chip * 32, 32), 32)
+    deltas = []
     for n in range(8):
-        full[:, :, n * 128 : (n + 1) * 128] = moved[n, :256].reshape(8, 32, 128)
+        cols = slice(n * 128, (n + 1) * 128)
+        full[:, :, cols] = moved[n].reshape(8, 32, 128)
+        deltas.append(moved[n, at, :])
+        full[pl.ds(chip, 1), :, cols] = updated(before[:, cols], deltas[n])[None]
+    return deltas
 
 
 def own_kernel(place, *refs):
-    ins, outs, rest = refs[:4], refs[4:8], refs[8:]
-    held, made, in_sems, out_sems = rest[:4], rest[4:8], rest[8], rest[9]
+    ins, outs, rest = refs[:5], refs[5:9], refs[9:]
+    held, made, in_sems, out_sems = rest[:5], rest[5:9], rest[9], rest[10]
+    chip = place[1] * 2 + place[2]
     loads, stores = [], []
     for g in range(8):
         views = [ins[0].at[:, g]] + [ref.at[:, block_cols(g)] for ref in ins[1:]]
@@ -96,15 +107,14 @@
     for copies in loads:
         for copy in copies:
             copy.start()
-    moved, merged, momentum, params = held
+    moved, before, merged, momentum, params = held
     full, new_params, new_momentum, new_error = made
     for g in range(8):
         for copy in loads[g]:
             copy.wait()
-        put_weights(moved.at[g], full.at[g])
-        for n in range(8):
+        for n, delta in enumerate(put_weights(moved.at[g], before.at[g], full.at[g], chip)):
             at = (g, slice(None), slice(n * 128, (n + 1) * 128))
-            delta = moved[g, n, 256:].astype(F32)
+            delta = delta.astype(F32)
             new_error[at] = merged[at] - delta
             step = 0.9 * momentum[at] + delta
             new_momentum[at] = step
@@ -121,59 +131,67 @@
 ANYWHERE = pl.BlockSpec(memory_space=pl.ANY)
 
 
-def own_rows(place, moved, merged, momentum, params):
+def own_rows(place, moved, before, merged, momentum, params):
     row_shape = jax.ShapeDtypeStruct((32, 8192), F32)
     rows = pltpu.VMEM((8, 32, 1024), F32)
+    weights = pltpu.VMEM((8, 8, 32, 1024), BF16)
     return pl.pallas_call(
         own_kernel,
-        in_specs=[SMEM] + [ANYWHERE] * 4,
+        in_specs=[SMEM] + [ANYWHERE] * 5,
         out_specs=[ANYWHERE] * 4,
         out_shape=[FULL_SHAPE, row_shape, row_shape, row_shape],
         scratch_shapes=[
-            pltpu.VMEM((8, 8, 288, 128), BF16), rows, rows, rows,
-            pltpu.VMEM((8, 8, 32, 1024), BF16), rows, rows, rows,
-            pltpu.SemaphoreType.DMA((4, 8)),
+            pltpu.VMEM((8, 8, 256, 128), BF16), pltpu.VMEM((8, 32, 1024), BF16), rows, rows, rows,
+            weights, rows, rows, rows,
+            pltpu.SemaphoreType.DMA((5, 8)),
             pltpu.SemaphoreType.DMA((4, 8)),
         ],
         compiler_params=pltpu.CompilerParams(vmem_limit_bytes=VMEM),
-    )(place, moved.reshape(8, 8, 288, 128), merged, momentum, params)
-
-
-def other_kernel(place, moved, _, full, held, made, in_sems, out_sems):
-    side = 1 - place[0]
+    )(place, moved.reshape(8, 8, 256, 128), before, merged, momentum, params)
+
+
+def other_kernel(place, moved, before, _, full, held, held_before, made, sems, before_sems, out_sems):
+    side, chip = 1 - place[0], place[1] * 2 + place[2]
     loads = [
-        pltpu.make_async_copy(moved.at[:, g, pl.ds(0, 256)], held.at[g], in_sems.at[g])
+        [
+            pltpu.make_async_copy(moved.at[:, g], held.at[g], sems.at[g]),
+            pltpu.make_async_copy(before.at[:, block_cols(g)], held_before.at[g], before_sems.at[g]),
+        ]
         for g in range(8)
     ]
     stores = [
         pltpu.make_async_copy(made.at[g], full.at[:, side, :, block_cols(g)], out_sems.at[g])
         for g in range(8)
     ]
-    for copy in loads:
-        copy.start()
+    for copies in loads:
+        for copy in copies:
+            copy.start()
     for g in range(8):
-        loads[g].wait()
-        put_weights(held.at[g], made.at[g])
+        for copy in loads[g]:
+            copy.wait()
+        put_weights(held.at[g], held_before.at[g], made.at[g], chip)
         stores[g].start()
     for copy in stores:
         copy.wait()
 
 
-def other_rows(place, moved, full):
+def other_rows(place, moved, before, full):
     return pl.pallas_call(
         other_kernel,
-        in_specs=[SMEM, ANYWHERE, ANYWHERE],
+        in_specs=[SMEM] + [ANYWHERE] * 3,
         out_specs=ANYWHERE,
         out_shape=FULL_SHAPE,
-        input_output_aliases={2: 0},
+        input_output_aliases={3: 0},
         scratch_shapes=[
             pltpu.VMEM((8, 8, 256, 128), BF16),
+            pltpu.VMEM((8, 32, 1024), BF16),
             pltpu.VMEM((8, 8, 32, 1024), BF16),
+            pltpu.SemaphoreType.DMA((8,)),
             pltpu.SemaphoreType.DMA((8,)),
             pltpu.SemaphoreType.DMA((8,)),
         ],
         compiler_params=pltpu.CompilerParams(vmem_limit_bytes=VMEM),
-    )(place, moved.reshape(8, 8, 288, 128), full)
+    )(place, moved.reshape(8, 8, 256, 128), before, full)
 
 
 def middle_kernel(place, blocks, q_own, q_other, mean, out):
@@ -410,26 +428,27 @@
     q_own = jnp.stack([pieces[:, :, n] for n in (0, 2, 1, 3)], 1).reshape(1024, 256)
     q_other = swap_cores(q_own)
 
-    def columns(value):
-        return lax.dynamic_index_in_dim(value.reshape(32, 8, 8, 128), isl, 2, False)
-
-    before = (columns(params) - (0.7 * 0.9 * 0.9) * columns(momentum)).astype(BF16)
-    before = before.transpose(1, 0, 2)
+    before = (params - (0.7 * 0.9 * 0.9) * momentum).astype(BF16)
+    before = lax.optimization_barrier(before)
+    before_other = swap_cores(before)
+    columns = lax.dynamic_index_in_dim(before.reshape(32, 8, 8, 128), isl, 2, False)
+    columns = columns.transpose(1, 0, 2)
 
     blocks = lax.all_to_all(blocks, ISLAND, 0, 0, tiled=True)
     mean, terms = middle(place, blocks, q_own, q_other)
     terms = lax.all_to_all(terms, ISLAND, 0, 0, tiled=True)
 
-    own = lax.all_to_all(gathered(terms, mean, before), ZY, 0, 0, tiled=True)
+    own = lax.all_to_all(gathered(terms, mean, columns), ZY, 0, 0, tiled=True)
     own = own.transpose(1, 0, 2, 3).reshape(4, 256, 128)
+    own, before_other = lax.optimization_barrier((own, before_other))
     other = swap_cores(own)
 
     moved_own = lax.all_to_all(factors(own, other), CHIPS, 0, 0, tiled=True)
     moved_other = swap_cores(moved_own)
     params_full, new_params, new_momentum, new_error = own_rows(
-        place, moved_own, merged, momentum, params
+        place, moved_own, before, merged, momentum, params
     )
-    params_full = other_rows(place, moved_other, params_full)
+    params_full = other_rows(place, moved_other, before_other, params_full)
     return (params_full.reshape(512, 8192), new_params, new_momentum, new_error[None])
 
 

time: 198 us -> 193 us (0.975)
  blocking collectives: 78.3 us -> 71.7 us
  waiting for transfers between devices: 37.6 us -> 32.6 us
  local copies, waits for them, and re-layouts: 4.55 us -> 7.95 us
  starting transfers between devices: 32.7 us -> 35.9 us
    all_to_all x1, blocking collectives: 62.3 us -> 56.1 us  [on_device(): moved_own = lax.all_to_all(factors(own, other), CHIPS, 0, 0, tiled=True)]
    ppermute x6, waiting for transfers between devices: 20.8 us -> 17.6 us  [along_z(): return lax.ppermute(value, 'z', [(at, (at + step) % 4) for at in range(4)])]
    ppermute x5 -> x6, starting transfers between devices: 9.46 us -> 12 us  [swap_cores(): return lax.ppermute(value, 'core', SWAP)]
    all_to_all x1, waiting for transfers between devices: 6.38 us -> 4.01 us  [on_device(): blocks = lax.all_to_all(blocks, ISLAND, 0, 0, tiled=True)]
    unnamed x44 -> x45, local copies, waits for them, and re-layouts: 2.71 us -> 4.75 us
  transfers between devices with their start and end apart: 15 -> 16, of which waited for: 8 -> 7; matrix products, arithmetic and copies ran while one was open for 3% -> 4% of each run, Pallas kernels for 12% -> 14%
where the time goes in v4:
time: 193 us; the launch traced here: 192 us
  blocking collectives  71.7 us (37%)
  Pallas kernels  39.2 us (20%)
  starting transfers between devices  35.9 us (19%)
  waiting for transfers between devices  32.6 us (17%)
  local copies, waits for them, and re-layouts  7.95 us (4%)
  other arithmetic  3.88 us (2%)
    all_to_all x1, blocking collectives, on_device(): moved_own = lax.all_to_all(factors(own, other), CHIPS, 0, 0, tiled=True)  56.1 us
    ppermute x6, waiting for transfers between devices, along_z(): return lax.ppermute(value, 'z', [(at, (at + step) % 4) for at in range(4)])  17.6 us
    all_to_all x1, blocking collectives, on_device(): own = lax.all_to_all(gathered(terms, mean, columns), ZY, 0, 0, tiled=True)  15.6 us
    ppermute x6, starting transfers between devices, swap_cores(): return lax.ppermute(value, 'core', SWAP)  12 us
    ppermute x6, starting transfers between devices, along_z(): return lax.ppermute(value, 'z', [(at, (at + step) % 4) for at in range(4)])  9.54 us
    pallas_call x1, Pallas kernels, own_rows(): pl.pallas_call(own_kernel, in_specs=[SMEM] + [ANYWHERE] * 5, out_specs=[A...  7.59 us
    pallas_call x2, Pallas kernels, theirs(): pl.pallas_call(functools.partial(theirs_kernel, half), in_specs=[pl.Block...  7.18 us
    pallas_call x2, Pallas kernels, pair_call(): pl.pallas_call(kernel, in_specs=[pl.BlockSpec(memory_space=pltpu.SMEM), a...  7.14 us
  transfers between devices with their start and end apart: 16, of which 7 were waited for; matrix products, arithmetic and copies ran while one was open for 4% of the time, Pallas kernels for 14%

profile of v4, /device:TPU:1, one launch (start us, length us, event | category | flops | bytes accessed | tf_op | source)
XLA Modules:
  0.0 192.5 jit_solution(13070640730950974408)
XLA Ops:
  0.6 0.0 copy-start
  0.7 0.6 pad_add_fusion.place
  1.3 3.6 %shard_map.84 = bf16[4,2,32,4096]{3,2,1,0:T(8,128)(2,1)} custom-call(s32[4]{0:T(128)} %pad_add_fusion.place, bf16[16,32,8192]{2,1,0:T(8,128)(2,1)} %bitcast.81), custom_call_target="tpu_custom_call" | custom-call | tf_op jit(solution)/shard_map/pallas_call | solution.py:315
  4.9 1.5 collective-permute-start.1
  6.4 3.6 %shard_map.85 = bf16[4,2,32,4096]{3,2,1,0:T(8,128)(2,1)} custom-call(s32[4]{0:T(128)} %pad_add_fusion.place, bf16[16,32,8192]{2,1,0:T(8,128)(2,1)} %bitcast.82), custom_call_target="tpu_custom_call" | custom-call | tf_op jit(solution)/shard_map/pallas_call | solution.py:315
  10.0 0.1 collective-permute-start
  10.1 0.6 pad_maximum_fusion.1.piece
  10.8 0.0 collective-permute-done.1.received
  10.8 4.1 %shard_map.86 = (bf16[64,4096]{1,0:T(8,128)(2,1)S(1)}, bf16[64,4608]{1,0:T(8,128)(2,1)}, bf16[64,4608]{1,0:T(8,128)(2,1)}, bf16[64,4608]{1,0:T(8,128)(2,1)S(1)}) custom-call(s32[4]{0:T(128)} %pad_add_fusion.place, bf16[16,32,8192]{2,1,0:T(8,128)(2,1)} %bitcast.83, bf16[4,2,32,4096]{3,2,1,0:T(8,128)(2,1)} %collective-permute-done.1.received, ...), custom_call_target="tpu_custom_call" | custom-call | tf_op jit(solution)/shard_map/pallas_call | solution.py:361
  14.9 0.8 copy-done.4
  15.7 1.7 collective-permute-start.2
  17.4 3.3 %collective-permute-start.3 = (bf16[64,4608]{1,0:T(8,128)(2,1)}, bf16[64,4608]{1,0:T(8,128)(2,1)}, u32[]{:S(2)}, u32[]{:S(2)}) collective-permute-start(bf16[64,4608]{1,0:T(8,128)(2,1)} %get-tuple-element.31), channel_id=1, source_target_pairs={{0,8},{4,12},{8,0},{12,4},{1,9},{5,13},{9,1},{13,5},{2,10},{6,14},... | collective-permute-start | bytes 1769480 | tf_op jit(solution)/shard_map/ppermute | solution.py:280
  20.7 0.7 collective-permute-start.4
  21.5 0.0 collective-permute-done.received
  21.5 3.0 %shard_map.88 = (bf16[4,32,4096]{2,1,0:T(8,128)(2,1)S(1)}, bf16[4,32,4096]{2,1,0:T(8,128)(2,1)S(1)}) custom-call(s32[4]{0:T(128)} %pad_add_fusion.place, bf16[16,32,8192]{2,1,0:T(8,128)(2,1)} %bitcast.84, bf16[4,2,32,4096]{3,2,1,0:T(8,128)(2,1)} %collective-permute-done.received), custom_call_target="tpu_custom_call" | custom-call | tf_op jit(solution)/shard_map/pallas_call | solution.py:361
  24.5 0.0 copy-start.1
  24.5 1.0 copy-done.1
  25.5 1.0 copy-done.6
  26.4 2.9 %collective-permute-start.6 = (bf16[4,32,4096]{2,1,0:T(8,128)(2,1)}, bf16[4,32,4096]{2,1,0:T(8,128)(2,1)}, u32[]{:S(2)}, u32[]{:S(2)}) collective-permute-start(bf16[4,32,4096]{2,1,0:T(8,128)(2,1)} %copy-done.6), channel_id=1, source_target_pairs={{0,2},{2,0},{1,3},{3,1},{4,6},{6,4},{5,7},{7,5},{8,10},{10,8},{9,1... | collective-permute-start | bytes 3145736 | tf_op jit(solution)/shard_map/ppermute | solution.py:405
  29.3 3.8 %collective-permute-done.2.up = bf16[64,4608]{1,0:T(8,128)(2,1)} collective-permute-done((bf16[64,4608]{1,0:T(8,128)(2,1)}, bf16[64,4608]{1,0:T(8,128)(2,1)}, u32[]{:S(2)}, u32[]{:S(2)}) %collective-permute-start.2) | collective-permute-done | bytes 589856 | tf_op jit(solution)/shard_map/ppermute | solution.py:280
  33.2 13.5 %collective-permute-done.3.far = bf16[64,4608]{1,0:T(8,128)(2,1)} collective-permute-done((bf16[64,4608]{1,0:T(8,128)(2,1)}, bf16[64,4608]{1,0:T(8,128)(2,1)}, u32[]{:S(2)}, u32[]{:S(2)}) %collective-permute-start.3) | collective-permute-done | bytes 589856 | tf_op jit(solution)/shard_map/ppermute | solution.py:280
  46.7 0.0 collective-permute-done.4.down
  46.7 1.8 shard_map.87
  48.5 0.0 copy-start.3
  48.5 3.0 %collective-permute-start.5 = (bf16[32,8192]{1,0:T(8,128)(2,1)S(1)}, bf16[32,8192]{1,0:T(8,128)(2,1)S(1)}, u32[]{:S(2)}, u32[]{:S(2)}) collective-permute-start(bf16[32,8192]{1,0:T(8,128)(2,1)S(1)} %get-tuple-element.34), channel_id=1, source_target_pairs={{0,2},{2,0},{1,3},{3,1},{4,6},{6,4},{5,7},{7,5},{8,10},{10,8},{9,1... | collective-permute-start | bytes 1572872 | tf_op jit(solution)/shard_map/ppermute | solution.py:410
  51.6 0.0 collective-permute-done.6
  51.7 2.4 %fusion.2 = (bf16[32,4096]{1,0:T(8,128)(2,1)}, bf16[32,4096]{1,0:T(8,128)(2,1)}, bf16[32,4096]{1,0:T(8,128)(2,1)}, f32[32,4096]{1,0:T(8,128)}) fusion(bf16[4,32,4096]{2,1,0:T(8,128)(2,1)} %collective-permute-done.6, bf16[4,32,4096]{2,1,0:T(8,128)(2,1)S(1)} %copy-done.2), kind=kLoop, calls=%fused_computation.9 | loop fusion | flops 1966080 | bytes 3407872 | tf_op jit(solution)/shard_map/convert_element_type | solution.py:408
  54.1 2.6 %collective-permute-start.9 = (bf16[32,4096]{1,0:T(8,128)(2,1)}, bf16[32,4096]{1,0:T(8,128)(2,1)S(1)}, u32[]{:S(2)}, u32[]{:S(2)}) collective-permute-start(bf16[32,4096]{1,0:T(8,128)(2,1)} %get-tuple-element.48), channel_id=1, source_target_pairs={{0,12},{4,0},{8,4},{12,8},{1,13},{5,1},{9,5},{13,9},{2,14},{6,2},{... | collective-permute-start | bytes 786440 | tf_op jit(solution)/shard_map/ppermute | solution.py:280
  56.7 0.0 collective-permute-start.8
  56.7 1.2 collective-permute-start.7
  57.8 5.4 %collective-permute-done.5.back = bf16[32,8192]{1,0:T(8,128)(2,1)S(1)} collective-permute-done((bf16[32,8192]{1,0:T(8,128)(2,1)S(1)}, bf16[32,8192]{1,0:T(8,128)(2,1)S(1)}, u32[]{:S(2)}, u32[]{:S(2)}) %collective-permute-start.5) | collective-permute-done | bytes 524320 | tf_op jit(solution)/shard_map/ppermute | solution.py:410
  63.4 0.6 copy-done.10
  64.0 0.1 maximum_select_fusion
  64.1 0.4 select_n.47
  64.5 1.1 fusion.11
  65.6 0.0 copy-start.8
  65.6 0.0 copy-start.9
  65.7 0.1 pad_maximum_fusion
  65.8 0.8 copy.33
  66.6 1.7 collective-permute-start.10
  68.3 0.0 collective-permute-done.9.down
  68.3 0.3 collective-permute-done.7.far
  68.7 0.4 copy-done.13
  69.0 3.3 %shard_map.89 = (f32[32,8192]{1,0:T(8,128)}, bf16[8,8,32,128]{3,2,1,0:T(8,128)(2,1)}) custom-call(f32[32,4096]{1,0:T(8,128)} %copy-done.3, bf16[32,8192]{1,0:T(8,128)(2,1)} %copy-done.10, f32[32,4096]{1,0:T(8,128)} %get-tuple-element.51.right, bf16[32,4096]{1,0:T(8,128)(2,1)} %collective-permute-done.7.far, bf16[32,4096]{1,0:T(8,128)(2,1)} %collective-permute-done.8.up, ...), custom_call_target="tpu_custom_call" | custom-call | tf_op jit(solution)/shard_map/pallas_call | solution.py:264
  72.3 5.0 %all-to-all-start = ((bf16[8,8,32,128]{3,2,1,0:T(8,128)(2,1)}), bf16[8,8,32,128]{3,2,1,0:T(8,128)(2,1)}, u32[]{:S(2)}, u32[]{:S(2)}) async-start(bf16[8,8,32,128]{3,2,1,0:T(8,128)(2,1)} %get-tuple-element.38), calls=%async_computation | async-start | bytes 1048576 | tf_op jit(solution)/shard_map/all_to_all | solution.py:437
  77.4 0.1 subtract_convert_fusion.refs_1_
  77.5 3.0 %collective-permute-start.11 = (bf16[32,8192]{1,0:T(8,128)(2,1)S(1)}, bf16[32,8192]{1,0:T(8,128)(2,1)S(1)}, u32[]{:S(2)}, u32[]{:S(2)}) collective-permute-start(bf16[32,8192]{1,0:T(8,128)(2,1)S(1)} %subtract_convert_fusion.refs_1_), channel_id=1, source_target_pairs={{0,1},{1,0},{2,3},{3,2},{4,5},{5,4},{6,7},{7,6},{8,9},{9,8},{10,11... | collective-permute-start | bytes 1572872 | tf_op jit(solution)/shard_map/ppermute | solution.py:276
  80.4 0.1 copy.40
  80.6 4.0 %all-to-all-done.blocks = bf16[8,8,32,128]{3,2,1,0:T(8,128)(2,1)} async-done(((bf16[8,8,32,128]{3,2,1,0:T(8,128)(2,1)}), bf16[8,8,32,128]{3,2,1,0:T(8,128)(2,1)}, u32[]{:S(2)}, u32[]{:S(2)}) %all-to-all-start) | async-done | bytes 524320 | tf_op jit(solution)/shard_map/all_to_all | solution.py:437
  84.6 2.3 %shard_map.90 = (bf16[8,32,128]{2,1,0:T(8,128)(2,1)S(1)}, bf16[8,32,256]{2,1,0:T(8,128)(2,1)}) custom-call(s32[4]{0:T(128)} %pad_add_fusion.place, bf16[8,8,32,128]{3,2,1,0:T(8,128)(2,1)} %all-to-all-done.blocks, bf16[1024,256]{1,0:T(8,128)(2,1)} %bitcast.20.q_own, bf16[1024,256]{1,0:T(8,128)(2,1)} %collective-permute-done.10.q_other), custom_call_target="tpu_custom_call" | custom-call | tf_op jit(solution)/shard_map/pallas_call | solution.py:215
  86.9 3.4 %all-to-all-start.1 = ((bf16[8,32,256]{2,1,0:T(8,128)(2,1)}), bf16[8,32,256]{2,1,0:T(8,128)(2,1)S(1)}, u32[]{:S(2)}, u32[]{:S(2)}) async-start(bf16[8,32,256]{2,1,0:T(8,128)(2,1)} %get-tuple-element.39), calls=%async_computation.1 | async-start | bytes 262144 | tf_op jit(solution)/shard_map/all_to_all | solution.py:439
  90.3 0.1 constant_dynamic-slice_fusion
  90.4 0.7 copy.46
  91.1 4.4 %all-to-all-done.1.terms = bf16[8,32,256]{2,1,0:T(8,128)(2,1)S(1)} async-done(((bf16[8,32,256]{2,1,0:T(8,128)(2,1)}), bf16[8,32,256]{2,1,0:T(8,128)(2,1)S(1)}, u32[]{:S(2)}, u32[]{:S(2)}) %all-to-all-start.1) | async-done | bytes 131104 | tf_op jit(solution)/shard_map/all_to_all | solution.py:439
  95.5 0.7 copy-done.12
  96.1 1.7 shard_map.91
  97.8 15.6 %all_to_all.20 = bf16[8,4,32,128]{3,2,1,0:T(8,128)(2,1)S(1)} all-to-all(bf16[8,4,32,128]{3,2,1,0:T(8,128)(2,1)} %shard_map.91), channel_id=1, replica_groups=mesh['x'=4,'ylo'=2,'z'=4,'yhi'=2,'core'=2] {'z','yhi'}, dimensions={0} | all-to-all | bytes 524288 | tf_op jit(solution)/shard_map/all_to_all | solution.py:441
  113.4 3.7 %collective-permute-start.12 = (bf16[4,256,128]{2,1,0:T(8,128)(2,1)S(1)}, bf16[4,256,128]{2,1,0:T(8,128)(2,1)S(1)}, u32[]{:S(2)}, u32[]{:S(2)}) collective-permute-start(bf16[4,256,128]{2,1,0:T(8,128)(2,1)S(1)} %bitcast.79), channel_id=1, source_target_pairs={{0,1},{1,0},{2,3},{3,2},{4,5},{5,4},{6,7},{7,6},{8,9},{9,8},{10,11... | collective-permute-start | bytes 786440 | tf_op jit(solution)/shard_map/ppermute | solution.py:276
  117.2 1.2 collective-permute-done.12.other_ref
  118.3 3.6 %shard_map.92 = bf16[64,256,128]{2,1,0:T(8,128)(2,1)S(1)} custom-call(bf16[4,256,128]{2,1,0:T(8,128)(2,1)S(1)} %bitcast.80, bf16[4,256,128]{2,1,0:T(8,128)(2,1)S(1)} %collective-permute-done.12.other_ref), custom_call_target="tpu_custom_call" | custom-call | tf_op jit(solution)/shard_map/pallas_call | solution.py:66
  122.0 56.1 %all_to_all.21 = bf16[64,256,128]{2,1,0:T(8,128)(2,1)} all-to-all(bf16[64,256,128]{2,1,0:T(8,128)(2,1)S(1)} %shard_map.92), channel_id=1, replica_groups=mesh['x'=4,'ylo'=2,'z'=4,'yhi'=2,'core'=2] {'x','ylo','z','yhi'}, dimensions={0} | all-to-all | bytes 8388608 | tf_op jit(solution)/shard_map/all_to_all | solution.py:446
  178.1 2.0 %collective-permute-start.13 = (bf16[64,256,128]{2,1,0:T(8,128)(2,1)}, bf16[64,256,128]{2,1,0:T(8,128)(2,1)}, u32[]{:S(2)}, u32[]{:S(2)}) collective-permute-start(bf16[64,256,128]{2,1,0:T(8,128)(2,1)} %all_to_all.21), channel_id=1, source_target_pairs={{0,1},{1,0},{2,3},{3,2},{4,5},{5,4},{6,7},{7,6},{8,9},{9,8},{10,11... | collective-permute-start | bytes 12582920 | tf_op jit(solution)/shard_map/ppermute | solution.py:276
  180.1 7.6 %shard_map.93 = (bf16[8,2,32,8192]{3,2,1,0:T(8,128)(2,1)}, f32[32,8192]{1,0:T(8,128)}, f32[32,8192]{1,0:T(8,128)}, f32[32,8192]{1,0:T(8,128)}) custom-call(s32[4]{0:T(128)} %pad_add_fusion.place, bf16[8,8,256,128]{3,2,1,0:T(8,128)(2,1)} %bitcast.26.refs_0_, bf16[32,8192]{1,0:T(8,128)(2,1)} %copy-done.7, f32[32,8192]{1,0:T(8,128)} %get-tuple-element.43.refs_2_, ...), custom_call_target="tpu_custom_call" | custom-call | tf_op jit(solution)/shard_map/pallas_call | solution.py:138
  187.8 4.6 %shard_map.94 = bf16[8,2,32,8192]{3,2,1,0:T(8,128)(2,1)} custom-call(s32[4]{0:T(128)} %pad_add_fusion.place, bf16[8,8,256,128]{3,2,1,0:T(8,128)(2,1)} %bitcast.25.moved, bf16[32,8192]{1,0:T(8,128)(2,1)} %copy-done.11, bf16[8,2,32,8192]{3,2,1,0:T(8,128)(2,1)} %get-tuple-element.44._), custom_call_target="tpu_custom_call", output_to_operand_aliasing={{}: (3, {})} | custom-call | tf_op jit(solution)/shard_map/pallas_call | solution.py:179
  (44 shorter events, 0.3 us)
Async XLA Ops:
  0.6 9.5 %copy-start = (f32[512,256]{1,0:T(8,128)S(1)}, f32[512,256]{1,0:T(8,128)}, u32[]{:S(2)}) copy-start(f32[512,256]{1,0:T(8,128)} %param.9) | copy-start | bytes 1572868
  4.9 5.9 %collective-permute-start.1 = (bf16[4,2,32,4096]{3,2,1,0:T(8,128)(2,1)}, bf16[4,2,32,4096]{3,2,1,0:T(8,128)(2,1)}, u32[]{:S(2)}, u32[]{:S(2)}) collective-permute-start(bf16[4,2,32,4096]{3,2,1,0:T(8,128)(2,1)} %shard_map.84), channel_id=1, source_target_pairs={{0,1},{1,0},{2,3},{3,2},{4,5},{5,4},{6,7},{7,6},{8,9},{9,8},{10,11... | collective-permute-start | bytes 6291464 | tf_op jit(solution)/shard_map/ppermute | solution.py:276
  10.0 11.5 %collective-permute-start = (bf16[4,2,32,4096]{3,2,1,0:T(8,128)(2,1)}, bf16[4,2,32,4096]{3,2,1,0:T(8,128)(2,1)}, u32[]{:S(2)}, u32[]{:S(2)}) collective-permute-start(bf16[4,2,32,4096]{3,2,1,0:T(8,128)(2,1)} %shard_map.85), channel_id=1, source_target_pairs={{0,1},{1,0},{2,3},{3,2},{4,5},{5,4},{6,7},{7,6},{8,9},{9,8},{10,11... | collective-permute-start | bytes 6291464 | tf_op jit(solution)/shard_map/ppermute | solution.py:276
  14.9 0.8 copy-start.4
  15.7 17.5 %collective-permute-start.2 = (bf16[64,4608]{1,0:T(8,128)(2,1)}, bf16[64,4608]{1,0:T(8,128)(2,1)}, u32[]{:S(2)}, u32[]{:S(2)}) collective-permute-start(bf16[64,4608]{1,0:T(8,128)(2,1)} %get-tuple-element.30), channel_id=1, source_target_pairs={{0,4},{4,8},{8,12},{12,0},{1,5},{5,9},{9,13},{13,1},{2,6},{6,10},{... | collective-permute-start | bytes 1769480 | tf_op jit(solution)/shard_map/ppermute | solution.py:280
  17.4 29.2 %collective-permute-start.3 = (bf16[64,4608]{1,0:T(8,128)(2,1)}, bf16[64,4608]{1,0:T(8,128)(2,1)}, u32[]{:S(2)}, u32[]{:S(2)}) collective-permute-start(bf16[64,4608]{1,0:T(8,128)(2,1)} %get-tuple-element.31), channel_id=1, source_target_pairs={{0,8},{4,12},{8,0},{12,4},{1,9},{5,13},{9,1},{13,5},{2,10},{6,14},... | collective-permute-start | bytes 1769480 | tf_op jit(solution)/shard_map/ppermute | solution.py:280
  20.7 25.9 %collective-permute-start.4 = (bf16[64,4608]{1,0:T(8,128)(2,1)S(1)}, bf16[64,4608]{1,0:T(8,128)(2,1)}, u32[]{:S(2)}, u32[]{:S(2)}) collective-permute-start(bf16[64,4608]{1,0:T(8,128)(2,1)S(1)} %get-tuple-element.32), channel_id=1, source_target_pairs={{0,12},{4,0},{8,4},{12,8},{1,13},{5,1},{9,5},{13,9},{2,14},{6,2},{... | collective-permute-start | bytes 1769480 | tf_op jit(solution)/shard_map/ppermute | solution.py:280
  24.5 1.0 copy-start.1
  25.5 1.0 copy-start.6
  26.4 25.2 %copy-start.2 = (bf16[4,32,4096]{2,1,0:T(8,128)(2,1)S(1)}, bf16[4,32,4096]{2,1,0:T(8,128)(2,1)}, u32[]{:S(2)}) copy-start(bf16[4,32,4096]{2,1,0:T(8,128)(2,1)} %copy-done.1) | copy-start | bytes 3145732
  26.4 25.2 %collective-permute-start.6 = (bf16[4,32,4096]{2,1,0:T(8,128)(2,1)}, bf16[4,32,4096]{2,1,0:T(8,128)(2,1)}, u32[]{:S(2)}, u32[]{:S(2)}) collective-permute-start(bf16[4,32,4096]{2,1,0:T(8,128)(2,1)} %copy-done.6), channel_id=1, source_target_pairs={{0,2},{2,0},{1,3},{3,1},{4,6},{6,4},{5,7},{7,5},{8,10},{10,8},{9,1... | collective-permute-start | bytes 3145736 | tf_op jit(solution)/shard_map/ppermute | solution.py:405
  48.5 16.0 %copy-start.3 = (f32[32,4096]{1,0:T(8,128)}, f32[32,4096]{1,0:T(8,128)S(1)}, u32[]{:S(2)}) copy-start(f32[32,4096]{1,0:T(8,128)S(1)} %get-tuple-element.33.left) | copy-start | bytes 1572868
  48.5 14.7 %collective-permute-start.5 = (bf16[32,8192]{1,0:T(8,128)(2,1)S(1)}, bf16[32,8192]{1,0:T(8,128)(2,1)S(1)}, u32[]{:S(2)}, u32[]{:S(2)}) collective-permute-start(bf16[32,8192]{1,0:T(8,128)(2,1)S(1)} %get-tuple-element.34), channel_id=1, source_target_pairs={{0,2},{2,0},{1,3},{3,1},{4,6},{6,4},{5,7},{7,5},{8,10},{10,8},{9,1... | collective-permute-start | bytes 1572872 | tf_op jit(solution)/shard_map/ppermute | solution.py:410
  54.1 14.3 %collective-permute-start.9 = (bf16[32,4096]{1,0:T(8,128)(2,1)}, bf16[32,4096]{1,0:T(8,128)(2,1)S(1)}, u32[]{:S(2)}, u32[]{:S(2)}) collective-permute-start(bf16[32,4096]{1,0:T(8,128)(2,1)} %get-tuple-element.48), channel_id=1, source_target_pairs={{0,12},{4,0},{8,4},{12,8},{1,13},{5,1},{9,5},{13,9},{2,14},{6,2},{... | collective-permute-start | bytes 786440 | tf_op jit(solution)/shard_map/ppermute | solution.py:280
  56.7 11.7 %collective-permute-start.8 = (bf16[32,4096]{1,0:T(8,128)(2,1)}, bf16[32,4096]{1,0:T(8,128)(2,1)}, u32[]{:S(2)}, u32[]{:S(2)}) collective-permute-start(bf16[32,4096]{1,0:T(8,128)(2,1)} %get-tuple-element.49), channel_id=1, source_target_pairs={{0,4},{4,8},{8,12},{12,0},{1,5},{5,9},{9,13},{13,1},{2,6},{6,10},{... | collective-permute-start | bytes 786440 | tf_op jit(solution)/shard_map/ppermute | solution.py:280
  56.7 12.0 %collective-permute-start.7 = (bf16[32,4096]{1,0:T(8,128)(2,1)}, bf16[32,4096]{1,0:T(8,128)(2,1)}, u32[]{:S(2)}, u32[]{:S(2)}) collective-permute-start(bf16[32,4096]{1,0:T(8,128)(2,1)} %get-tuple-element.50), channel_id=1, source_target_pairs={{0,8},{4,12},{8,0},{12,4},{1,9},{5,13},{9,1},{13,5},{2,10},{6,14},... | collective-permute-start | bytes 786440 | tf_op jit(solution)/shard_map/ppermute | solution.py:280
  63.2 0.8 copy-start.10
  65.6 11.8 %copy-start.8 = (f32[32,8192]{1,0:T(8,128)S(1)}, f32[32,8192]{1,0:T(8,128)}, u32[]{:S(2)}) copy-start(f32[32,8192]{1,0:T(8,128)} %refs_4_.1) | copy-start | bytes 3145732
  65.6 11.8 %copy-start.9 = (f32[32,8192]{1,0:T(8,128)S(1)}, f32[32,8192]{1,0:T(8,128)}, u32[]{:S(2)}) copy-start(f32[32,8192]{1,0:T(8,128)} %refs_3_.1) | copy-start | bytes 3145732
  66.6 14.0 %collective-permute-start.10 = (bf16[1024,256]{1,0:T(8,128)(2,1)}, bf16[1024,256]{1,0:T(8,128)(2,1)}, u32[]{:S(2)}, u32[]{:S(2)}) collective-permute-start(bf16[1024,256]{1,0:T(8,128)(2,1)} %bitcast.20.q_own), channel_id=1, source_target_pairs={{0,1},{1,0},{2,3},{3,2},{4,5},{5,4},{6,7},{7,6},{8,9},{9,8},{10,11... | collective-permute-start | bytes 1572872 | tf_op jit(solution)/shard_map/ppermute | solution.py:276
  68.3 0.7 copy-start.13
  72.3 12.3 %all-to-all-start = ((bf16[8,8,32,128]{3,2,1,0:T(8,128)(2,1)}), bf16[8,8,32,128]{3,2,1,0:T(8,128)(2,1)}, u32[]{:S(2)}, u32[]{:S(2)}) async-start(bf16[8,8,32,128]{3,2,1,0:T(8,128)(2,1)} %get-tuple-element.38), calls=%async_computation | async-start | bytes 1048576 | tf_op jit(solution)/shard_map/all_to_all | solution.py:437
  77.5 44.5 %copy-start.7 = (bf16[32,8192]{1,0:T(8,128)(2,1)}, bf16[32,8192]{1,0:T(8,128)(2,1)S(1)}, u32[]{:S(2)}) copy-start(bf16[32,8192]{1,0:T(8,128)(2,1)S(1)} %subtract_convert_fusion.refs_1_) | copy-start | bytes 1572868
  77.5 35.9 %collective-permute-start.11 = (bf16[32,8192]{1,0:T(8,128)(2,1)S(1)}, bf16[32,8192]{1,0:T(8,128)(2,1)S(1)}, u32[]{:S(2)}, u32[]{:S(2)}) collective-permute-start(bf16[32,8192]{1,0:T(8,128)(2,1)S(1)} %subtract_convert_fusion.refs_1_), channel_id=1, source_target_pairs={{0,1},{1,0},{2,3},{3,2},{4,5},{5,4},{6,7},{7,6},{8,9},{9,8},{10,11... | collective-permute-start | bytes 1572872 | tf_op jit(solution)/shard_map/ppermute | solution.py:276
  86.9 8.6 %copy-start.5 = (bf16[8,32,128]{2,1,0:T(8,128)(2,1)}, bf16[8,32,128]{2,1,0:T(8,128)(2,1)S(1)}, u32[]{:S(2)}) copy-start(bf16[8,32,128]{2,1,0:T(8,128)(2,1)S(1)} %get-tuple-element.40.mean) | copy-start | bytes 196612
  86.9 8.6 %all-to-all-start.1 = ((bf16[8,32,256]{2,1,0:T(8,128)(2,1)}), bf16[8,32,256]{2,1,0:T(8,128)(2,1)S(1)}, u32[]{:S(2)}, u32[]{:S(2)}) async-start(bf16[8,32,256]{2,1,0:T(8,128)(2,1)} %get-tuple-element.39), calls=%async_computation.1 | async-start | bytes 262144 | tf_op jit(solution)/shard_map/all_to_all | solution.py:439
  95.5 0.7 copy-start.12
  113.4 64.7 %copy-start.11 = (bf16[32,8192]{1,0:T(8,128)(2,1)}, bf16[32,8192]{1,0:T(8,128)(2,1)S(1)}, u32[]{:S(2)}) copy-start(bf16[32,8192]{1,0:T(8,128)(2,1)S(1)} %collective-permute-done.11.before) | copy-start | bytes 1572868
  113.4 4.9 %collective-permute-start.12 = (bf16[4,256,128]{2,1,0:T(8,128)(2,1)S(1)}, bf16[4,256,128]{2,1,0:T(8,128)(2,1)S(1)}, u32[]{:S(2)}, u32[]{:S(2)}) collective-permute-start(bf16[4,256,128]{2,1,0:T(8,128)(2,1)S(1)} %bitcast.79), channel_id=1, source_target_pairs={{0,1},{1,0},{2,3},{3,2},{4,5},{5,4},{6,7},{7,6},{8,9},{9,8},{10,11... | collective-permute-start | bytes 786440 | tf_op jit(solution)/shard_map/ppermute | solution.py:276
  178.1 9.6 %collective-permute-start.13 = (bf16[64,256,128]{2,1,0:T(8,128)(2,1)}, bf16[64,256,128]{2,1,0:T(8,128)(2,1)}, u32[]{:S(2)}, u32[]{:S(2)}) collective-permute-start(bf16[64,256,128]{2,1,0:T(8,128)(2,1)} %all_to_all.21), channel_id=1, source_target_pairs={{0,1},{1,0},{2,3},{3,2},{4,5},{5,4},{6,7},{7,6},{8,9},{9,8},{10,11... | collective-permute-start | bytes 12582920 | tf_op jit(solution)/shard_map/ppermute | solution.py:276

commit v5 on v4

--- a/solution.py
+++ b/solution.py
@@ -303,24 +303,26 @@
     ]
 
 
-def theirs_kernel(half, place, parts, out, sems):
-    copies = block_copies(place, parts, out, sems, 1, half)
-    for copy in copies:
-        copy.start()
-    for copy in copies:
-        copy.wait()
+def theirs_kernel(half, place, parts, out, held, in_sems, out_sems):
+    loads = block_copies(place, parts, held, in_sems, 1, half)
+    stores = [pltpu.make_async_copy(held.at[k, j], out.at[k, j], out_sems.at[k, j]) for k, j in BLOCKS]
+    for load in loads:
+        load.start()
+    for load, store in zip(loads, stores):
+        load.wait()
+        store.start()
+    for store in stores:
+        store.wait()
 
 
 def theirs(place, parts, half):
+    shape = (4, 2, 32, WIDE)
     return pl.pallas_call(
         functools.partial(theirs_kernel, half),
-        in_specs=[
-            pl.BlockSpec(memory_space=pltpu.SMEM),
-            pl.BlockSpec(memory_space=pl.ANY),
-        ],
-        out_specs=pl.BlockSpec(memory_space=pltpu.VMEM),
-        out_shape=pltpu.VMEM((4, 2, 32, WIDE), BF16),
-        scratch_shapes=[pltpu.SemaphoreType.DMA((4, 2))],
+        in_specs=[SMEM, ANYWHERE],
+        out_specs=ANYWHERE,
+        out_shape=jax.ShapeDtypeStruct(shape, BF16),
+        scratch_shapes=[pltpu.VMEM(shape, BF16)] + [pltpu.SemaphoreType.DMA((4, 2))] * 2,
     )(place, parts)
 
 
@@ -342,28 +344,41 @@
         yield k, j, add(ours[k, j], theirs[k, j])
 
 
-def right_kernel(place, parts, received, keep, send, *scratch):
+def right_kernel(place, parts, received, keep, send, made, out_sems, *scratch):
+    stores = []
     for k, j, total in pair_sums(1, place, parts, received, *scratch):
-        (send if j else keep)[k] = total
-
-
-def left_kernel(place, parts, received, piece, keep, up, far, down, *scratch):
-    outs = (keep, up, far, down)
-    for out in outs[1:]:
-        out[:, WIDE:] = piece[...]
+        made[k, j] = total
+        stores.append(pltpu.make_async_copy(made.at[k, j], (send if j else keep).at[k], out_sems.at[k, j]))
+        stores[-1].start()
+    for store in stores:
+        store.wait()
+
+
+def left_kernel(place, parts, received, piece, keep, up, far, down, made, out_sems, *scratch):
+    outs, stores = (keep, up, far, down), []
     for k, j, total in pair_sums(0, place, parts, received, *scratch):
-        outs[k][32 * j : 32 * j + 32, :WIDE] = total
-
-
-def pair_call(kernel, shapes, place, parts, received, *rest):
-    vmem = pl.BlockSpec(memory_space=pltpu.VMEM)
-    anywhere = pl.BlockSpec(memory_space=pl.ANY)
+        made[k, 32 * j : 32 * j + 32, :WIDE] = total
+        if j == 0:
+            made[k, :, WIDE:] = piece[...]
+            continue
+        view = made.at[k] if k else made.at[k, :, pl.ds(0, WIDE)]
+        stores.append(pltpu.make_async_copy(view, outs[k], out_sems.at[k, 0]))
+        stores[-1].start()
+    for store in stores:
+        store.wait()
+
+
+def pair_call(kernel, shapes, made, place, parts, received, *rest):
+    vmem = pl.BlockSpec(memory_space=pltpu.VMEM)
     return pl.pallas_call(
         kernel,
-        in_specs=[pl.BlockSpec(memory_space=pltpu.SMEM), anywhere, anywhere] + [vmem] * len(rest),
-        out_specs=[vmem] * len(shapes),
-        out_shape=[pltpu.VMEM(shape, BF16) for shape in shapes],
-        scratch_shapes=[pltpu.VMEM((4, 2, 32, WIDE), BF16)] * 2 + [pltpu.SemaphoreType.DMA((4, 2))] * 2,
+        in_specs=[SMEM, ANYWHERE, ANYWHERE] + [vmem] * len(rest),
+        out_specs=[ANYWHERE] * len(shapes),
+        out_shape=[jax.ShapeDtypeStruct(shape, BF16) for shape in shapes],
+        scratch_shapes=[pltpu.VMEM(made, BF16), pltpu.SemaphoreType.DMA((4, 2))]
+        + [pltpu.VMEM((4, 2, 32, WIDE), BF16)] * 2
+        + [pltpu.SemaphoreType.DMA((4, 2))] * 2,
+        compiler_params=pltpu.CompilerParams(vmem_limit_bytes=VMEM),
     )(place, parts, received, *rest)
 
 
@@ -399,9 +414,13 @@
     left_out, parts_later = lax.optimization_barrier((theirs(place, parts, 0), parts))
     left_in, right_in = swap_cores(left_out), swap_cores(theirs(place, parts_later, 1))
     shapes = [(64, WIDE)] + [(64, WIDE + 512)] * 3
-    left, up, far, down = pair_call(left_kernel, shapes, place, parts, left_in, piece)
+    left, up, far, down = pair_call(
+        left_kernel, shapes, (4, 64, WIDE + 512), place, parts, left_in, piece
+    )
     right_in, left = lax.optimization_barrier((right_in, left))
-    right, across = pair_call(right_kernel, [(4, 32, WIDE)] * 2, place, parts, right_in)
+    right, across = pair_call(
+        right_kernel, [(4, 32, WIDE)] * 2, (4, 2, 32, WIDE), place, parts, right_in
+    )
     across = lax.ppermute(across, "yhi", SWAP)
     far, up, down = along_z(far, 2), along_z(up, 1), along_z(down, 3)
     sums = [right[k].astype(F32) + across[k].astype(F32) for k in range(4)]

time: 193 us -> 192 us (level)
    unnamed x45 -> x43, local copies, waits for them, and re-layouts: 4.75 us -> 3.65 us
  transfers between devices with their start and end apart: 16 -> 16, of which waited for: 7 -> 8; matrix products, arithmetic and copies ran while one was open for 4% -> 4% of each run, Pallas kernels for 14% -> 15%
where the time goes in v5:
time: 192 us; the launch traced here: 191 us
  blocking collectives  71.3 us (37%)
  Pallas kernels  39.2 us (20%)
  starting transfers between devices  34.8 us (18%)
  waiting for transfers between devices  33.8 us (18%)
  local copies, waits for them, and re-layouts  6.86 us (4%)
  other arithmetic  3.85 us (2%)
    all_to_all x1, blocking collectives, on_device(): moved_own = lax.all_to_all(factors(own, other), CHIPS, 0, 0, tiled=True)  56.1 us
    ppermute x6, waiting for transfers between devices, along_z(): return lax.ppermute(value, 'z', [(at, (at + step) % 4) for at in range(4)])  17 us
    all_to_all x1, blocking collectives, on_device(): own = lax.all_to_all(gathered(terms, mean, columns), ZY, 0, 0, tiled=True)  15.1 us
    ppermute x6, starting transfers between devices, swap_cores(): return lax.ppermute(value, 'core', SWAP)  11.2 us
    ppermute x6, starting transfers between devices, along_z(): return lax.ppermute(value, 'z', [(at, (at + step) % 4) for at in range(4)])  9.2 us
    pallas_call x2, Pallas kernels, pair_call(): pl.pallas_call(kernel, in_specs=[SMEM, ANYWHERE, ANYWHERE] + [vmem] * len...  8.13 us
    pallas_call x1, Pallas kernels, own_rows(): pl.pallas_call(own_kernel, in_specs=[SMEM] + [ANYWHERE] * 5, out_specs=[A...  7.59 us
    ppermute x1, waiting for transfers between devices, summed_rows(): back = lax.ppermute(sent, 'yhi', SWAP)  6.29 us
  transfers between devices with their start and end apart: 16, of which 8 were waited for; matrix products, arithmetic and copies ran while one was open for 4% of the time, Pallas kernels for 15%

profile of v5, /device:TPU:1, one launch (start us, length us, event | category | flops | bytes accessed | tf_op | source)
XLA Modules:
  0.0 191.0 jit_solution(11433259291520192716)
XLA Ops:
  0.6 0.0 copy-start
  0.7 0.6 pad_add_fusion.place
  1.3 3.1 %shard_map.84 = bf16[4,2,32,4096]{3,2,1,0:T(8,128)(2,1)} custom-call(s32[4]{0:T(128)} %pad_add_fusion.place, bf16[16,32,8192]{2,1,0:T(8,128)(2,1)} %bitcast.81), custom_call_target="tpu_custom_call" | custom-call | tf_op jit(solution)/shard_map/pallas_call | solution.py:320
  4.3 1.5 collective-permute-start.1
  5.8 3.1 %shard_map.85 = bf16[4,2,32,4096]{3,2,1,0:T(8,128)(2,1)} custom-call(s32[4]{0:T(128)} %pad_add_fusion.place, bf16[16,32,8192]{2,1,0:T(8,128)(2,1)} %bitcast.82), custom_call_target="tpu_custom_call" | custom-call | tf_op jit(solution)/shard_map/pallas_call | solution.py:320
  9.0 0.1 collective-permute-start
  9.1 0.6 pad_maximum_fusion.1.piece
  9.8 0.2 collective-permute-done.1.received
  10.0 4.1 %shard_map.86 = (bf16[64,4096]{1,0:T(8,128)(2,1)}, bf16[64,4608]{1,0:T(8,128)(2,1)}, bf16[64,4608]{1,0:T(8,128)(2,1)}, bf16[64,4608]{1,0:T(8,128)(2,1)}) custom-call(s32[4]{0:T(128)} %pad_add_fusion.place, bf16[16,32,8192]{2,1,0:T(8,128)(2,1)} %bitcast.83, bf16[4,2,32,4096]{3,2,1,0:T(8,128)(2,1)} %collective-permute-done.1.received, ...), custom_call_target="tpu_custom_call" | custom-call | tf_op jit(solution)/shard_map/pallas_call | solution.py:373
  14.1 1.8 collective-permute-start.2
  15.9 3.3 %collective-permute-start.3 = (bf16[64,4608]{1,0:T(8,128)(2,1)}, bf16[64,4608]{1,0:T(8,128)(2,1)}, u32[]{:S(2)}, u32[]{:S(2)}) collective-permute-start(bf16[64,4608]{1,0:T(8,128)(2,1)} %get-tuple-element.31), channel_id=1, source_target_pairs={{0,8},{4,12},{8,0},{12,4},{1,9},{5,13},{9,1},{13,5},{2,10},{6,14},... | collective-permute-start | bytes 1769480 | tf_op jit(solution)/shard_map/ppermute | solution.py:280
  19.2 0.7 collective-permute-start.4
  19.9 0.0 collective-permute-done.received
  19.9 1.3 copy-done.7
  21.2 4.0 %shard_map.88 = (bf16[4,32,4096]{2,1,0:T(8,128)(2,1)}, bf16[4,32,4096]{2,1,0:T(8,128)(2,1)}) custom-call(s32[4]{0:T(128)} %pad_add_fusion.place, bf16[16,32,8192]{2,1,0:T(8,128)(2,1)} %bitcast.84, bf16[4,2,32,4096]{3,2,1,0:T(8,128)(2,1)} %copy-done.7), custom_call_target="tpu_custom_call" | custom-call | tf_op jit(solution)/shard_map/pallas_call | solution.py:373
  25.3 0.0 copy-start.8
  25.3 3.0 %collective-permute-start.6 = (bf16[4,32,4096]{2,1,0:T(8,128)(2,1)}, bf16[4,32,4096]{2,1,0:T(8,128)(2,1)}, u32[]{:S(2)}, u32[]{:S(2)}) collective-permute-start(bf16[4,32,4096]{2,1,0:T(8,128)(2,1)} %get-tuple-element.37), channel_id=1, source_target_pairs={{0,2},{2,0},{1,3},{3,1},{4,6},{6,4},{5,7},{7,5},{8,10},{10,8},{9,1... | collective-permute-start | bytes 3145736 | tf_op jit(solution)/shard_map/ppermute | solution.py:424
  28.3 3.5 %collective-permute-done.2.up = bf16[64,4608]{1,0:T(8,128)(2,1)S(1)} collective-permute-done((bf16[64,4608]{1,0:T(8,128)(2,1)}, bf16[64,4608]{1,0:T(8,128)(2,1)S(1)}, u32[]{:S(2)}, u32[]{:S(2)}) %collective-permute-start.2) | collective-permute-done | bytes 589856 | tf_op jit(solution)/shard_map/ppermute | solution.py:280
  31.7 13.5 %collective-permute-done.3.far = bf16[64,4608]{1,0:T(8,128)(2,1)} collective-permute-done((bf16[64,4608]{1,0:T(8,128)(2,1)}, bf16[64,4608]{1,0:T(8,128)(2,1)}, u32[]{:S(2)}, u32[]{:S(2)}) %collective-permute-start.3) | collective-permute-done | bytes 589856 | tf_op jit(solution)/shard_map/ppermute | solution.py:280
  45.2 0.0 collective-permute-done.4.down
  45.2 1.8 shard_map.87
  47.1 0.0 copy-start.1
  47.1 3.0 %collective-permute-start.5 = (bf16[32,8192]{1,0:T(8,128)(2,1)S(1)}, bf16[32,8192]{1,0:T(8,128)(2,1)S(1)}, u32[]{:S(2)}, u32[]{:S(2)}) collective-permute-start(bf16[32,8192]{1,0:T(8,128)(2,1)S(1)} %get-tuple-element.34), channel_id=1, source_target_pairs={{0,2},{2,0},{1,3},{3,1},{4,6},{6,4},{5,7},{7,5},{8,10},{10,8},{9,1... | collective-permute-start | bytes 1572872 | tf_op jit(solution)/shard_map/ppermute | solution.py:429
  50.2 0.4 collective-permute-done.6
  50.6 2.4 %fusion.2 = (bf16[32,4096]{1,0:T(8,128)(2,1)}, bf16[32,4096]{1,0:T(8,128)(2,1)}, bf16[32,4096]{1,0:T(8,128)(2,1)}, f32[32,4096]{1,0:T(8,128)}) fusion(bf16[4,32,4096]{2,1,0:T(8,128)(2,1)} %collective-permute-done.6, bf16[4,32,4096]{2,1,0:T(8,128)(2,1)S(1)} %copy-done.8), kind=kLoop, calls=%fused_computation.9 | loop fusion | flops 1966080 | bytes 3407872 | tf_op jit(solution)/shard_map/convert_element_type | solution.py:427
  53.0 2.2 %collective-permute-start.9 = (bf16[32,4096]{1,0:T(8,128)(2,1)}, bf16[32,4096]{1,0:T(8,128)(2,1)S(1)}, u32[]{:S(2)}, u32[]{:S(2)}) collective-permute-start(bf16[32,4096]{1,0:T(8,128)(2,1)} %get-tuple-element.48), channel_id=1, source_target_pairs={{0,12},{4,0},{8,4},{12,8},{1,13},{5,1},{9,5},{13,9},{2,14},{6,2},{... | collective-permute-start | bytes 786440 | tf_op jit(solution)/shard_map/ppermute | solution.py:280
  55.2 0.0 collective-permute-start.8
  55.2 1.2 collective-permute-start.7
  56.4 6.3 %collective-permute-done.5.back = bf16[32,8192]{1,0:T(8,128)(2,1)S(1)} collective-permute-done((bf16[32,8192]{1,0:T(8,128)(2,1)S(1)}, bf16[32,8192]{1,0:T(8,128)(2,1)S(1)}, u32[]{:S(2)}, u32[]{:S(2)}) %collective-permute-start.5) | collective-permute-done | bytes 524320 | tf_op jit(solution)/shard_map/ppermute | solution.py:429
  62.8 0.6 copy-done.6
  63.5 0.1 maximum_select_fusion
  63.5 0.4 select_n.47
  63.9 1.1 fusion.11
  65.0 0.0 copy-start.4
  65.0 0.0 copy-start.5
  65.2 0.1 pad_maximum_fusion
  65.2 0.8 copy.33
  66.1 1.2 collective-permute-start.10
  67.3 0.0 collective-permute-done.9.down
  67.3 0.0 collective-permute-done.8.up
  67.3 0.0 collective-permute-done.7.far
  67.3 0.7 copy-done.12
  68.0 3.3 %shard_map.89 = (f32[32,8192]{1,0:T(8,128)}, bf16[8,8,32,128]{3,2,1,0:T(8,128)(2,1)}) custom-call(f32[32,4096]{1,0:T(8,128)} %copy-done.1, bf16[32,8192]{1,0:T(8,128)(2,1)} %copy-done.6, f32[32,4096]{1,0:T(8,128)} %get-tuple-element.51.right, bf16[32,4096]{1,0:T(8,128)(2,1)} %collective-permute-done.7.far, bf16[32,4096]{1,0:T(8,128)(2,1)} %collective-permute-done.8.up, ...), custom_call_target="tpu_custom_call" | custom-call | tf_op jit(solution)/shard_map/pallas_call | solution.py:264
  71.2 5.0 %all-to-all-start = ((bf16[8,8,32,128]{3,2,1,0:T(8,128)(2,1)}), bf16[8,8,32,128]{3,2,1,0:T(8,128)(2,1)}, u32[]{:S(2)}, u32[]{:S(2)}) async-start(bf16[8,8,32,128]{3,2,1,0:T(8,128)(2,1)} %get-tuple-element.38), calls=%async_computation | async-start | bytes 1048576 | tf_op jit(solution)/shard_map/all_to_all | solution.py:456
  76.3 0.1 subtract_convert_fusion.refs_1_
  76.4 2.6 %collective-permute-start.11 = (bf16[32,8192]{1,0:T(8,128)(2,1)S(1)}, bf16[32,8192]{1,0:T(8,128)(2,1)S(1)}, u32[]{:S(2)}, u32[]{:S(2)}) collective-permute-start(bf16[32,8192]{1,0:T(8,128)(2,1)S(1)} %subtract_convert_fusion.refs_1_), channel_id=1, source_target_pairs={{0,1},{1,0},{2,3},{3,2},{4,5},{5,4},{6,7},{7,6},{8,9},{9,8},{10,11... | collective-permute-start | bytes 1572872 | tf_op jit(solution)/shard_map/ppermute | solution.py:276
  79.0 0.1 copy.40
  79.1 4.4 %all-to-all-done.blocks = bf16[8,8,32,128]{3,2,1,0:T(8,128)(2,1)} async-done(((bf16[8,8,32,128]{3,2,1,0:T(8,128)(2,1)}), bf16[8,8,32,128]{3,2,1,0:T(8,128)(2,1)}, u32[]{:S(2)}, u32[]{:S(2)}) %all-to-all-start) | async-done | bytes 524320 | tf_op jit(solution)/shard_map/all_to_all | solution.py:456
  83.5 2.3 %shard_map.90 = (bf16[8,32,128]{2,1,0:T(8,128)(2,1)S(1)}, bf16[8,32,256]{2,1,0:T(8,128)(2,1)}) custom-call(s32[4]{0:T(128)} %pad_add_fusion.place, bf16[8,8,32,128]{3,2,1,0:T(8,128)(2,1)} %all-to-all-done.blocks, bf16[1024,256]{1,0:T(8,128)(2,1)} %bitcast.20.q_own, bf16[1024,256]{1,0:T(8,128)(2,1)} %collective-permute-done.10.q_other), custom_call_target="tpu_custom_call" | custom-call | tf_op jit(solution)/shard_map/pallas_call | solution.py:215
  85.8 3.4 %all-to-all-start.1 = ((bf16[8,32,256]{2,1,0:T(8,128)(2,1)}), bf16[8,32,256]{2,1,0:T(8,128)(2,1)S(1)}, u32[]{:S(2)}, u32[]{:S(2)}) async-start(bf16[8,32,256]{2,1,0:T(8,128)(2,1)} %get-tuple-element.39), calls=%async_computation.1 | async-start | bytes 262144 | tf_op jit(solution)/shard_map/all_to_all | solution.py:458
  89.2 0.1 constant_dynamic-slice_fusion
  89.3 0.7 copy.46
  90.0 4.4 %all-to-all-done.1.terms = bf16[8,32,256]{2,1,0:T(8,128)(2,1)S(1)} async-done(((bf16[8,32,256]{2,1,0:T(8,128)(2,1)}), bf16[8,32,256]{2,1,0:T(8,128)(2,1)S(1)}, u32[]{:S(2)}, u32[]{:S(2)}) %all-to-all-start.1) | async-done | bytes 131104 | tf_op jit(solution)/shard_map/all_to_all | solution.py:458
  94.4 0.7 copy-done.11
  95.0 1.7 shard_map.91
  96.7 15.1 %all_to_all.20 = bf16[8,4,32,128]{3,2,1,0:T(8,128)(2,1)S(1)} all-to-all(bf16[8,4,32,128]{3,2,1,0:T(8,128)(2,1)} %shard_map.91), channel_id=1, replica_groups=mesh['x'=4,'ylo'=2,'z'=4,'yhi'=2,'core'=2] {'z','yhi'}, dimensions={0} | all-to-all | bytes 524288 | tf_op jit(solution)/shard_map/all_to_all | solution.py:460
  111.9 3.8 %collective-permute-start.12 = (bf16[4,256,128]{2,1,0:T(8,128)(2,1)S(1)}, bf16[4,256,128]{2,1,0:T(8,128)(2,1)S(1)}, u32[]{:S(2)}, u32[]{:S(2)}) collective-permute-start(bf16[4,256,128]{2,1,0:T(8,128)(2,1)S(1)} %bitcast.79), channel_id=1, source_target_pairs={{0,1},{1,0},{2,3},{3,2},{4,5},{5,4},{6,7},{7,6},{8,9},{9,8},{10,11... | collective-permute-start | bytes 786440 | tf_op jit(solution)/shard_map/ppermute | solution.py:276
  115.7 1.2 collective-permute-done.12.other_ref
  116.9 3.6 %shard_map.92 = bf16[64,256,128]{2,1,0:T(8,128)(2,1)S(1)} custom-call(bf16[4,256,128]{2,1,0:T(8,128)(2,1)S(1)} %bitcast.80, bf16[4,256,128]{2,1,0:T(8,128)(2,1)S(1)} %collective-permute-done.12.other_ref), custom_call_target="tpu_custom_call" | custom-call | tf_op jit(solution)/shard_map/pallas_call | solution.py:66
  120.5 56.1 %all_to_all.21 = bf16[64,256,128]{2,1,0:T(8,128)(2,1)} all-to-all(bf16[64,256,128]{2,1,0:T(8,128)(2,1)S(1)} %shard_map.92), channel_id=1, replica_groups=mesh['x'=4,'ylo'=2,'z'=4,'yhi'=2,'core'=2] {'x','ylo','z','yhi'}, dimensions={0} | all-to-all | bytes 8388608 | tf_op jit(solution)/shard_map/all_to_all | solution.py:465
  176.7 2.0 %collective-permute-start.13 = (bf16[64,256,128]{2,1,0:T(8,128)(2,1)}, bf16[64,256,128]{2,1,0:T(8,128)(2,1)}, u32[]{:S(2)}, u32[]{:S(2)}) collective-permute-start(bf16[64,256,128]{2,1,0:T(8,128)(2,1)} %all_to_all.21), channel_id=1, source_target_pairs={{0,1},{1,0},{2,3},{3,2},{4,5},{5,4},{6,7},{7,6},{8,9},{9,8},{10,11... | collective-permute-start | bytes 12582920 | tf_op jit(solution)/shard_map/ppermute | solution.py:276
  178.7 7.6 %shard_map.93 = (bf16[8,2,32,8192]{3,2,1,0:T(8,128)(2,1)}, f32[32,8192]{1,0:T(8,128)}, f32[32,8192]{1,0:T(8,128)}, f32[32,8192]{1,0:T(8,128)}) custom-call(s32[4]{0:T(128)} %pad_add_fusion.place, bf16[8,8,256,128]{3,2,1,0:T(8,128)(2,1)} %bitcast.26.refs_0_, bf16[32,8192]{1,0:T(8,128)(2,1)} %copy-done.3, f32[32,8192]{1,0:T(8,128)} %get-tuple-element.43.refs_2_, ...), custom_call_target="tpu_custom_call" | custom-call | tf_op jit(solution)/shard_map/pallas_call | solution.py:138
  186.3 0.0 collective-permute-done.13
  186.3 4.6 %shard_map.94 = bf16[8,2,32,8192]{3,2,1,0:T(8,128)(2,1)} custom-call(s32[4]{0:T(128)} %pad_add_fusion.place, bf16[8,8,256,128]{3,2,1,0:T(8,128)(2,1)} %bitcast.25.moved, bf16[32,8192]{1,0:T(8,128)(2,1)} %copy-done.10, bf16[8,2,32,8192]{3,2,1,0:T(8,128)(2,1)} %get-tuple-element.44._), custom_call_target="tpu_custom_call", output_to_operand_aliasing={{}: (3, {})} | custom-call | tf_op jit(solution)/shard_map/pallas_call | solution.py:179
  (42 shorter events, 0.3 us)
Async XLA Ops:
  0.6 8.4 %copy-start = (f32[512,256]{1,0:T(8,128)S(1)}, f32[512,256]{1,0:T(8,128)}, u32[]{:S(2)}) copy-start(f32[512,256]{1,0:T(8,128)} %param.9) | copy-start | bytes 1572868
  4.3 5.6 %collective-permute-start.1 = (bf16[4,2,32,4096]{3,2,1,0:T(8,128)(2,1)}, bf16[4,2,32,4096]{3,2,1,0:T(8,128)(2,1)}, u32[]{:S(2)}, u32[]{:S(2)}) collective-permute-start(bf16[4,2,32,4096]{3,2,1,0:T(8,128)(2,1)} %shard_map.84), channel_id=1, source_target_pairs={{0,1},{1,0},{2,3},{3,2},{4,5},{5,4},{6,7},{7,6},{8,9},{9,8},{10,11... | collective-permute-start | bytes 6291464 | tf_op jit(solution)/shard_map/ppermute | solution.py:276
  9.0 11.0 %collective-permute-start = (bf16[4,2,32,4096]{3,2,1,0:T(8,128)(2,1)}, bf16[4,2,32,4096]{3,2,1,0:T(8,128)(2,1)S(1)}, u32[]{:S(2)}, u32[]{:S(2)}) collective-permute-start(bf16[4,2,32,4096]{3,2,1,0:T(8,128)(2,1)} %shard_map.85), channel_id=1, source_target_pairs={{0,1},{1,0},{2,3},{3,2},{4,5},{5,4},{6,7},{7,6},{8,9},{9,8},{10,11... | collective-permute-start | bytes 6291464 | tf_op jit(solution)/shard_map/ppermute | solution.py:276
  14.1 17.6 %collective-permute-start.2 = (bf16[64,4608]{1,0:T(8,128)(2,1)}, bf16[64,4608]{1,0:T(8,128)(2,1)S(1)}, u32[]{:S(2)}, u32[]{:S(2)}) collective-permute-start(bf16[64,4608]{1,0:T(8,128)(2,1)} %get-tuple-element.30), channel_id=1, source_target_pairs={{0,4},{4,8},{8,12},{12,0},{1,5},{5,9},{9,13},{13,1},{2,6},{6,10},{... | collective-permute-start | bytes 1769480 | tf_op jit(solution)/shard_map/ppermute | solution.py:280
  15.9 29.3 %collective-permute-start.3 = (bf16[64,4608]{1,0:T(8,128)(2,1)}, bf16[64,4608]{1,0:T(8,128)(2,1)}, u32[]{:S(2)}, u32[]{:S(2)}) collective-permute-start(bf16[64,4608]{1,0:T(8,128)(2,1)} %get-tuple-element.31), channel_id=1, source_target_pairs={{0,8},{4,12},{8,0},{12,4},{1,9},{5,13},{9,1},{13,5},{2,10},{6,14},... | collective-permute-start | bytes 1769480 | tf_op jit(solution)/shard_map/ppermute | solution.py:280
  19.2 26.0 %collective-permute-start.4 = (bf16[64,4608]{1,0:T(8,128)(2,1)}, bf16[64,4608]{1,0:T(8,128)(2,1)}, u32[]{:S(2)}, u32[]{:S(2)}) collective-permute-start(bf16[64,4608]{1,0:T(8,128)(2,1)} %get-tuple-element.32), channel_id=1, source_target_pairs={{0,12},{4,0},{8,4},{12,8},{1,13},{5,1},{9,5},{13,9},{2,14},{6,2},{... | collective-permute-start | bytes 1769480 | tf_op jit(solution)/shard_map/ppermute | solution.py:280
  19.9 1.3 copy-start.7
  25.3 25.3 %copy-start.8 = (bf16[4,32,4096]{2,1,0:T(8,128)(2,1)S(1)}, bf16[4,32,4096]{2,1,0:T(8,128)(2,1)}, u32[]{:S(2)}) copy-start(bf16[4,32,4096]{2,1,0:T(8,128)(2,1)} %get-tuple-element.36) | copy-start | bytes 3145732
  25.3 25.3 %collective-permute-start.6 = (bf16[4,32,4096]{2,1,0:T(8,128)(2,1)}, bf16[4,32,4096]{2,1,0:T(8,128)(2,1)}, u32[]{:S(2)}, u32[]{:S(2)}) collective-permute-start(bf16[4,32,4096]{2,1,0:T(8,128)(2,1)} %get-tuple-element.37), channel_id=1, source_target_pairs={{0,2},{2,0},{1,3},{3,1},{4,6},{6,4},{5,7},{7,5},{8,10},{10,8},{9,1... | collective-permute-start | bytes 3145736 | tf_op jit(solution)/shard_map/ppermute | solution.py:424
  31.7 13.5 %copy-start.9 = (bf16[64,4608]{1,0:T(8,128)(2,1)}, bf16[64,4608]{1,0:T(8,128)(2,1)S(1)}, u32[]{:S(2)}) copy-start(bf16[64,4608]{1,0:T(8,128)(2,1)S(1)} %collective-permute-done.2.up) | copy-start | bytes 1769476
  47.1 16.9 %copy-start.1 = (f32[32,4096]{1,0:T(8,128)}, f32[32,4096]{1,0:T(8,128)S(1)}, u32[]{:S(2)}) copy-start(f32[32,4096]{1,0:T(8,128)S(1)} %get-tuple-element.33.left) | copy-start | bytes 1572868
  47.1 15.6 %collective-permute-start.5 = (bf16[32,8192]{1,0:T(8,128)(2,1)S(1)}, bf16[32,8192]{1,0:T(8,128)(2,1)S(1)}, u32[]{:S(2)}, u32[]{:S(2)}) collective-permute-start(bf16[32,8192]{1,0:T(8,128)(2,1)S(1)} %get-tuple-element.34), channel_id=1, source_target_pairs={{0,2},{2,0},{1,3},{3,1},{4,6},{6,4},{5,7},{7,5},{8,10},{10,8},{9,1... | collective-permute-start | bytes 1572872 | tf_op jit(solution)/shard_map/ppermute | solution.py:429
  53.0 14.3 %collective-permute-start.9 = (bf16[32,4096]{1,0:T(8,128)(2,1)}, bf16[32,4096]{1,0:T(8,128)(2,1)S(1)}, u32[]{:S(2)}, u32[]{:S(2)}) collective-permute-start(bf16[32,4096]{1,0:T(8,128)(2,1)} %get-tuple-element.48), channel_id=1, source_target_pairs={{0,12},{4,0},{8,4},{12,8},{1,13},{5,1},{9,5},{13,9},{2,14},{6,2},{... | collective-permute-start | bytes 786440 | tf_op jit(solution)/shard_map/ppermute | solution.py:280
  55.2 12.1 %collective-permute-start.8 = (bf16[32,4096]{1,0:T(8,128)(2,1)}, bf16[32,4096]{1,0:T(8,128)(2,1)}, u32[]{:S(2)}, u32[]{:S(2)}) collective-permute-start(bf16[32,4096]{1,0:T(8,128)(2,1)} %get-tuple-element.49), channel_id=1, source_target_pairs={{0,4},{4,8},{8,12},{12,0},{1,5},{5,9},{9,13},{13,1},{2,6},{6,10},{... | collective-permute-start | bytes 786440 | tf_op jit(solution)/shard_map/ppermute | solution.py:280
  55.2 12.1 %collective-permute-start.7 = (bf16[32,4096]{1,0:T(8,128)(2,1)}, bf16[32,4096]{1,0:T(8,128)(2,1)}, u32[]{:S(2)}, u32[]{:S(2)}) collective-permute-start(bf16[32,4096]{1,0:T(8,128)(2,1)} %get-tuple-element.50), channel_id=1, source_target_pairs={{0,8},{4,12},{8,0},{12,4},{1,9},{5,13},{9,1},{13,5},{2,10},{6,14},... | collective-permute-start | bytes 786440 | tf_op jit(solution)/shard_map/ppermute | solution.py:280
  62.7 0.8 copy-start.6
  65.0 11.3 %copy-start.4 = (f32[32,8192]{1,0:T(8,128)S(1)}, f32[32,8192]{1,0:T(8,128)}, u32[]{:S(2)}) copy-start(f32[32,8192]{1,0:T(8,128)} %refs_4_.1) | copy-start | bytes 3145732
  65.0 11.2 %copy-start.5 = (f32[32,8192]{1,0:T(8,128)S(1)}, f32[32,8192]{1,0:T(8,128)}, u32[]{:S(2)}) copy-start(f32[32,8192]{1,0:T(8,128)} %refs_3_.1) | copy-start | bytes 3145732
  66.1 13.1 %collective-permute-start.10 = (bf16[1024,256]{1,0:T(8,128)(2,1)}, bf16[1024,256]{1,0:T(8,128)(2,1)}, u32[]{:S(2)}, u32[]{:S(2)}) collective-permute-start(bf16[1024,256]{1,0:T(8,128)(2,1)} %bitcast.20.q_own), channel_id=1, source_target_pairs={{0,1},{1,0},{2,3},{3,2},{4,5},{5,4},{6,7},{7,6},{8,9},{9,8},{10,11... | collective-permute-start | bytes 1572872 | tf_op jit(solution)/shard_map/ppermute | solution.py:276
  67.3 0.7 copy-start.12
  71.2 12.3 %all-to-all-start = ((bf16[8,8,32,128]{3,2,1,0:T(8,128)(2,1)}), bf16[8,8,32,128]{3,2,1,0:T(8,128)(2,1)}, u32[]{:S(2)}, u32[]{:S(2)}) async-start(bf16[8,8,32,128]{3,2,1,0:T(8,128)(2,1)} %get-tuple-element.38), calls=%async_computation | async-start | bytes 1048576 | tf_op jit(solution)/shard_map/all_to_all | solution.py:456
  76.4 44.1 %copy-start.3 = (bf16[32,8192]{1,0:T(8,128)(2,1)}, bf16[32,8192]{1,0:T(8,128)(2,1)S(1)}, u32[]{:S(2)}) copy-start(bf16[32,8192]{1,0:T(8,128)(2,1)S(1)} %subtract_convert_fusion.refs_1_) | copy-start | bytes 1572868
  76.4 35.4 %collective-permute-start.11 = (bf16[32,8192]{1,0:T(8,128)(2,1)S(1)}, bf16[32,8192]{1,0:T(8,128)(2,1)S(1)}, u32[]{:S(2)}, u32[]{:S(2)}) collective-permute-start(bf16[32,8192]{1,0:T(8,128)(2,1)S(1)} %subtract_convert_fusion.refs_1_), channel_id=1, source_target_pairs={{0,1},{1,0},{2,3},{3,2},{4,5},{5,4},{6,7},{7,6},{8,9},{9,8},{10,11... | collective-permute-start | bytes 1572872 | tf_op jit(solution)/shard_map/ppermute | solution.py:276
  85.8 8.6 %copy-start.2 = (bf16[8,32,128]{2,1,0:T(8,128)(2,1)}, bf16[8,32,128]{2,1,0:T(8,128)(2,1)S(1)}, u32[]{:S(2)}) copy-start(bf16[8,32,128]{2,1,0:T(8,128)(2,1)S(1)} %get-tuple-element.40.mean) | copy-start | bytes 196612
  85.8 8.6 %all-to-all-start.1 = ((bf16[8,32,256]{2,1,0:T(8,128)(2,1)}), bf16[8,32,256]{2,1,0:T(8,128)(2,1)S(1)}, u32[]{:S(2)}, u32[]{:S(2)}) async-start(bf16[8,32,256]{2,1,0:T(8,128)(2,1)} %get-tuple-element.39), calls=%async_computation.1 | async-start | bytes 262144 | tf_op jit(solution)/shard_map/all_to_all | solution.py:458
  94.4 0.7 copy-start.11
  111.9 64.8 %copy-start.10 = (bf16[32,8192]{1,0:T(8,128)(2,1)}, bf16[32,8192]{1,0:T(8,128)(2,1)S(1)}, u32[]{:S(2)}) copy-start(bf16[32,8192]{1,0:T(8,128)(2,1)S(1)} %collective-permute-done.11.before) | copy-start | bytes 1572868
  111.9 5.0 %collective-permute-start.12 = (bf16[4,256,128]{2,1,0:T(8,128)(2,1)S(1)}, bf16[4,256,128]{2,1,0:T(8,128)(2,1)S(1)}, u32[]{:S(2)}, u32[]{:S(2)}) collective-permute-start(bf16[4,256,128]{2,1,0:T(8,128)(2,1)S(1)} %bitcast.79), channel_id=1, source_target_pairs={{0,1},{1,0},{2,3},{3,2},{4,5},{5,4},{6,7},{7,6},{8,9},{9,8},{10,11... | collective-permute-start | bytes 786440 | tf_op jit(solution)/shard_map/ppermute | solution.py:276
  176.7 9.6 %collective-permute-start.13 = (bf16[64,256,128]{2,1,0:T(8,128)(2,1)}, bf16[64,256,128]{2,1,0:T(8,128)(2,1)}, u32[]{:S(2)}, u32[]{:S(2)}) collective-permute-start(bf16[64,256,128]{2,1,0:T(8,128)(2,1)} %all_to_all.21), channel_id=1, source_target_pairs={{0,1},{1,0},{2,3},{3,2},{4,5},{5,4},{6,7},{7,6},{8,9},{9,8},{10,11... | collective-permute-start | bytes 12582920 | tf_op jit(solution)/shard_map/ppermute | solution.py:276

commit v6 on v5

--- a/solution.py
+++ b/solution.py
@@ -303,7 +303,8 @@
     ]
 
 
-def theirs_kernel(half, place, parts, out, held, in_sems, out_sems):
+def theirs_kernel(half, parts, out, held, in_sems, out_sems):
+    place = [lax.axis_index(name) for name in ("core", "z", "yhi")]
     loads = block_copies(place, parts, held, in_sems, 1, half)
     stores = [pltpu.make_async_copy(held.at[k, j], out.at[k, j], out_sems.at[k, j]) for k, j in BLOCKS]
     for load in loads:
@@ -315,15 +316,15 @@
         store.wait()
 
 
-def theirs(place, parts, half):
+def theirs(parts, half):
     shape = (4, 2, 32, WIDE)
     return pl.pallas_call(
         functools.partial(theirs_kernel, half),
-        in_specs=[SMEM, ANYWHERE],
+        in_specs=[ANYWHERE],
         out_specs=ANYWHERE,
         out_shape=jax.ShapeDtypeStruct(shape, BF16),
         scratch_shapes=[pltpu.VMEM(shape, BF16)] + [pltpu.SemaphoreType.DMA((4, 2))] * 2,
-    )(place, parts)
+    )(parts)
 
 
 def add(left, right):
@@ -411,8 +412,8 @@
 
 def summed_rows(partials, error, piece, place, z, yhi):
     parts = partials.reshape(16, 32, 8192)
-    left_out, parts_later = lax.optimization_barrier((theirs(place, parts, 0), parts))
-    left_in, right_in = swap_cores(left_out), swap_cores(theirs(place, parts_later, 1))
+    left_out, parts_later = lax.optimization_barrier((theirs(parts, 0), parts))
+    left_in, right_in = swap_cores(left_out), swap_cores(theirs(parts_later, 1))
     shapes = [(64, WIDE)] + [(64, WIDE + 512)] * 3
     left, up, far, down = pair_call(
         left_kernel, shapes, (4, 64, WIDE + 512), place, parts, left_in, piece

time: 192 us -> 191 us (level)
  transfers between devices with their start and end apart: 16 -> 16, of which waited for: 8 -> 8; matrix products, arithmetic and copies ran while one was open for 4% -> 4% of each run, Pallas kernels for 15% -> 14%
where the time goes in v6:
time: 191 us; the launch traced here: 190 us
  blocking collectives  71.3 us (37%)
  Pallas kernels  37.9 us (20%)
  starting transfers between devices  34.8 us (18%)
  waiting for transfers between devices  33.9 us (18%)
  local copies, waits for them, and re-layouts  6.85 us (4%)
  other arithmetic  3.85 us (2%)
    all_to_all x1, blocking collectives, on_device(): moved_own = lax.all_to_all(factors(own, other), CHIPS, 0, 0, tiled=True)  56.1 us
    ppermute x6, waiting for transfers between devices, along_z(): return lax.ppermute(value, 'z', [(at, (at + step) % 4) for at in range(4)])  17 us
    all_to_all x1, blocking collectives, on_device(): own = lax.all_to_all(gathered(terms, mean, columns), ZY, 0, 0, tiled=True)  15.1 us
    ppermute x6, starting transfers between devices, swap_cores(): return lax.ppermute(value, 'core', SWAP)  11.2 us
    ppermute x6, starting transfers between devices, along_z(): return lax.ppermute(value, 'z', [(at, (at + step) % 4) for at in range(4)])  9.2 us
    pallas_call x2, Pallas kernels, pair_call(): pl.pallas_call(kernel, in_specs=[SMEM, ANYWHERE, ANYWHERE] + [vmem] * len...  8.13 us
    pallas_call x1, Pallas kernels, own_rows(): pl.pallas_call(own_kernel, in_specs=[SMEM] + [ANYWHERE] * 5, out_specs=[A...  7.59 us
    ppermute x1, waiting for transfers between devices, summed_rows(): back = lax.ppermute(sent, 'yhi', SWAP)  6.29 us
  transfers between devices with their start and end apart: 16, of which 8 were waited for; matrix products, arithmetic and copies ran while one was open for 4% of the time, Pallas kernels for 14%

profile of v6, /device:TPU:1, one launch (start us, length us, event | category | flops | bytes accessed | tf_op | source)
XLA Modules:
  0.0 189.8 jit_solution(14380682057565844056)
XLA Ops:
  0.6 0.0 copy-start
  0.6 2.5 %shard_map.84 = bf16[4,2,32,4096]{3,2,1,0:T(8,128)(2,1)} custom-call(bf16[16,32,8192]{2,1,0:T(8,128)(2,1)} %bitcast.81), custom_call_target="tpu_custom_call" | custom-call | tf_op jit(solution)/shard_map/pallas_call | solution.py:321
  3.1 1.5 collective-permute-start.1
  4.6 2.4 %shard_map.85 = bf16[4,2,32,4096]{3,2,1,0:T(8,128)(2,1)} custom-call(bf16[16,32,8192]{2,1,0:T(8,128)(2,1)} %bitcast.82), custom_call_target="tpu_custom_call" | custom-call | tf_op jit(solution)/shard_map/pallas_call | solution.py:321
  7.1 0.1 collective-permute-start
  7.2 0.6 pad_add_fusion.place
  7.8 0.6 pad_maximum_fusion.1.piece
  8.4 0.3 collective-permute-done.1.received
  8.7 4.1 %shard_map.86 = (bf16[64,4096]{1,0:T(8,128)(2,1)}, bf16[64,4608]{1,0:T(8,128)(2,1)}, bf16[64,4608]{1,0:T(8,128)(2,1)}, bf16[64,4608]{1,0:T(8,128)(2,1)}) custom-call(s32[4]{0:T(128)} %pad_add_fusion.place, bf16[16,32,8192]{2,1,0:T(8,128)(2,1)} %bitcast.83, bf16[4,2,32,4096]{3,2,1,0:T(8,128)(2,1)} %collective-permute-done.1.received, ...), custom_call_target="tpu_custom_call" | custom-call | tf_op jit(solution)/shard_map/pallas_call | solution.py:374
  12.9 1.8 collective-permute-start.2
  14.7 3.3 %collective-permute-start.3 = (bf16[64,4608]{1,0:T(8,128)(2,1)}, bf16[64,4608]{1,0:T(8,128)(2,1)}, u32[]{:S(2)}, u32[]{:S(2)}) collective-permute-start(bf16[64,4608]{1,0:T(8,128)(2,1)} %get-tuple-element.31), channel_id=1, source_target_pairs={{0,8},{4,12},{8,0},{12,4},{1,9},{5,13},{9,1},{13,5},{2,10},{6,14},... | collective-permute-start | bytes 1769480 | tf_op jit(solution)/shard_map/ppermute | solution.py:280
  18.0 0.7 collective-permute-start.4
  18.7 0.0 collective-permute-done.received
  18.7 1.3 copy-done.7
  20.0 4.0 %shard_map.88 = (bf16[4,32,4096]{2,1,0:T(8,128)(2,1)}, bf16[4,32,4096]{2,1,0:T(8,128)(2,1)}) custom-call(s32[4]{0:T(128)} %pad_add_fusion.place, bf16[16,32,8192]{2,1,0:T(8,128)(2,1)} %bitcast.84, bf16[4,2,32,4096]{3,2,1,0:T(8,128)(2,1)} %copy-done.7), custom_call_target="tpu_custom_call" | custom-call | tf_op jit(solution)/shard_map/pallas_call | solution.py:374
  24.0 0.0 copy-start.8
  24.1 3.0 %collective-permute-start.6 = (bf16[4,32,4096]{2,1,0:T(8,128)(2,1)}, bf16[4,32,4096]{2,1,0:T(8,128)(2,1)}, u32[]{:S(2)}, u32[]{:S(2)}) collective-permute-start(bf16[4,32,4096]{2,1,0:T(8,128)(2,1)} %get-tuple-element.37), channel_id=1, source_target_pairs={{0,2},{2,0},{1,3},{3,1},{4,6},{6,4},{5,7},{7,5},{8,10},{10,8},{9,1... | collective-permute-start | bytes 3145736 | tf_op jit(solution)/shard_map/ppermute | solution.py:425
  27.0 3.5 %collective-permute-done.2.up = bf16[64,4608]{1,0:T(8,128)(2,1)S(1)} collective-permute-done((bf16[64,4608]{1,0:T(8,128)(2,1)}, bf16[64,4608]{1,0:T(8,128)(2,1)S(1)}, u32[]{:S(2)}, u32[]{:S(2)}) %collective-permute-start.2) | collective-permute-done | bytes 589856 | tf_op jit(solution)/shard_map/ppermute | solution.py:280
  30.5 13.5 %collective-permute-done.3.far = bf16[64,4608]{1,0:T(8,128)(2,1)} collective-permute-done((bf16[64,4608]{1,0:T(8,128)(2,1)}, bf16[64,4608]{1,0:T(8,128)(2,1)}, u32[]{:S(2)}, u32[]{:S(2)}) %collective-permute-start.3) | collective-permute-done | bytes 589856 | tf_op jit(solution)/shard_map/ppermute | solution.py:280
  44.0 0.0 collective-permute-done.4.down
  44.0 1.8 shard_map.87
  45.8 0.0 copy-start.1
  45.9 3.0 %collective-permute-start.5 = (bf16[32,8192]{1,0:T(8,128)(2,1)S(1)}, bf16[32,8192]{1,0:T(8,128)(2,1)S(1)}, u32[]{:S(2)}, u32[]{:S(2)}) collective-permute-start(bf16[32,8192]{1,0:T(8,128)(2,1)S(1)} %get-tuple-element.34), channel_id=1, source_target_pairs={{0,2},{2,0},{1,3},{3,1},{4,6},{6,4},{5,7},{7,5},{8,10},{10,8},{9,1... | collective-permute-start | bytes 1572872 | tf_op jit(solution)/shard_map/ppermute | solution.py:430
  49.0 0.4 collective-permute-done.6
  49.4 2.4 %fusion.2 = (bf16[32,4096]{1,0:T(8,128)(2,1)}, bf16[32,4096]{1,0:T(8,128)(2,1)}, bf16[32,4096]{1,0:T(8,128)(2,1)}, f32[32,4096]{1,0:T(8,128)}) fusion(bf16[4,32,4096]{2,1,0:T(8,128)(2,1)} %collective-permute-done.6, bf16[4,32,4096]{2,1,0:T(8,128)(2,1)S(1)} %copy-done.8), kind=kLoop, calls=%fused_computation.9 | loop fusion | flops 1966080 | bytes 3407872 | tf_op jit(solution)/shard_map/convert_element_type | solution.py:428
  51.8 2.2 %collective-permute-start.9 = (bf16[32,4096]{1,0:T(8,128)(2,1)}, bf16[32,4096]{1,0:T(8,128)(2,1)S(1)}, u32[]{:S(2)}, u32[]{:S(2)}) collective-permute-start(bf16[32,4096]{1,0:T(8,128)(2,1)} %get-tuple-element.48), channel_id=1, source_target_pairs={{0,12},{4,0},{8,4},{12,8},{1,13},{5,1},{9,5},{13,9},{2,14},{6,2},{... | collective-permute-start | bytes 786440 | tf_op jit(solution)/shard_map/ppermute | solution.py:280
  54.0 0.0 collective-permute-start.8
  54.0 1.2 collective-permute-start.7
  55.2 6.3 %collective-permute-done.5.back = bf16[32,8192]{1,0:T(8,128)(2,1)S(1)} collective-permute-done((bf16[32,8192]{1,0:T(8,128)(2,1)S(1)}, bf16[32,8192]{1,0:T(8,128)(2,1)S(1)}, u32[]{:S(2)}, u32[]{:S(2)}) %collective-permute-start.5) | collective-permute-done | bytes 524320 | tf_op jit(solution)/shard_map/ppermute | solution.py:430
  61.6 0.6 copy-done.6
  62.2 0.1 maximum_select_fusion
  62.3 0.4 select_n.47
  62.7 1.1 fusion.11
  63.8 0.0 copy-start.4
  63.8 0.0 copy-start.5
  63.9 0.1 pad_maximum_fusion
  64.0 0.8 copy.33
  64.8 1.2 collective-permute-start.10
  66.0 0.0 collective-permute-done.9.down
  66.0 0.0 collective-permute-done.7.far
  66.1 0.7 copy-done.12
  66.7 3.3 %shard_map.89 = (f32[32,8192]{1,0:T(8,128)}, bf16[8,8,32,128]{3,2,1,0:T(8,128)(2,1)}) custom-call(f32[32,4096]{1,0:T(8,128)} %copy-done.1, bf16[32,8192]{1,0:T(8,128)(2,1)} %copy-done.6, f32[32,4096]{1,0:T(8,128)} %get-tuple-element.51.right, bf16[32,4096]{1,0:T(8,128)(2,1)} %collective-permute-done.7.far, bf16[32,4096]{1,0:T(8,128)(2,1)} %collective-permute-done.8.up, ...), custom_call_target="tpu_custom_call" | custom-call | tf_op jit(solution)/shard_map/pallas_call | solution.py:264
  70.0 5.0 %all-to-all-start = ((bf16[8,8,32,128]{3,2,1,0:T(8,128)(2,1)}), bf16[8,8,32,128]{3,2,1,0:T(8,128)(2,1)}, u32[]{:S(2)}, u32[]{:S(2)}) async-start(bf16[8,8,32,128]{3,2,1,0:T(8,128)(2,1)} %get-tuple-element.38), calls=%async_computation | async-start | bytes 1048576 | tf_op jit(solution)/shard_map/all_to_all | solution.py:457
  75.1 0.1 subtract_convert_fusion.refs_1_
  75.2 2.6 %collective-permute-start.11 = (bf16[32,8192]{1,0:T(8,128)(2,1)S(1)}, bf16[32,8192]{1,0:T(8,128)(2,1)S(1)}, u32[]{:S(2)}, u32[]{:S(2)}) collective-permute-start(bf16[32,8192]{1,0:T(8,128)(2,1)S(1)} %subtract_convert_fusion.refs_1_), channel_id=1, source_target_pairs={{0,1},{1,0},{2,3},{3,2},{4,5},{5,4},{6,7},{7,6},{8,9},{9,8},{10,11... | collective-permute-start | bytes 1572872 | tf_op jit(solution)/shard_map/ppermute | solution.py:276
  77.8 0.1 copy.40
  77.9 0.0 collective-permute-done.10.q_other
  77.9 4.4 %all-to-all-done.blocks = bf16[8,8,32,128]{3,2,1,0:T(8,128)(2,1)} async-done(((bf16[8,8,32,128]{3,2,1,0:T(8,128)(2,1)}), bf16[8,8,32,128]{3,2,1,0:T(8,128)(2,1)}, u32[]{:S(2)}, u32[]{:S(2)}) %all-to-all-start) | async-done | bytes 524320 | tf_op jit(solution)/shard_map/all_to_all | solution.py:457
  82.3 2.3 %shard_map.90 = (bf16[8,32,128]{2,1,0:T(8,128)(2,1)S(1)}, bf16[8,32,256]{2,1,0:T(8,128)(2,1)}) custom-call(s32[4]{0:T(128)} %pad_add_fusion.place, bf16[8,8,32,128]{3,2,1,0:T(8,128)(2,1)} %all-to-all-done.blocks, bf16[1024,256]{1,0:T(8,128)(2,1)} %bitcast.20.q_own, bf16[1024,256]{1,0:T(8,128)(2,1)} %collective-permute-done.10.q_other), custom_call_target="tpu_custom_call" | custom-call | tf_op jit(solution)/shard_map/pallas_call | solution.py:215
  84.6 3.4 %all-to-all-start.1 = ((bf16[8,32,256]{2,1,0:T(8,128)(2,1)}), bf16[8,32,256]{2,1,0:T(8,128)(2,1)S(1)}, u32[]{:S(2)}, u32[]{:S(2)}) async-start(bf16[8,32,256]{2,1,0:T(8,128)(2,1)} %get-tuple-element.39), calls=%async_computation.1 | async-start | bytes 262144 | tf_op jit(solution)/shard_map/all_to_all | solution.py:459
  88.0 0.1 constant_dynamic-slice_fusion
  88.1 0.7 copy.46
  88.8 4.4 %all-to-all-done.1.terms = bf16[8,32,256]{2,1,0:T(8,128)(2,1)S(1)} async-done(((bf16[8,32,256]{2,1,0:T(8,128)(2,1)}), bf16[8,32,256]{2,1,0:T(8,128)(2,1)S(1)}, u32[]{:S(2)}, u32[]{:S(2)}) %all-to-all-start.1) | async-done | bytes 131104 | tf_op jit(solution)/shard_map/all_to_all | solution.py:459
  93.2 0.7 copy-done.11
  93.8 1.7 shard_map.91
  95.5 15.1 %all_to_all.20 = bf16[8,4,32,128]{3,2,1,0:T(8,128)(2,1)S(1)} all-to-all(bf16[8,4,32,128]{3,2,1,0:T(8,128)(2,1)} %shard_map.91), channel_id=1, replica_groups=mesh['x'=4,'ylo'=2,'z'=4,'yhi'=2,'core'=2] {'z','yhi'}, dimensions={0} | all-to-all | bytes 524288 | tf_op jit(solution)/shard_map/all_to_all | solution.py:461
  110.6 0.0 collective-permute-done.11.before
  110.7 3.8 %collective-permute-start.12 = (bf16[4,256,128]{2,1,0:T(8,128)(2,1)S(1)}, bf16[4,256,128]{2,1,0:T(8,128)(2,1)S(1)}, u32[]{:S(2)}, u32[]{:S(2)}) collective-permute-start(bf16[4,256,128]{2,1,0:T(8,128)(2,1)S(1)} %bitcast.79), channel_id=1, source_target_pairs={{0,1},{1,0},{2,3},{3,2},{4,5},{5,4},{6,7},{7,6},{8,9},{9,8},{10,11... | collective-permute-start | bytes 786440 | tf_op jit(solution)/shard_map/ppermute | solution.py:276
  114.5 1.2 collective-permute-done.12.other_ref
  115.7 3.6 %shard_map.92 = bf16[64,256,128]{2,1,0:T(8,128)(2,1)S(1)} custom-call(bf16[4,256,128]{2,1,0:T(8,128)(2,1)S(1)} %bitcast.80, bf16[4,256,128]{2,1,0:T(8,128)(2,1)S(1)} %collective-permute-done.12.other_ref), custom_call_target="tpu_custom_call" | custom-call | tf_op jit(solution)/shard_map/pallas_call | solution.py:66
  119.3 56.1 %all_to_all.21 = bf16[64,256,128]{2,1,0:T(8,128)(2,1)} all-to-all(bf16[64,256,128]{2,1,0:T(8,128)(2,1)S(1)} %shard_map.92), channel_id=1, replica_groups=mesh['x'=4,'ylo'=2,'z'=4,'yhi'=2,'core'=2] {'x','ylo','z','yhi'}, dimensions={0} | all-to-all | bytes 8388608 | tf_op jit(solution)/shard_map/all_to_all | solution.py:466
  175.4 2.0 %collective-permute-start.13 = (bf16[64,256,128]{2,1,0:T(8,128)(2,1)}, bf16[64,256,128]{2,1,0:T(8,128)(2,1)}, u32[]{:S(2)}, u32[]{:S(2)}) collective-permute-start(bf16[64,256,128]{2,1,0:T(8,128)(2,1)} %all_to_all.21), channel_id=1, source_target_pairs={{0,1},{1,0},{2,3},{3,2},{4,5},{5,4},{6,7},{7,6},{8,9},{9,8},{10,11... | collective-permute-start | bytes 12582920 | tf_op jit(solution)/shard_map/ppermute | solution.py:276
  177.5 7.6 %shard_map.93 = (bf16[8,2,32,8192]{3,2,1,0:T(8,128)(2,1)}, f32[32,8192]{1,0:T(8,128)}, f32[32,8192]{1,0:T(8,128)}, f32[32,8192]{1,0:T(8,128)}) custom-call(s32[4]{0:T(128)} %pad_add_fusion.place, bf16[8,8,256,128]{3,2,1,0:T(8,128)(2,1)} %bitcast.26.refs_0_, bf16[32,8192]{1,0:T(8,128)(2,1)} %copy-done.3, f32[32,8192]{1,0:T(8,128)} %get-tuple-element.43.refs_2_, ...), custom_call_target="tpu_custom_call" | custom-call | tf_op jit(solution)/shard_map/pallas_call | solution.py:138
  185.1 4.6 %shard_map.94 = bf16[8,2,32,8192]{3,2,1,0:T(8,128)(2,1)} custom-call(s32[4]{0:T(128)} %pad_add_fusion.place, bf16[8,8,256,128]{3,2,1,0:T(8,128)(2,1)} %bitcast.25.moved, bf16[32,8192]{1,0:T(8,128)(2,1)} %copy-done.10, bf16[8,2,32,8192]{3,2,1,0:T(8,128)(2,1)} %get-tuple-element.44._), custom_call_target="tpu_custom_call", output_to_operand_aliasing={{}: (3, {})} | custom-call | tf_op jit(solution)/shard_map/pallas_call | solution.py:179
  (42 shorter events, 0.3 us)
Async XLA Ops:
  0.6 7.2 %copy-start = (f32[512,256]{1,0:T(8,128)S(1)}, f32[512,256]{1,0:T(8,128)}, u32[]{:S(2)}) copy-start(f32[512,256]{1,0:T(8,128)} %param.9) | copy-start | bytes 1572868
  3.1 5.6 %collective-permute-start.1 = (bf16[4,2,32,4096]{3,2,1,0:T(8,128)(2,1)}, bf16[4,2,32,4096]{3,2,1,0:T(8,128)(2,1)}, u32[]{:S(2)}, u32[]{:S(2)}) collective-permute-start(bf16[4,2,32,4096]{3,2,1,0:T(8,128)(2,1)} %shard_map.84), channel_id=1, source_target_pairs={{0,1},{1,0},{2,3},{3,2},{4,5},{5,4},{6,7},{7,6},{8,9},{9,8},{10,11... | collective-permute-start | bytes 6291464 | tf_op jit(solution)/shard_map/ppermute | solution.py:276
  7.1 11.6 %collective-permute-start = (bf16[4,2,32,4096]{3,2,1,0:T(8,128)(2,1)}, bf16[4,2,32,4096]{3,2,1,0:T(8,128)(2,1)S(1)}, u32[]{:S(2)}, u32[]{:S(2)}) collective-permute-start(bf16[4,2,32,4096]{3,2,1,0:T(8,128)(2,1)} %shard_map.85), channel_id=1, source_target_pairs={{0,1},{1,0},{2,3},{3,2},{4,5},{5,4},{6,7},{7,6},{8,9},{9,8},{10,11... | collective-permute-start | bytes 6291464 | tf_op jit(solution)/shard_map/ppermute | solution.py:276
  12.9 17.6 %collective-permute-start.2 = (bf16[64,4608]{1,0:T(8,128)(2,1)}, bf16[64,4608]{1,0:T(8,128)(2,1)S(1)}, u32[]{:S(2)}, u32[]{:S(2)}) collective-permute-start(bf16[64,4608]{1,0:T(8,128)(2,1)} %get-tuple-element.30), channel_id=1, source_target_pairs={{0,4},{4,8},{8,12},{12,0},{1,5},{5,9},{9,13},{13,1},{2,6},{6,10},{... | collective-permute-start | bytes 1769480 | tf_op jit(solution)/shard_map/ppermute | solution.py:280
  14.7 29.3 %collective-permute-start.3 = (bf16[64,4608]{1,0:T(8,128)(2,1)}, bf16[64,4608]{1,0:T(8,128)(2,1)}, u32[]{:S(2)}, u32[]{:S(2)}) collective-permute-start(bf16[64,4608]{1,0:T(8,128)(2,1)} %get-tuple-element.31), channel_id=1, source_target_pairs={{0,8},{4,12},{8,0},{12,4},{1,9},{5,13},{9,1},{13,5},{2,10},{6,14},... | collective-permute-start | bytes 1769480 | tf_op jit(solution)/shard_map/ppermute | solution.py:280
  18.0 26.0 %collective-permute-start.4 = (bf16[64,4608]{1,0:T(8,128)(2,1)}, bf16[64,4608]{1,0:T(8,128)(2,1)}, u32[]{:S(2)}, u32[]{:S(2)}) collective-permute-start(bf16[64,4608]{1,0:T(8,128)(2,1)} %get-tuple-element.32), channel_id=1, source_target_pairs={{0,12},{4,0},{8,4},{12,8},{1,13},{5,1},{9,5},{13,9},{2,14},{6,2},{... | collective-permute-start | bytes 1769480 | tf_op jit(solution)/shard_map/ppermute | solution.py:280
  18.7 1.3 copy-start.7
  24.0 25.3 %copy-start.8 = (bf16[4,32,4096]{2,1,0:T(8,128)(2,1)S(1)}, bf16[4,32,4096]{2,1,0:T(8,128)(2,1)}, u32[]{:S(2)}) copy-start(bf16[4,32,4096]{2,1,0:T(8,128)(2,1)} %get-tuple-element.36) | copy-start | bytes 3145732
  24.1 25.3 %collective-permute-start.6 = (bf16[4,32,4096]{2,1,0:T(8,128)(2,1)}, bf16[4,32,4096]{2,1,0:T(8,128)(2,1)}, u32[]{:S(2)}, u32[]{:S(2)}) collective-permute-start(bf16[4,32,4096]{2,1,0:T(8,128)(2,1)} %get-tuple-element.37), channel_id=1, source_target_pairs={{0,2},{2,0},{1,3},{3,1},{4,6},{6,4},{5,7},{7,5},{8,10},{10,8},{9,1... | collective-permute-start | bytes 3145736 | tf_op jit(solution)/shard_map/ppermute | solution.py:425
  30.5 13.5 %copy-start.9 = (bf16[64,4608]{1,0:T(8,128)(2,1)}, bf16[64,4608]{1,0:T(8,128)(2,1)S(1)}, u32[]{:S(2)}) copy-start(bf16[64,4608]{1,0:T(8,128)(2,1)S(1)} %collective-permute-done.2.up) | copy-start | bytes 1769476
  45.8 16.9 %copy-start.1 = (f32[32,4096]{1,0:T(8,128)}, f32[32,4096]{1,0:T(8,128)S(1)}, u32[]{:S(2)}) copy-start(f32[32,4096]{1,0:T(8,128)S(1)} %get-tuple-element.33.left) | copy-start | bytes 1572868
  45.9 15.6 %collective-permute-start.5 = (bf16[32,8192]{1,0:T(8,128)(2,1)S(1)}, bf16[32,8192]{1,0:T(8,128)(2,1)S(1)}, u32[]{:S(2)}, u32[]{:S(2)}) collective-permute-start(bf16[32,8192]{1,0:T(8,128)(2,1)S(1)} %get-tuple-element.34), channel_id=1, source_target_pairs={{0,2},{2,0},{1,3},{3,1},{4,6},{6,4},{5,7},{7,5},{8,10},{10,8},{9,1... | collective-permute-start | bytes 1572872 | tf_op jit(solution)/shard_map/ppermute | solution.py:430
  51.8 14.3 %collective-permute-start.9 = (bf16[32,4096]{1,0:T(8,128)(2,1)}, bf16[32,4096]{1,0:T(8,128)(2,1)S(1)}, u32[]{:S(2)}, u32[]{:S(2)}) collective-permute-start(bf16[32,4096]{1,0:T(8,128)(2,1)} %get-tuple-element.48), channel_id=1, source_target_pairs={{0,12},{4,0},{8,4},{12,8},{1,13},{5,1},{9,5},{13,9},{2,14},{6,2},{... | collective-permute-start | bytes 786440 | tf_op jit(solution)/shard_map/ppermute | solution.py:280
  54.0 12.1 %collective-permute-start.8 = (bf16[32,4096]{1,0:T(8,128)(2,1)}, bf16[32,4096]{1,0:T(8,128)(2,1)}, u32[]{:S(2)}, u32[]{:S(2)}) collective-permute-start(bf16[32,4096]{1,0:T(8,128)(2,1)} %get-tuple-element.49), channel_id=1, source_target_pairs={{0,4},{4,8},{8,12},{12,0},{1,5},{5,9},{9,13},{13,1},{2,6},{6,10},{... | collective-permute-start | bytes 786440 | tf_op jit(solution)/shard_map/ppermute | solution.py:280
  54.0 12.1 %collective-permute-start.7 = (bf16[32,4096]{1,0:T(8,128)(2,1)}, bf16[32,4096]{1,0:T(8,128)(2,1)}, u32[]{:S(2)}, u32[]{:S(2)}) collective-permute-start(bf16[32,4096]{1,0:T(8,128)(2,1)} %get-tuple-element.50), channel_id=1, source_target_pairs={{0,8},{4,12},{8,0},{12,4},{1,9},{5,13},{9,1},{13,5},{2,10},{6,14},... | collective-permute-start | bytes 786440 | tf_op jit(solution)/shard_map/ppermute | solution.py:280
  61.5 0.8 copy-start.6
  63.8 11.3 %copy-start.4 = (f32[32,8192]{1,0:T(8,128)S(1)}, f32[32,8192]{1,0:T(8,128)}, u32[]{:S(2)}) copy-start(f32[32,8192]{1,0:T(8,128)} %refs_4_.1) | copy-start | bytes 3145732
  63.8 11.2 %copy-start.5 = (f32[32,8192]{1,0:T(8,128)S(1)}, f32[32,8192]{1,0:T(8,128)}, u32[]{:S(2)}) copy-start(f32[32,8192]{1,0:T(8,128)} %refs_3_.1) | copy-start | bytes 3145732
  64.8 13.1 %collective-permute-start.10 = (bf16[1024,256]{1,0:T(8,128)(2,1)}, bf16[1024,256]{1,0:T(8,128)(2,1)}, u32[]{:S(2)}, u32[]{:S(2)}) collective-permute-start(bf16[1024,256]{1,0:T(8,128)(2,1)} %bitcast.20.q_own), channel_id=1, source_target_pairs={{0,1},{1,0},{2,3},{3,2},{4,5},{5,4},{6,7},{7,6},{8,9},{9,8},{10,11... | collective-permute-start | bytes 1572872 | tf_op jit(solution)/shard_map/ppermute | solution.py:276
  66.0 0.7 copy-start.12
  70.0 12.3 %all-to-all-start = ((bf16[8,8,32,128]{3,2,1,0:T(8,128)(2,1)}), bf16[8,8,32,128]{3,2,1,0:T(8,128)(2,1)}, u32[]{:S(2)}, u32[]{:S(2)}) async-start(bf16[8,8,32,128]{3,2,1,0:T(8,128)(2,1)} %get-tuple-element.38), calls=%async_computation | async-start | bytes 1048576 | tf_op jit(solution)/shard_map/all_to_all | solution.py:457
  75.2 44.1 %copy-start.3 = (bf16[32,8192]{1,0:T(8,128)(2,1)}, bf16[32,8192]{1,0:T(8,128)(2,1)S(1)}, u32[]{:S(2)}) copy-start(bf16[32,8192]{1,0:T(8,128)(2,1)S(1)} %subtract_convert_fusion.refs_1_) | copy-start | bytes 1572868
  75.2 35.4 %collective-permute-start.11 = (bf16[32,8192]{1,0:T(8,128)(2,1)S(1)}, bf16[32,8192]{1,0:T(8,128)(2,1)S(1)}, u32[]{:S(2)}, u32[]{:S(2)}) collective-permute-start(bf16[32,8192]{1,0:T(8,128)(2,1)S(1)} %subtract_convert_fusion.refs_1_), channel_id=1, source_target_pairs={{0,1},{1,0},{2,3},{3,2},{4,5},{5,4},{6,7},{7,6},{8,9},{9,8},{10,11... | collective-permute-start | bytes 1572872 | tf_op jit(solution)/shard_map/ppermute | solution.py:276
  84.6 8.6 %copy-start.2 = (bf16[8,32,128]{2,1,0:T(8,128)(2,1)}, bf16[8,32,128]{2,1,0:T(8,128)(2,1)S(1)}, u32[]{:S(2)}) copy-start(bf16[8,32,128]{2,1,0:T(8,128)(2,1)S(1)} %get-tuple-element.40.mean) | copy-start | bytes 196612
  84.6 8.6 %all-to-all-start.1 = ((bf16[8,32,256]{2,1,0:T(8,128)(2,1)}), bf16[8,32,256]{2,1,0:T(8,128)(2,1)S(1)}, u32[]{:S(2)}, u32[]{:S(2)}) async-start(bf16[8,32,256]{2,1,0:T(8,128)(2,1)} %get-tuple-element.39), calls=%async_computation.1 | async-start | bytes 262144 | tf_op jit(solution)/shard_map/all_to_all | solution.py:459
  93.2 0.7 copy-start.11
  110.7 64.8 %copy-start.10 = (bf16[32,8192]{1,0:T(8,128)(2,1)}, bf16[32,8192]{1,0:T(8,128)(2,1)S(1)}, u32[]{:S(2)}) copy-start(bf16[32,8192]{1,0:T(8,128)(2,1)S(1)} %collective-permute-done.11.before) | copy-start | bytes 1572868
  110.7 5.0 %collective-permute-start.12 = (bf16[4,256,128]{2,1,0:T(8,128)(2,1)S(1)}, bf16[4,256,128]{2,1,0:T(8,128)(2,1)S(1)}, u32[]{:S(2)}, u32[]{:S(2)}) collective-permute-start(bf16[4,256,128]{2,1,0:T(8,128)(2,1)S(1)} %bitcast.79), channel_id=1, source_target_pairs={{0,1},{1,0},{2,3},{3,2},{4,5},{5,4},{6,7},{7,6},{8,9},{9,8},{10,11... | collective-permute-start | bytes 786440 | tf_op jit(solution)/shard_map/ppermute | solution.py:276
  175.4 9.6 %collective-permute-start.13 = (bf16[64,256,128]{2,1,0:T(8,128)(2,1)}, bf16[64,256,128]{2,1,0:T(8,128)(2,1)}, u32[]{:S(2)}, u32[]{:S(2)}) collective-permute-start(bf16[64,256,128]{2,1,0:T(8,128)(2,1)} %all_to_all.21), channel_id=1, source_target_pairs={{0,1},{1,0},{2,3},{3,2},{4,5},{5,4},{6,7},{7,6},{8,9},{9,8},{10,11... | collective-permute-start | bytes 12582920 | tf_op jit(solution)/shard_map/ppermute | solution.py:276

commit v7 on v6

--- a/solution.py
+++ b/solution.py
@@ -371,16 +371,19 @@
 
 def pair_call(kernel, shapes, made, place, parts, received, *rest):
     vmem = pl.BlockSpec(memory_space=pltpu.VMEM)
-    return pl.pallas_call(
-        kernel,
-        in_specs=[SMEM, ANYWHERE, ANYWHERE] + [vmem] * len(rest),
+    def placed(*refs):
+        kernel([lax.axis_index(name) for name in ("core", "z", "yhi")], *refs)
+
+    return pl.pallas_call(
+        placed,
+        in_specs=[ANYWHERE, ANYWHERE] + [vmem] * len(rest),
         out_specs=[ANYWHERE] * len(shapes),
         out_shape=[jax.ShapeDtypeStruct(shape, BF16) for shape in shapes],
         scratch_shapes=[pltpu.VMEM(made, BF16), pltpu.SemaphoreType.DMA((4, 2))]
         + [pltpu.VMEM((4, 2, 32, WIDE), BF16)] * 2
         + [pltpu.SemaphoreType.DMA((4, 2))] * 2,
         compiler_params=pltpu.CompilerParams(vmem_limit_bytes=VMEM),
-    )(place, parts, received, *rest)
+    )(parts, received, *rest)
 
 
 def turn_kernel(left, up, far, down, piece, keep, back):

time: 191 us -> 190 us (level)
  no operation moved by 1% of the time
where the time goes in v7:
time: 190 us
  blocking collectives  72 us (38%)
  Pallas kernels  37.2 us (20%)
  starting transfers between devices  36.5 us (19%)
  waiting for transfers between devices  32.8 us (17%)
  local copies, waits for them, and re-layouts  6.18 us (3%)
  other arithmetic  3.85 us (2%)
    all_to_all x1, blocking collectives, on_device(): moved_own = lax.all_to_all(factors(own, other), CHIPS, 0, 0, tiled=True)  56.1 us
    ppermute x6, waiting for transfers between devices, along_z(): return lax.ppermute(value, 'z', [(at, (at + step) % 4) for at in range(4)])  18.3 us
    all_to_all x1, blocking collectives, on_device(): own = lax.all_to_all(gathered(terms, mean, columns), ZY, 0, 0, tiled=True)  15.9 us
    ppermute x6, starting transfers between devices, swap_cores(): return lax.ppermute(value, 'core', SWAP)  12.5 us
    ppermute x6, starting transfers between devices, along_z(): return lax.ppermute(value, 'z', [(at, (at + step) % 4) for at in range(4)])  9.59 us
    pallas_call x1, Pallas kernels, own_rows(): pl.pallas_call(own_kernel, in_specs=[SMEM] + [ANYWHERE] * 5, out_specs=[A...  7.59 us
    pallas_call x2, Pallas kernels, pair_call(): pl.pallas_call(placed, in_specs=[ANYWHERE, ANYWHERE] + [vmem] * len(rest)...  7.44 us
    all_to_all x1, starting transfers between devices, on_device(): blocks = lax.all_to_all(blocks, ISLAND, 0, 0, tiled=True)  5.03 us
  transfers between devices with their start and end apart: 16, of which 8 were waited for; matrix products, arithmetic and copies ran while one was open for 4% of the time, Pallas kernels for 14%

profile of v7, /device:TPU:1, one launch (start us, length us, event | category | flops | bytes accessed | tf_op | source)
XLA Modules:
  0.0 189.8 jit_solution(2326569070737070376)
XLA Ops:
  0.6 0.0 copy-start
  0.6 2.5 %shard_map.84 = bf16[4,2,32,4096]{3,2,1,0:T(8,128)(2,1)} custom-call(bf16[16,32,8192]{2,1,0:T(8,128)(2,1)} %bitcast.81), custom_call_target="tpu_custom_call" | custom-call | tf_op jit(solution)/shard_map/pallas_call | solution.py:321
  3.1 1.5 collective-permute-start.1
  4.6 2.4 %shard_map.85 = bf16[4,2,32,4096]{3,2,1,0:T(8,128)(2,1)} custom-call(bf16[16,32,8192]{2,1,0:T(8,128)(2,1)} %bitcast.82), custom_call_target="tpu_custom_call" | custom-call | tf_op jit(solution)/shard_map/pallas_call | solution.py:321
  7.1 0.1 collective-permute-start
  7.2 0.6 pad_maximum_fusion.1.refs_2_.piece
  7.9 0.9 collective-permute-done.1.refs_1_
  8.7 4.1 %shard_map.86 = (bf16[64,4096]{1,0:T(8,128)(2,1)}, bf16[64,4608]{1,0:T(8,128)(2,1)}, bf16[64,4608]{1,0:T(8,128)(2,1)}, bf16[64,4608]{1,0:T(8,128)(2,1)}) custom-call(bf16[16,32,8192]{2,1,0:T(8,128)(2,1)} %bitcast.83, bf16[4,2,32,4096]{3,2,1,0:T(8,128)(2,1)} %collective-permute-done.1.refs_1_, bf16[64,512]{1,0:T(8,128)(2,1)} %pad_maximum_fusion.1.refs_2_.piece), custom_call_target="tpu_custom_call" | custom-call | tf_op jit(solution)/shard_map/pallas_call | solution.py:377
  12.9 1.8 collective-permute-start.2
  14.6 3.3 %collective-permute-start.3 = (bf16[64,4608]{1,0:T(8,128)(2,1)}, bf16[64,4608]{1,0:T(8,128)(2,1)}, u32[]{:S(2)}, u32[]{:S(2)}) collective-permute-start(bf16[64,4608]{1,0:T(8,128)(2,1)} %get-tuple-element.31), channel_id=1, source_target_pairs={{0,8},{4,12},{8,0},{12,4},{1,9},{5,13},{9,1},{13,5},{2,10},{6,14},... | collective-permute-start | bytes 1769480 | tf_op jit(solution)/shard_map/ppermute | solution.py:280
  17.9 0.7 collective-permute-start.4
  18.7 0.0 collective-permute-done.refs_1_
  18.7 1.3 copy-done.6
  20.0 3.3 %shard_map.88 = (bf16[4,32,4096]{2,1,0:T(8,128)(2,1)}, bf16[4,32,4096]{2,1,0:T(8,128)(2,1)}) custom-call(bf16[16,32,8192]{2,1,0:T(8,128)(2,1)} %bitcast.84, bf16[4,2,32,4096]{3,2,1,0:T(8,128)(2,1)} %copy-done.6), custom_call_target="tpu_custom_call" | custom-call | tf_op jit(solution)/shard_map/pallas_call | solution.py:377
  23.3 0.0 copy-start.8
  23.4 3.0 %collective-permute-start.6 = (bf16[4,32,4096]{2,1,0:T(8,128)(2,1)}, bf16[4,32,4096]{2,1,0:T(8,128)(2,1)}, u32[]{:S(2)}, u32[]{:S(2)}) collective-permute-start(bf16[4,32,4096]{2,1,0:T(8,128)(2,1)} %get-tuple-element.37), channel_id=1, source_target_pairs={{0,2},{2,0},{1,3},{3,1},{4,6},{6,4},{5,7},{7,5},{8,10},{10,8},{9,1... | collective-permute-start | bytes 3145736 | tf_op jit(solution)/shard_map/ppermute | solution.py:428
  26.4 4.1 %collective-permute-done.2.up = bf16[64,4608]{1,0:T(8,128)(2,1)S(1)} collective-permute-done((bf16[64,4608]{1,0:T(8,128)(2,1)}, bf16[64,4608]{1,0:T(8,128)(2,1)S(1)}, u32[]{:S(2)}, u32[]{:S(2)}) %collective-permute-start.2) | collective-permute-done | bytes 589856 | tf_op jit(solution)/shard_map/ppermute | solution.py:280
  30.5 13.5 %collective-permute-done.3.far = bf16[64,4608]{1,0:T(8,128)(2,1)} collective-permute-done((bf16[64,4608]{1,0:T(8,128)(2,1)}, bf16[64,4608]{1,0:T(8,128)(2,1)}, u32[]{:S(2)}, u32[]{:S(2)}) %collective-permute-start.3) | collective-permute-done | bytes 589856 | tf_op jit(solution)/shard_map/ppermute | solution.py:280
  44.0 0.0 collective-permute-done.4.down
  44.0 1.8 shard_map.87
  45.8 0.0 copy-start.1
  45.8 3.0 %collective-permute-start.5 = (bf16[32,8192]{1,0:T(8,128)(2,1)S(1)}, bf16[32,8192]{1,0:T(8,128)(2,1)S(1)}, u32[]{:S(2)}, u32[]{:S(2)}) collective-permute-start(bf16[32,8192]{1,0:T(8,128)(2,1)S(1)} %get-tuple-element.34), channel_id=1, source_target_pairs={{0,2},{2,0},{1,3},{3,1},{4,6},{6,4},{5,7},{7,5},{8,10},{10,8},{9,1... | collective-permute-start | bytes 1572872 | tf_op jit(solution)/shard_map/ppermute | solution.py:433
  49.0 0.0 collective-permute-done.6
  49.0 2.4 %fusion.2 = (bf16[32,4096]{1,0:T(8,128)(2,1)}, bf16[32,4096]{1,0:T(8,128)(2,1)}, bf16[32,4096]{1,0:T(8,128)(2,1)}, f32[32,4096]{1,0:T(8,128)}) fusion(bf16[4,32,4096]{2,1,0:T(8,128)(2,1)} %collective-permute-done.6, bf16[4,32,4096]{2,1,0:T(8,128)(2,1)S(1)} %copy-done.8), kind=kLoop, calls=%fused_computation.9 | loop fusion | flops 1966080 | bytes 3407872 | tf_op jit(solution)/shard_map/convert_element_type | solution.py:431
  51.4 2.6 %collective-permute-start.9 = (bf16[32,4096]{1,0:T(8,128)(2,1)}, bf16[32,4096]{1,0:T(8,128)(2,1)S(1)}, u32[]{:S(2)}, u32[]{:S(2)}) collective-permute-start(bf16[32,4096]{1,0:T(8,128)(2,1)} %get-tuple-element.48), channel_id=1, source_target_pairs={{0,12},{4,0},{8,4},{12,8},{1,13},{5,1},{9,5},{13,9},{2,14},{6,2},{... | collective-permute-start | bytes 786440 | tf_op jit(solution)/shard_map/ppermute | solution.py:280
  54.0 0.0 collective-permute-start.8
  54.0 1.2 collective-permute-start.7
  55.1 4.9 %collective-permute-done.5.back = bf16[32,8192]{1,0:T(8,128)(2,1)S(1)} collective-permute-done((bf16[32,8192]{1,0:T(8,128)(2,1)S(1)}, bf16[32,8192]{1,0:T(8,128)(2,1)S(1)}, u32[]{:S(2)}, u32[]{:S(2)}) %collective-permute-start.5) | collective-permute-done | bytes 524320 | tf_op jit(solution)/shard_map/ppermute | solution.py:433
  60.2 0.6 copy-done.7
  60.8 0.1 maximum_select_fusion
  60.9 0.4 select_n.47
  61.3 1.1 fusion.11
  62.4 0.0 copy-start.4
  62.4 0.0 copy-start.5
  62.5 0.1 pad_maximum_fusion
  62.6 0.8 copy.33
  63.4 1.9 %collective-permute-start.10 = (bf16[1024,256]{1,0:T(8,128)(2,1)}, bf16[1024,256]{1,0:T(8,128)(2,1)}, u32[]{:S(2)}, u32[]{:S(2)}) collective-permute-start(bf16[1024,256]{1,0:T(8,128)(2,1)} %bitcast.20.q_own), channel_id=1, source_target_pairs={{0,1},{1,0},{2,3},{3,2},{4,5},{5,4},{6,7},{7,6},{8,9},{9,8},{10,11... | collective-permute-start | bytes 1572872 | tf_op jit(solution)/shard_map/ppermute | solution.py:276
  65.3 0.0 collective-permute-done.9.down
  65.4 0.7 collective-permute-done.7.far
  66.0 0.0 copy-done.12
  66.1 3.3 %shard_map.89 = (f32[32,8192]{1,0:T(8,128)}, bf16[8,8,32,128]{3,2,1,0:T(8,128)(2,1)}) custom-call(f32[32,4096]{1,0:T(8,128)} %copy-done.1, bf16[32,8192]{1,0:T(8,128)(2,1)} %copy-done.7, f32[32,4096]{1,0:T(8,128)} %get-tuple-element.51.right, bf16[32,4096]{1,0:T(8,128)(2,1)} %collective-permute-done.7.far, bf16[32,4096]{1,0:T(8,128)(2,1)} %collective-permute-done.8.up, ...), custom_call_target="tpu_custom_call" | custom-call | tf_op jit(solution)/shard_map/pallas_call | solution.py:264
  69.3 5.0 %all-to-all-start = ((bf16[8,8,32,128]{3,2,1,0:T(8,128)(2,1)}), bf16[8,8,32,128]{3,2,1,0:T(8,128)(2,1)}, u32[]{:S(2)}, u32[]{:S(2)}) async-start(bf16[8,8,32,128]{3,2,1,0:T(8,128)(2,1)} %get-tuple-element.38), calls=%async_computation | async-start | bytes 1048576 | tf_op jit(solution)/shard_map/all_to_all | solution.py:460
  74.4 0.1 subtract_convert_fusion.refs_1_
  74.5 3.2 %collective-permute-start.11 = (bf16[32,8192]{1,0:T(8,128)(2,1)S(1)}, bf16[32,8192]{1,0:T(8,128)(2,1)S(1)}, u32[]{:S(2)}, u32[]{:S(2)}) collective-permute-start(bf16[32,8192]{1,0:T(8,128)(2,1)S(1)} %subtract_convert_fusion.refs_1_), channel_id=1, source_target_pairs={{0,1},{1,0},{2,3},{3,2},{4,5},{5,4},{6,7},{7,6},{8,9},{9,8},{10,11... | collective-permute-start | bytes 1572872 | tf_op jit(solution)/shard_map/ppermute | solution.py:276
  77.7 0.1 copy.40
  77.9 0.6 pad_add_fusion.place
  78.5 0.0 collective-permute-done.10.q_other
  78.5 3.1 %all-to-all-done.blocks = bf16[8,8,32,128]{3,2,1,0:T(8,128)(2,1)} async-done(((bf16[8,8,32,128]{3,2,1,0:T(8,128)(2,1)}), bf16[8,8,32,128]{3,2,1,0:T(8,128)(2,1)}, u32[]{:S(2)}, u32[]{:S(2)}) %all-to-all-start) | async-done | bytes 524320 | tf_op jit(solution)/shard_map/all_to_all | solution.py:460
  81.6 2.3 %shard_map.90 = (bf16[8,32,128]{2,1,0:T(8,128)(2,1)S(1)}, bf16[8,32,256]{2,1,0:T(8,128)(2,1)}) custom-call(s32[4]{0:T(128)} %pad_add_fusion.place, bf16[8,8,32,128]{3,2,1,0:T(8,128)(2,1)} %all-to-all-done.blocks, bf16[1024,256]{1,0:T(8,128)(2,1)} %bitcast.20.q_own, bf16[1024,256]{1,0:T(8,128)(2,1)} %collective-permute-done.10.q_other), custom_call_target="tpu_custom_call" | custom-call | tf_op jit(solution)/shard_map/pallas_call | solution.py:215
  83.9 3.4 %all-to-all-start.1 = ((bf16[8,32,256]{2,1,0:T(8,128)(2,1)}), bf16[8,32,256]{2,1,0:T(8,128)(2,1)S(1)}, u32[]{:S(2)}, u32[]{:S(2)}) async-start(bf16[8,32,256]{2,1,0:T(8,128)(2,1)} %get-tuple-element.39), calls=%async_computation.1 | async-start | bytes 262144 | tf_op jit(solution)/shard_map/all_to_all | solution.py:462
  87.3 0.1 constant_dynamic-slice_fusion
  87.4 0.7 copy.46
  88.1 4.4 %all-to-all-done.1.terms = bf16[8,32,256]{2,1,0:T(8,128)(2,1)S(1)} async-done(((bf16[8,32,256]{2,1,0:T(8,128)(2,1)}), bf16[8,32,256]{2,1,0:T(8,128)(2,1)S(1)}, u32[]{:S(2)}, u32[]{:S(2)}) %all-to-all-start.1) | async-done | bytes 131104 | tf_op jit(solution)/shard_map/all_to_all | solution.py:462
  92.5 0.7 copy-done.11
  93.1 1.7 shard_map.91
  94.8 15.9 %all_to_all.20 = bf16[8,4,32,128]{3,2,1,0:T(8,128)(2,1)S(1)} all-to-all(bf16[8,4,32,128]{3,2,1,0:T(8,128)(2,1)} %shard_map.91), channel_id=1, replica_groups=mesh['x'=4,'ylo'=2,'z'=4,'yhi'=2,'core'=2] {'z','yhi'}, dimensions={0} | all-to-all | bytes 524288 | tf_op jit(solution)/shard_map/all_to_all | solution.py:464
  110.7 3.7 %collective-permute-start.12 = (bf16[4,256,128]{2,1,0:T(8,128)(2,1)S(1)}, bf16[4,256,128]{2,1,0:T(8,128)(2,1)S(1)}, u32[]{:S(2)}, u32[]{:S(2)}) collective-permute-start(bf16[4,256,128]{2,1,0:T(8,128)(2,1)S(1)} %bitcast.79), channel_id=1, source_target_pairs={{0,1},{1,0},{2,3},{3,2},{4,5},{5,4},{6,7},{7,6},{8,9},{9,8},{10,11... | collective-permute-start | bytes 786440 | tf_op jit(solution)/shard_map/ppermute | solution.py:276
  114.5 1.2 collective-permute-done.12.other_ref
  115.6 3.6 %shard_map.92 = bf16[64,256,128]{2,1,0:T(8,128)(2,1)S(1)} custom-call(bf16[4,256,128]{2,1,0:T(8,128)(2,1)S(1)} %bitcast.80, bf16[4,256,128]{2,1,0:T(8,128)(2,1)S(1)} %collective-permute-done.12.other_ref), custom_call_target="tpu_custom_call" | custom-call | tf_op jit(solution)/shard_map/pallas_call | solution.py:66
  119.3 56.1 %all_to_all.21 = bf16[64,256,128]{2,1,0:T(8,128)(2,1)} all-to-all(bf16[64,256,128]{2,1,0:T(8,128)(2,1)S(1)} %shard_map.92), channel_id=1, replica_groups=mesh['x'=4,'ylo'=2,'z'=4,'yhi'=2,'core'=2] {'x','ylo','z','yhi'}, dimensions={0} | all-to-all | bytes 8388608 | tf_op jit(solution)/shard_map/all_to_all | solution.py:469
  175.4 2.0 %collective-permute-start.13 = (bf16[64,256,128]{2,1,0:T(8,128)(2,1)}, bf16[64,256,128]{2,1,0:T(8,128)(2,1)}, u32[]{:S(2)}, u32[]{:S(2)}) collective-permute-start(bf16[64,256,128]{2,1,0:T(8,128)(2,1)} %all_to_all.21), channel_id=1, source_target_pairs={{0,1},{1,0},{2,3},{3,2},{4,5},{5,4},{6,7},{7,6},{8,9},{9,8},{10,11... | collective-permute-start | bytes 12582920 | tf_op jit(solution)/shard_map/ppermute | solution.py:276
  177.4 7.6 %shard_map.93 = (bf16[8,2,32,8192]{3,2,1,0:T(8,128)(2,1)}, f32[32,8192]{1,0:T(8,128)}, f32[32,8192]{1,0:T(8,128)}, f32[32,8192]{1,0:T(8,128)}) custom-call(s32[4]{0:T(128)} %pad_add_fusion.place, bf16[8,8,256,128]{3,2,1,0:T(8,128)(2,1)} %bitcast.26.refs_0_, bf16[32,8192]{1,0:T(8,128)(2,1)} %copy-done.3, f32[32,8192]{1,0:T(8,128)} %get-tuple-element.43.refs_2_, ...), custom_call_target="tpu_custom_call" | custom-call | tf_op jit(solution)/shard_map/pallas_call | solution.py:138
  185.0 0.0 collective-permute-done.13
  185.1 4.6 %shard_map.94 = bf16[8,2,32,8192]{3,2,1,0:T(8,128)(2,1)} custom-call(s32[4]{0:T(128)} %pad_add_fusion.place, bf16[8,8,256,128]{3,2,1,0:T(8,128)(2,1)} %bitcast.25.moved, bf16[32,8192]{1,0:T(8,128)(2,1)} %copy-done.10, bf16[8,2,32,8192]{3,2,1,0:T(8,128)(2,1)} %get-tuple-element.44._), custom_call_target="tpu_custom_call", output_to_operand_aliasing={{}: (3, {})} | custom-call | tf_op jit(solution)/shard_map/pallas_call | solution.py:179
  (42 shorter events, 0.3 us)
Async XLA Ops:
  0.6 6.6 %copy-start = (f32[512,256]{1,0:T(8,128)S(1)}, f32[512,256]{1,0:T(8,128)}, u32[]{:S(2)}) copy-start(f32[512,256]{1,0:T(8,128)} %param.9) | copy-start | bytes 1572868
  3.1 5.6 %collective-permute-start.1 = (bf16[4,2,32,4096]{3,2,1,0:T(8,128)(2,1)}, bf16[4,2,32,4096]{3,2,1,0:T(8,128)(2,1)}, u32[]{:S(2)}, u32[]{:S(2)}) collective-permute-start(bf16[4,2,32,4096]{3,2,1,0:T(8,128)(2,1)} %shard_map.84), channel_id=1, source_target_pairs={{0,1},{1,0},{2,3},{3,2},{4,5},{5,4},{6,7},{7,6},{8,9},{9,8},{10,11... | collective-permute-start | bytes 6291464 | tf_op jit(solution)/shard_map/ppermute | solution.py:276
  7.1 11.6 %collective-permute-start = (bf16[4,2,32,4096]{3,2,1,0:T(8,128)(2,1)}, bf16[4,2,32,4096]{3,2,1,0:T(8,128)(2,1)S(1)}, u32[]{:S(2)}, u32[]{:S(2)}) collective-permute-start(bf16[4,2,32,4096]{3,2,1,0:T(8,128)(2,1)} %shard_map.85), channel_id=1, source_target_pairs={{0,1},{1,0},{2,3},{3,2},{4,5},{5,4},{6,7},{7,6},{8,9},{9,8},{10,11... | collective-permute-start | bytes 6291464 | tf_op jit(solution)/shard_map/ppermute | solution.py:276
  12.9 17.6 %collective-permute-start.2 = (bf16[64,4608]{1,0:T(8,128)(2,1)}, bf16[64,4608]{1,0:T(8,128)(2,1)S(1)}, u32[]{:S(2)}, u32[]{:S(2)}) collective-permute-start(bf16[64,4608]{1,0:T(8,128)(2,1)} %get-tuple-element.30), channel_id=1, source_target_pairs={{0,4},{4,8},{8,12},{12,0},{1,5},{5,9},{9,13},{13,1},{2,6},{6,10},{... | collective-permute-start | bytes 1769480 | tf_op jit(solution)/shard_map/ppermute | solution.py:280
  14.6 29.3 %collective-permute-start.3 = (bf16[64,4608]{1,0:T(8,128)(2,1)}, bf16[64,4608]{1,0:T(8,128)(2,1)}, u32[]{:S(2)}, u32[]{:S(2)}) collective-permute-start(bf16[64,4608]{1,0:T(8,128)(2,1)} %get-tuple-element.31), channel_id=1, source_target_pairs={{0,8},{4,12},{8,0},{12,4},{1,9},{5,13},{9,1},{13,5},{2,10},{6,14},... | collective-permute-start | bytes 1769480 | tf_op jit(solution)/shard_map/ppermute | solution.py:280
  17.9 26.0 %collective-permute-start.4 = (bf16[64,4608]{1,0:T(8,128)(2,1)}, bf16[64,4608]{1,0:T(8,128)(2,1)}, u32[]{:S(2)}, u32[]{:S(2)}) collective-permute-start(bf16[64,4608]{1,0:T(8,128)(2,1)} %get-tuple-element.32), channel_id=1, source_target_pairs={{0,12},{4,0},{8,4},{12,8},{1,13},{5,1},{9,5},{13,9},{2,14},{6,2},{... | collective-permute-start | bytes 1769480 | tf_op jit(solution)/shard_map/ppermute | solution.py:280
  18.7 1.3 copy-start.6
  23.3 25.6 %copy-start.8 = (bf16[4,32,4096]{2,1,0:T(8,128)(2,1)S(1)}, bf16[4,32,4096]{2,1,0:T(8,128)(2,1)}, u32[]{:S(2)}) copy-start(bf16[4,32,4096]{2,1,0:T(8,128)(2,1)} %get-tuple-element.36) | copy-start | bytes 3145732
  23.4 25.6 %collective-permute-start.6 = (bf16[4,32,4096]{2,1,0:T(8,128)(2,1)}, bf16[4,32,4096]{2,1,0:T(8,128)(2,1)}, u32[]{:S(2)}, u32[]{:S(2)}) collective-permute-start(bf16[4,32,4096]{2,1,0:T(8,128)(2,1)} %get-tuple-element.37), channel_id=1, source_target_pairs={{0,2},{2,0},{1,3},{3,1},{4,6},{6,4},{5,7},{7,5},{8,10},{10,8},{9,1... | collective-permute-start | bytes 3145736 | tf_op jit(solution)/shard_map/ppermute | solution.py:428
  30.5 13.5 %copy-start.9 = (bf16[64,4608]{1,0:T(8,128)(2,1)}, bf16[64,4608]{1,0:T(8,128)(2,1)S(1)}, u32[]{:S(2)}) copy-start(bf16[64,4608]{1,0:T(8,128)(2,1)S(1)} %collective-permute-done.2.up) | copy-start | bytes 1769476
  45.8 15.5 %copy-start.1 = (f32[32,4096]{1,0:T(8,128)}, f32[32,4096]{1,0:T(8,128)S(1)}, u32[]{:S(2)}) copy-start(f32[32,4096]{1,0:T(8,128)S(1)} %get-tuple-element.33.left) | copy-start | bytes 1572868
  45.8 14.2 %collective-permute-start.5 = (bf16[32,8192]{1,0:T(8,128)(2,1)S(1)}, bf16[32,8192]{1,0:T(8,128)(2,1)S(1)}, u32[]{:S(2)}, u32[]{:S(2)}) collective-permute-start(bf16[32,8192]{1,0:T(8,128)(2,1)S(1)} %get-tuple-element.34), channel_id=1, source_target_pairs={{0,2},{2,0},{1,3},{3,1},{4,6},{6,4},{5,7},{7,5},{8,10},{10,8},{9,1... | collective-permute-start | bytes 1572872 | tf_op jit(solution)/shard_map/ppermute | solution.py:433
  51.4 14.0 %collective-permute-start.9 = (bf16[32,4096]{1,0:T(8,128)(2,1)}, bf16[32,4096]{1,0:T(8,128)(2,1)S(1)}, u32[]{:S(2)}, u32[]{:S(2)}) collective-permute-start(bf16[32,4096]{1,0:T(8,128)(2,1)} %get-tuple-element.48), channel_id=1, source_target_pairs={{0,12},{4,0},{8,4},{12,8},{1,13},{5,1},{9,5},{13,9},{2,14},{6,2},{... | collective-permute-start | bytes 786440 | tf_op jit(solution)/shard_map/ppermute | solution.py:280
  54.0 11.4 %collective-permute-start.8 = (bf16[32,4096]{1,0:T(8,128)(2,1)}, bf16[32,4096]{1,0:T(8,128)(2,1)}, u32[]{:S(2)}, u32[]{:S(2)}) collective-permute-start(bf16[32,4096]{1,0:T(8,128)(2,1)} %get-tuple-element.49), channel_id=1, source_target_pairs={{0,4},{4,8},{8,12},{12,0},{1,5},{5,9},{9,13},{13,1},{2,6},{6,10},{... | collective-permute-start | bytes 786440 | tf_op jit(solution)/shard_map/ppermute | solution.py:280
  54.0 12.1 %collective-permute-start.7 = (bf16[32,4096]{1,0:T(8,128)(2,1)}, bf16[32,4096]{1,0:T(8,128)(2,1)}, u32[]{:S(2)}, u32[]{:S(2)}) collective-permute-start(bf16[32,4096]{1,0:T(8,128)(2,1)} %get-tuple-element.50), channel_id=1, source_target_pairs={{0,8},{4,12},{8,0},{12,4},{1,9},{5,13},{9,1},{13,5},{2,10},{6,14},... | collective-permute-start | bytes 786440 | tf_op jit(solution)/shard_map/ppermute | solution.py:280
  60.0 0.8 copy-start.7
  62.4 12.0 %copy-start.4 = (f32[32,8192]{1,0:T(8,128)S(1)}, f32[32,8192]{1,0:T(8,128)}, u32[]{:S(2)}) copy-start(f32[32,8192]{1,0:T(8,128)} %refs_4_.1) | copy-start | bytes 3145732
  62.4 12.0 %copy-start.5 = (f32[32,8192]{1,0:T(8,128)S(1)}, f32[32,8192]{1,0:T(8,128)}, u32[]{:S(2)}) copy-start(f32[32,8192]{1,0:T(8,128)} %refs_3_.1) | copy-start | bytes 3145732
  63.4 15.1 %collective-permute-start.10 = (bf16[1024,256]{1,0:T(8,128)(2,1)}, bf16[1024,256]{1,0:T(8,128)(2,1)}, u32[]{:S(2)}, u32[]{:S(2)}) collective-permute-start(bf16[1024,256]{1,0:T(8,128)(2,1)} %bitcast.20.q_own), channel_id=1, source_target_pairs={{0,1},{1,0},{2,3},{3,2},{4,5},{5,4},{6,7},{7,6},{8,9},{9,8},{10,11... | collective-permute-start | bytes 1572872 | tf_op jit(solution)/shard_map/ppermute | solution.py:276
  65.3 0.7 copy-start.12
  69.3 12.2 %all-to-all-start = ((bf16[8,8,32,128]{3,2,1,0:T(8,128)(2,1)}), bf16[8,8,32,128]{3,2,1,0:T(8,128)(2,1)}, u32[]{:S(2)}, u32[]{:S(2)}) async-start(bf16[8,8,32,128]{3,2,1,0:T(8,128)(2,1)} %get-tuple-element.38), calls=%async_computation | async-start | bytes 1048576 | tf_op jit(solution)/shard_map/all_to_all | solution.py:460
  74.5 44.8 %copy-start.3 = (bf16[32,8192]{1,0:T(8,128)(2,1)}, bf16[32,8192]{1,0:T(8,128)(2,1)S(1)}, u32[]{:S(2)}) copy-start(bf16[32,8192]{1,0:T(8,128)(2,1)S(1)} %subtract_convert_fusion.refs_1_) | copy-start | bytes 1572868
  74.5 36.2 %collective-permute-start.11 = (bf16[32,8192]{1,0:T(8,128)(2,1)S(1)}, bf16[32,8192]{1,0:T(8,128)(2,1)S(1)}, u32[]{:S(2)}, u32[]{:S(2)}) collective-permute-start(bf16[32,8192]{1,0:T(8,128)(2,1)S(1)} %subtract_convert_fusion.refs_1_), channel_id=1, source_target_pairs={{0,1},{1,0},{2,3},{3,2},{4,5},{5,4},{6,7},{7,6},{8,9},{9,8},{10,11... | collective-permute-start | bytes 1572872 | tf_op jit(solution)/shard_map/ppermute | solution.py:276
  83.9 8.6 %copy-start.2 = (bf16[8,32,128]{2,1,0:T(8,128)(2,1)}, bf16[8,32,128]{2,1,0:T(8,128)(2,1)S(1)}, u32[]{:S(2)}) copy-start(bf16[8,32,128]{2,1,0:T(8,128)(2,1)S(1)} %get-tuple-element.40.mean) | copy-start | bytes 196612
  83.9 8.6 %all-to-all-start.1 = ((bf16[8,32,256]{2,1,0:T(8,128)(2,1)}), bf16[8,32,256]{2,1,0:T(8,128)(2,1)S(1)}, u32[]{:S(2)}, u32[]{:S(2)}) async-start(bf16[8,32,256]{2,1,0:T(8,128)(2,1)} %get-tuple-element.39), calls=%async_computation.1 | async-start | bytes 262144 | tf_op jit(solution)/shard_map/all_to_all | solution.py:462
  92.5 0.7 copy-start.11
  110.7 64.7 %copy-start.10 = (bf16[32,8192]{1,0:T(8,128)(2,1)}, bf16[32,8192]{1,0:T(8,128)(2,1)S(1)}, u32[]{:S(2)}) copy-start(bf16[32,8192]{1,0:T(8,128)(2,1)S(1)} %collective-permute-done.11.before) | copy-start | bytes 1572868
  110.7 4.9 %collective-permute-start.12 = (bf16[4,256,128]{2,1,0:T(8,128)(2,1)S(1)}, bf16[4,256,128]{2,1,0:T(8,128)(2,1)S(1)}, u32[]{:S(2)}, u32[]{:S(2)}) collective-permute-start(bf16[4,256,128]{2,1,0:T(8,128)(2,1)S(1)} %bitcast.79), channel_id=1, source_target_pairs={{0,1},{1,0},{2,3},{3,2},{4,5},{5,4},{6,7},{7,6},{8,9},{9,8},{10,11... | collective-permute-start | bytes 786440 | tf_op jit(solution)/shard_map/ppermute | solution.py:276
  175.4 9.6 %collective-permute-start.13 = (bf16[64,256,128]{2,1,0:T(8,128)(2,1)}, bf16[64,256,128]{2,1,0:T(8,128)(2,1)}, u32[]{:S(2)}, u32[]{:S(2)}) collective-permute-start(bf16[64,256,128]{2,1,0:T(8,128)(2,1)} %all_to_all.21), channel_id=1, source_target_pairs={{0,1},{1,0},{2,3},{3,2},{4,5},{5,4},{6,7},{7,6},{8,9},{9,8},{10,11... | collective-permute-start | bytes 12582920 | tf_op jit(solution)/shard_map/ppermute | solution.py:276
